TPU v7x, 32 devices: a whole 2x2x4 slice. The times are simulated.
32 devices in a mesh: pole: 2 (over y), prow: 4 (over z), pcol: 4 (over x, core).
Axes of the slice: x: 2, y: 2, z: 4, core: 2. Of those that a mesh axis runs over, the one named last changes fastest.
Arguments:
- known_inverse: bfloat16 [4096, 2048], P(('pole', 'prow'), 'pcol'), parts along dimension 0, may hold values from -6 to 6
- upper_panel: bfloat16 [32, 4, 128, 128], P(('pole', 'prow'), 'pcol'), parts along dimension 0, may hold values from -0.125 to 0.125
- upper_slots: int32 [16, 4], P('prow', 'pcol'), may hold values from -1 to 3, as said below
- upper_pivots: float32 [1024, 128], P(('pole', 'prow', 'pcol')), parts along dimension 0, may hold values from -6 to 6
- lower_panel: bfloat16 [32, 4, 128, 128], P(('pole', 'prow'), 'pcol'), parts along dimension 0, may hold values from -0.125 to 0.125
- lower_slots: int32 [16, 4], P('prow', 'pcol'), may hold values from -1 to 4, as said below
- lower_pivots: float32 [1024, 128], P(('pole', 'prow', 'pcol')), parts along dimension 0, may hold values from -6 to 6
Outputs:
- upper_rows: bfloat16 [1024, 2048], P(('pole', 'prow'), 'pcol'), parts along dimension 0
- upper_diagonal: float32 [1024, 128], P(('pole', 'prow', 'pcol')), parts along dimension 0
- lower_rows: bfloat16 [1024, 2048], P(('pole', 'prow'), 'pcol'), parts along dimension 0
- lower_diagonal: float32 [1024, 128], P(('pole', 'prow', 'pcol')), parts along dimension 0
There are 2 independent parts, one for each index of `pole`. A program takes and returns all parts, laid end to end along the dimension named above; an argument that names none is the same for every part. Nothing has to cross between parts.
Inputs may be any that keep to these rules, and one draw needn't show every extreme that they name: `upper_slots`: rows r*4 to r*4 + 3 of a column k form supernode k's list on process row r: distinct values, live entries first, -1 marking an empty slot; value v names ancestor r*4+v. `lower_slots`: rows r*4 to r*4 + 3 of a column k form supernode k's list on process row r: distinct values, live entries first, -1 marking an empty slot; value v below 4 names ancestor r*4+v, value 4 names upper-level supernode r. The first entry of row floor(k)*4 is always 4, and 4 appears nowhere else.
All inputs are finite; a program needn't handle non-finite values.
Results may differ from a plain program's by a relative error of at most 0.006.
Values may be sent and summed in bfloat16 or wider, within the bound.
No kernel may reach another device: no remote copies, remote signals or barrier semaphores. Data moves between devices by JAX's collectives and lax.ppermute only.
A program may use at most 64 MiB of HBM per device.

v0:
```python
import jax
import jax.numpy as jnp
from jax import lax
from jax.sharding import PartitionSpec as P

AR = 4
CH = 1


precise = lax.Precision.HIGHEST


def spread_local(blocks, slot_index, extent):
    selector = (slot_index[:, :, None] == jnp.arange(extent, dtype=jnp.int32)).astype(jnp.bfloat16)
    expanded = jnp.einsum("ska,skij->aikj", selector, blocks, preferred_element_type=jnp.float32)
    return expanded.reshape(extent * blocks.shape[2], blocks.shape[1] * blocks.shape[3]).astype(
        jnp.bfloat16
    )


def column_dense(column_list):
    pieces = []
    for arrived in column_list:
        blocks = arrived[0]
        chosen = arrived[1]
        pieces.append(spread_local(blocks, chosen, AR))
    return jnp.concatenate(pieces, axis=0)


def pick_sources(blocks, chosen, first_source, source_count):
    picked = []
    for offset in range(source_count):
        start = (first_source + offset) * AR
        picked.append(
            (
                lax.dynamic_slice_in_dim(blocks, start, AR, 0),
                lax.dynamic_slice_in_dim(chosen, start, AR, 0),
            )
        )
    return picked


def per_device(
    known_inverse, upper_panel, upper_slots, upper_pivots, lower_panel, lower_slots, lower_pivots
):
    prow_index = lax.axis_index("prow")
    pcol_index = lax.axis_index("pcol")
    row_ratio = lax.axis_size("prow") // lax.axis_size("pcol")
    first_source = pcol_index * row_ratio
    block_side = upper_panel.shape[2]
    numbers = (((0,), (0,)), ((), ()))
    upper_gathered, upper_chosen = (
        lax.all_gather(upper_panel, "pcol", axis=1, tiled=True),
        lax.all_gather(upper_slots, "pcol", axis=1, tiled=True),
    )
    swapped = (
        lax.all_to_all(upper_gathered, "prow", split_axis=1, concat_axis=0, tiled=True),
        lax.all_to_all(upper_chosen, "prow", split_axis=1, concat_axis=0, tiled=True),
    )
    upper_columns = pick_sources(swapped[0], swapped[1], first_source, row_ratio)
    upper_local = spread_local(upper_gathered, upper_chosen, AR)
    selected = upper_local
    upper_sum = lax.psum_scatter(
        lax.dot_general(selected, known_inverse, numbers, preferred_element_type=jnp.float32),
        "prow",
        scatter_dimension=0,
        tiled=True,
    )
    upper_rows = (-upper_sum).astype(jnp.bfloat16)
    own_cols = column_dense(upper_columns)
    upper_part = jnp.dot(
        upper_sum,
        own_cols.astype(jnp.float32),
        precision=precise,
        preferred_element_type=jnp.float32,
    )
    upper_diagonal = upper_pivots + lax.psum_scatter(
        upper_part.astype(jnp.bfloat16), "pcol", scatter_dimension=0, tiled=True
    ).astype(jnp.float32)
    lower_gathered, lower_chosen = (
        lax.all_gather(lower_panel, "pcol", axis=1, tiled=True),
        lax.all_gather(lower_slots, "pcol", axis=1, tiled=True),
    )
    swapped = (
        lax.all_to_all(lower_gathered, "prow", split_axis=1, concat_axis=0, tiled=True),
        lax.all_to_all(lower_chosen, "prow", split_axis=1, concat_axis=0, tiled=True),
    )
    lower_columns = pick_sources(swapped[0], swapped[1], first_source, row_ratio)
    extended = jnp.concatenate([known_inverse, upper_rows], axis=0)
    lower_local = spread_local(lower_gathered, lower_chosen, AR + 1)
    selected = lower_local
    lower_sum = lax.psum_scatter(
        lax.dot_general(selected, extended, numbers, preferred_element_type=jnp.float32),
        "prow",
        scatter_dimension=0,
        tiled=True,
    )
    lower_rows = (-lower_sum).astype(jnp.bfloat16)
    parent_panel = lax.dynamic_slice_in_dim(lower_gathered[0], prow_index * CH, CH, 0).astype(
        jnp.float32
    )
    pivot_count = upper_diagonal.shape[0]
    parent_piece = lax.dynamic_slice_in_dim(parent_panel, pcol_index * pivot_count, pivot_count, 1)
    pivot_times = jnp.einsum("ab,kbj->kaj", upper_diagonal, parent_panel, precision=precise)
    pivot_part = jnp.einsum("kai,kaj->kij", parent_piece, pivot_times, precision=precise)
    own_cols = column_dense(lower_columns).reshape(-1, CH, block_side)
    first_part = jnp.einsum(
        "jin,njm->jim",
        lower_sum.reshape(CH, block_side, -1),
        own_cols.astype(jnp.float32),
        precision=precise,
    )
    coupling = jnp.einsum("in,njm->jim", upper_rows, own_cols, preferred_element_type=jnp.float32)
    side_term = jnp.einsum("jai,jab->jib", coupling, parent_panel, precision=precise) + pivot_part
    lower_part = (first_part + side_term).reshape(CH * block_side, block_side)
    lower_diagonal = lower_pivots + lax.psum_scatter(
        lower_part.astype(jnp.bfloat16), "pcol", scatter_dimension=0, tiled=True
    ).astype(jnp.float32)
    return (upper_rows, upper_diagonal, lower_rows, lower_diagonal)


def solution(mesh):
    placed = (
        P(("pole", "prow"), "pcol"),
        P(("pole", "prow"), "pcol", None, None),
        P("prow", "pcol"),
        P(("pole", "prow", "pcol"), None),
        P(("pole", "prow"), "pcol", None, None),
        P("prow", "pcol"),
        P(("pole", "prow", "pcol"), None),
    )
    return jax.shard_map(
        per_device,
        mesh=mesh,
        in_specs=placed,
        out_specs=(
            P(("pole", "prow"), "pcol"),
            P(("pole", "prow", "pcol"), None),
            P(("pole", "prow"), "pcol"),
            P(("pole", "prow", "pcol"), None),
        ),
        check_vma=False,
    )
```

profile of v0, /device:TPU:0, one launch (start us, length us, event | category | flops | bytes accessed | tf_op | source)
XLA Modules:
  0.0 164.0 jit_solution(13394235189239229467)
XLA Ops:
  7.2 10.1 %all_gather.13 = bf16[4,4,128,128]{3,2,0,1:T(8,128)(2,1)} all-gather(bf16[4,1,128,128]{3,2,0,1:T(8,128)(2,1)} %bitcast.116), channel_id=1, replica_groups=mesh['pole'=2,'prow'=4,'pcol'=4] {'pcol'}, dimensions={1}, use_global_device_ids=true | all-gather | bytes 655360 | tf_op jit(solution)/shard_map/all_gather | solution.py:53
  17.3 5.7 %all-gather = s32[4,1,4]{2,1,0:T(1,128)} all-gather(s32[1,1,4]{2,1,0:T(1,128)} %bitcast.118), channel_id=1, replica_groups=mesh['pole'=2,'prow'=4,'pcol'=4] {'pcol'}, dimensions={0}, use_global_device_ids=true | all-gather | bytes 80 | tf_op jit(solution)/shard_map/all_gather | solution.py:54
  23.0 1.6 fusion.1
  25.0 1.4 fusion.12
  26.5 5.0 %all-to-all-start.1 = ((s32[4,4,1]{0,2,1:T(1,128)}), s32[4,4,1]{0,2,1:T(1,128)S(1)}, u32[]{:S(2)}, u32[]{:S(2)}) async-start(s32[4,4,1]{0,2,1:T(1,128)} %bitcast.46), calls=%async_computation.2 | async-start | bytes 4096 | tf_op jit(solution)/shard_map/all_to_all | solution.py:58
  31.5 5.0 %all-gather.1 = s32[4,1,4]{2,1,0:T(1,128)} all-gather(s32[1,1,4]{2,1,0:T(1,128)S(1)} %bitcast.119), channel_id=1, replica_groups=mesh['pole'=2,'prow'=4,'pcol'=4] {'pcol'}, dimensions={0}, use_global_device_ids=true | all-gather | bytes 80 | tf_op jit(solution)/shard_map/all_gather | solution.py:82
  37.0 4.6 %all-to-all-start.3 = ((s32[4,4,1]{0,2,1:T(1,128)}), s32[4,4,1]{0,2,1:T(1,128)S(1)}, u32[]{:S(2)}, u32[]{:S(2)}) async-start(s32[4,4,1]{0,2,1:T(1,128)} %bitcast.53), calls=%async_computation.6 | async-start | bytes 4096 | tf_op jit(solution)/shard_map/all_to_all | solution.py:86
  41.7 6.9 %all_gather.15 = bf16[4,4,128,128]{3,2,0,1:T(8,128)(2,1)S(1)} all-gather(bf16[4,1,128,128]{3,2,0,1:T(8,128)(2,1)S(1)} %bitcast.117), channel_id=1, replica_groups=mesh['pole'=2,'prow'=4,'pcol'=4] {'pcol'}, dimensions={1}, use_global_device_ids=true | all-gather | bytes 655360 | tf_op jit(solution)/shard_map/all_gather | solution.py:81
  48.6 19.6 %all_to_all.74 = bf16[4,4,128,128]{3,2,0,1:T(8,128)(2,1)S(1)} all-to-all(bf16[4,4,128,128]{3,2,0,1:T(8,128)(2,1)S(1)} %all_gather.15), channel_id=1, replica_groups=mesh['pole'=2,'prow'=4,'pcol'=4] {'prow'}, dimensions={1} | all-to-all | bytes 1048576 | tf_op jit(solution)/shard_map/all_to_all | solution.py:85
  68.2 3.5 %all-to-all-start = ((bf16[4,4,128,128]{3,2,0,1:T(8,128)(2,1)}), bf16[4,4,128,128]{3,2,0,1:T(8,128)(2,1)S(1)}, u32[]{:S(2)}, u32[]{:S(2)}) async-start(bf16[4,4,128,128]{3,2,0,1:T(8,128)(2,1)} %all_gather.13), calls=%async_computation.1 | async-start | bytes 1048576 | tf_op jit(solution)/shard_map/all_to_all | solution.py:57
  71.7 1.3 fusion
  73.1 0.6 copy.45
  73.8 12.0 %all-to-all-done = bf16[4,4,128,128]{3,2,0,1:T(8,128)(2,1)S(1)} async-done(((bf16[4,4,128,128]{3,2,0,1:T(8,128)(2,1)}), bf16[4,4,128,128]{3,2,0,1:T(8,128)(2,1)S(1)}, u32[]{:S(2)}, u32[]{:S(2)}) %all-to-all-start) | async-done | bytes 524320 | tf_op jit(solution)/shard_map/all_to_all | solution.py:57
  86.2 1.8 %convolution_convert_fusion.4 = bf16[128,128]{1,0:T(8,128)(2,1)} fusion(f32[128,512]{1,0:T(8,128)} %reduce-scatter.5.cloned.1.call-done, bf16[512,128]{1,0:T(8,128)(2,1)S(1)} %bitcast.115), kind=kOutput, calls=%fused_computation.11 | convolution fusion | flops 100679680 | bytes 425984 | tf_op jit(solution)/shard_map/dot_general | solution.py:71
  88.1 1.0 negate_convert_fusion.1
  89.1 1.6 fusion.6
  91.8 14.5 %reduce-scatter.7.cloned.1.call-done = bf16[32,128]{1,0:T(8,128)(2,1)} async-done(((bf16[128,128]{1,0:T(8,128)(2,1)}), bf16[32,128]{1,0:T(8,128)(2,1)}) %reduce-scatter.7.cloned.1.call-update) | async-done | bytes 8208 | tf_op jit(solution)/shard_map/reduce_scatter | solution.py:77
  106.3 0.7 convert_add_fusion.1
  107.1 28.6 %reduce-scatter.9.cloned.1.call-done = f32[128,512]{1,0:T(8,128)} async-done(((f32[512,512]{1,0:T(8,128)}), f32[128,512]{1,0:T(8,128)}) %reduce-scatter.9.cloned.1.call-update) | async-done | bytes 262160 | tf_op jit(solution)/shard_map/reduce_scatter | solution.py:92
  135.8 1.2 fusion.47
  137.0 0.9 fusion.5
  137.9 1.6 negate_convert_fusion
  139.5 16.7 %reduce-scatter.11.cloned.1.call-done = bf16[32,128]{1,0:T(8,128)(2,1)} async-done(((bf16[128,128]{1,0:T(8,128)(2,1)}), bf16[32,128]{1,0:T(8,128)(2,1)}) %reduce-scatter.11.cloned.1.call-update) | async-done | bytes 8208 | tf_op jit(solution)/shard_map/reduce_scatter | solution.py:116
  156.2 1.3 convert_add_fusion
  (40 shorter events, 2.8 us)
Async XLA Ops:
  7.2 79.1 %reduce-scatter.5.cloned.1.call-start = ((), (), s32[]{:S(2)}) async-start(), calls=%async_computation.8 | async-start | bytes 1310720 | tf_op jit(solution)/shard_map/reduce_scatter | solution.py:63
  23.0 2.0 %copy-start.1 = (bf16[512,512]{1,0:T(8,128)(2,1)S(1)}, bf16[512,512]{1,0:T(8,128)(2,1)}, u32[]{:S(2)}) copy-start(bf16[512,512]{1,0:T(8,128)(2,1)} %param.7) | copy-start | bytes 1572868
  26.5 5.0 %copy-start.6 = (s32[4,1]{0,1:T(1,128)S(1)}, s32[4,1]{0,1:T(1,128)}, u32[]{:S(2)}) copy-start(s32[4,1]{0,1:T(1,128)} %param.12) | copy-start | bytes 52
  26.5 15.2 %copy-start.2 = (bf16[4,1,128,128]{3,2,1,0:T(8,128)(2,1)S(1)}, bf16[4,1,128,128]{3,2,1,0:T(8,128)(2,1)}, u32[]{:S(2)}) copy-start(bf16[4,1,128,128]{3,2,1,0:T(8,128)(2,1)} %param.11) | copy-start | bytes 393220
  26.5 10.5 %all-to-all-start.1 = ((s32[4,4,1]{0,2,1:T(1,128)}), s32[4,4,1]{0,2,1:T(1,128)S(1)}, u32[]{:S(2)}, u32[]{:S(2)}) async-start(s32[4,4,1]{0,2,1:T(1,128)} %bitcast.46), calls=%async_computation.2 | async-start | bytes 4096 | tf_op jit(solution)/shard_map/all_to_all | solution.py:58
  37.0 11.6 %all-to-all-start.3 = ((s32[4,4,1]{0,2,1:T(1,128)}), s32[4,4,1]{0,2,1:T(1,128)S(1)}, u32[]{:S(2)}, u32[]{:S(2)}) async-start(s32[4,4,1]{0,2,1:T(1,128)} %bitcast.53), calls=%async_computation.6 | async-start | bytes 4096 | tf_op jit(solution)/shard_map/all_to_all | solution.py:86
  68.2 17.6 %all-to-all-start = ((bf16[4,4,128,128]{3,2,0,1:T(8,128)(2,1)}), bf16[4,4,128,128]{3,2,0,1:T(8,128)(2,1)S(1)}, u32[]{:S(2)}, u32[]{:S(2)}) async-start(bf16[4,4,128,128]{3,2,0,1:T(8,128)(2,1)} %all_gather.13), calls=%async_computation.1 | async-start | bytes 1048576 | tf_op jit(solution)/shard_map/all_to_all | solution.py:57
  71.7 34.6 %reduce-scatter.7.cloned.1.call-start = ((), (), s32[]{:S(2)}) async-start(), calls=%async_computation.9 | async-start | bytes 40960 | tf_op jit(solution)/shard_map/reduce_scatter | solution.py:77
  88.1 47.7 %reduce-scatter.9.cloned.1.call-start = ((), (), s32[]{:S(2)}) async-start(), calls=%async_computation.10 | async-start | bytes 1310720 | tf_op jit(solution)/shard_map/reduce_scatter | solution.py:92
  89.1 2.2 %copy-start = (bf16[128,512]{1,0:T(8,128)(2,1)}, bf16[128,512]{1,0:T(8,128)(2,1)S(1)}, u32[]{:S(2)}) copy-start(bf16[128,512]{1,0:T(8,128)(2,1)S(1)} %negate_convert_fusion.1) | copy-start | bytes 393220
  90.7 15.6 %copy-start.4 = (f32[32,128]{1,0:T(8,128)S(1)}, f32[32,128]{1,0:T(8,128)}, u32[]{:S(2)}) copy-start(f32[32,128]{1,0:T(8,128)} %param.10) | copy-start | bytes 49156
  90.7 65.5 %reduce-scatter.11.cloned.1.call-start = ((), (), s32[]{:S(2)}) async-start(), calls=%async_computation.11 | async-start | bytes 40960 | tf_op jit(solution)/shard_map/reduce_scatter | solution.py:116
  91.0 65.2 %copy-start.5 = (f32[32,128]{1,0:T(8,128)S(1)}, f32[32,128]{1,0:T(8,128)}, u32[]{:S(2)}) copy-start(f32[32,128]{1,0:T(8,128)} %param.13) | copy-start | bytes 49156
  107.0 50.5 %copy-start.3 = (f32[32,128]{1,0:T(8,128)}, f32[32,128]{1,0:T(8,128)S(1)}, u32[]{:S(2)}) copy-start(f32[32,128]{1,0:T(8,128)S(1)} %convert_add_fusion.1) | copy-start | bytes 49156
Sparse Core Ops, SparseCore 0:
  26.6 27.5 reduce-scatter.4
  88.2 18.0 reduce-scatter.6
  108.6 27.1 reduce-scatter.8
  138.2 17.9 reduce-scatter.10
where the time goes:
time: 165 us; the launch traced here: 164 us
  waiting for transfers between devices  72.4 us (44%)
  blocking collectives  47.4 us (29%)
  between operations  13.9 us (8%)
  starting transfers between devices  13.3 us (8%)
  matrix products  11 us (7%)
  other arithmetic  4.6 us (3%)
    reduce_scatter x1, waiting for transfers between devices, per_device(): lax.psum_scatter(lax.dot_general(selected, extended, numbers, preferred_e...  28.6 us
    all_to_all x1, blocking collectives, per_device(): lax.all_to_all(lower_gathered, 'prow', split_axis=1, concat_axis=0, tiled...  19.6 us
    reduce_scatter x1, waiting for transfers between devices, per_device(): lax.psum_scatter(lower_part.astype(jnp.bfloat16), 'pcol', scatter_dimensi...  16.7 us
    reduce_scatter x1, waiting for transfers between devices, per_device(): lax.psum_scatter(upper_part.astype(jnp.bfloat16), 'pcol', scatter_dimensi...  14.5 us
    all_to_all x1, waiting for transfers between devices, per_device(): lax.all_to_all(upper_gathered, 'prow', split_axis=1, concat_axis=0, tiled...  12 us
    all_gather x1, blocking collectives, per_device(): lax.all_gather(upper_panel, 'pcol', axis=1, tiled=True)  10.1 us
    all_gather x1, blocking collectives, per_device(): lax.all_gather(lower_panel, 'pcol', axis=1, tiled=True)  6.93 us
    all_gather x1, blocking collectives, per_device(): lax.all_gather(upper_slots, 'pcol', axis=1, tiled=True)  5.68 us
  transfers between devices with their start and end apart: 7, of which 5 were waited for; matrix products, arithmetic and copies ran while one was open for 5% of the time, Pallas kernels for 0%

commit v1 on v0

v1 whole, which is shorter than its diff:
```python
import functools

import jax
import jax.numpy as jnp
from jax import lax
from jax.experimental import pallas as pl
from jax.experimental.pallas import tpu as pltpu
from jax.sharding import PartitionSpec as P

AR = 4
BF = jnp.bfloat16
F32 = jnp.float32
VMEM = pl.BlockSpec(memory_space=pltpu.VMEM)
SMEM = pl.BlockSpec(memory_space=pltpu.SMEM)


def tdot(a, b):
    return lax.dot_general(a, b, (((0,), (0,)), ((), ())), preferred_element_type=F32)


def ndot(a, b):
    return lax.dot_general(a, b, (((1,), (0,)), ((), ())), preferred_element_type=F32)


def split(x):
    hi = x.astype(BF)
    return hi, (x - hi.astype(F32)).astype(BF)


def spread(dense, row_start, panel, column, slots, slot_start):
    side = panel.shape[2]
    for s in range(AR):
        v = slots[slot_start + s, column]

        @pl.when((v >= 0) & (v < AR))
        def _():
            rows = pl.ds(pl.multiple_of(row_start + v * side, side), side)
            dense[rows, :] = panel[s, column]


def partial_kernel(prow, pcol, columns, slot_start, with_parent, *refs):
    panels, refs = refs[:pcol], refs[pcol:]
    slots, refs = refs[:pcol], refs[pcol:]
    known, refs = refs[0], refs[1:]
    outs, refs = refs[:prow], refs[prow:]
    dense = refs[-1]
    r = lax.axis_index("prow")
    c = lax.axis_index("pcol")
    side = panels[0].shape[2]
    extent = AR * side
    dense[...] = jnp.zeros_like(dense)
    for j in range(pcol):
        for i in range(columns):
            k = (c ^ j) * columns + i
            spread(dense, k * extent, panels[j], i, slots[j], slot_start)
            if with_parent:

                @pl.when(k == r)
                def _():
                    refs[0][...] = panels[j][0, i]

    for t in range(prow):
        rows = pl.ds(pl.multiple_of((r ^ t) * extent, extent), extent)
        outs[t][...] = tdot(dense[rows, :], known[...]).astype(outs[t].dtype)


def finish_kernel(prow, pcol, columns, *refs):
    upper_parts, refs = refs[:prow], refs[prow:]
    lower_parts, refs = refs[:prow], refs[prow:]
    upper_turned, refs = refs[:columns], refs[columns:]
    lower_turned, refs = refs[:columns], refs[columns:]
    slots_turned, refs = refs[:columns], refs[columns:]
    parent_ref, pivots, refs = refs[0], refs[1], refs[2:]
    upper_rows, lower_rows, refs = refs[0], refs[1], refs[2:]
    pieces, refs = refs[:pcol], refs[pcol:]
    dense, parts = refs
    r = lax.axis_index("prow")
    c = lax.axis_index("pcol")
    side = parent_ref.shape[0]
    extent = AR * side
    share = pivots.shape[0]
    dense[...] = jnp.zeros_like(dense)
    for p in range(columns):
        q = (r - p) % columns if columns > 1 else 0
        spread(dense.at[0], q * extent, upper_turned[p], 0, slots_turned[p], 0)
        spread(dense.at[1], q * extent, lower_turned[p], 0, slots_turned[p], AR)
    parent = parent_ref[...]
    upper_sum = upper_parts[0][...]
    for t in range(1, prow):
        upper_sum += upper_parts[t][...].astype(F32)
    hi, lo = split(upper_sum)
    rows = -hi
    upper_rows[...] = rows
    upper_part = ndot(hi, dense[0]) + ndot(lo, dense[0])
    parts[0] = upper_part
    parts[1] = upper_part
    own = pl.ds(pl.multiple_of(c * share, share), share)
    parts[1, own, :] += pivots[...]
    lower_sum = lower_parts[0][...] + tdot(parent, rows)
    for t in range(1, prow):
        lower_sum += lower_parts[t][...].astype(F32)
    hi, lo = split(lower_sum)
    lower_rows[...] = -hi
    lower_part = ndot(hi, dense[1]) + ndot(lo, dense[1])
    coupling_hi, coupling_lo = split(ndot(rows, dense[1]))
    lower_part += tdot(coupling_hi, parent) + tdot(coupling_lo, parent)
    hi, lo = split(parts[1])
    hi, lo = split(ndot(hi, parent) + ndot(lo, parent))
    parts[1] = lower_part + tdot(parent, hi) + tdot(parent, lo)
    for s in range(pcol):
        theirs = pl.ds(pl.multiple_of((c ^ s) * share, share), share)
        pieces[s][0] = parts[0, theirs, :].astype(pieces[s].dtype)
        pieces[s][1] = parts[1, theirs, :].astype(pieces[s].dtype)


def sum_kernel(pcol, *refs):
    pieces, refs = refs[:pcol], refs[pcol:]
    upper_pivots, lower_pivots, upper_diagonal, lower_diagonal = refs
    total = pieces[0][...]
    for s in range(1, pcol):
        total += pieces[s][...].astype(F32)
    upper_diagonal[...] = upper_pivots[...] + total[0]
    lower_diagonal[...] = lower_pivots[...] + total[1]


def call(kernel, outs, specs, scratch=()):
    return pl.pallas_call(
        kernel,
        out_shape=outs,
        in_specs=specs,
        out_specs=tuple(VMEM for _ in outs),
        scratch_shapes=scratch,
        compiler_params=pltpu.CompilerParams(vmem_limit_bytes=48 << 20),
    )


def per_device(
    known_inverse, upper_panel, upper_slots, upper_pivots, lower_panel, lower_slots, lower_pivots
):
    prow = lax.axis_size("prow")
    pcol = lax.axis_size("pcol")
    columns = upper_panel.shape[1]
    side = upper_panel.shape[2]
    width = known_inverse.shape[1]
    extent = AR * side
    share = upper_pivots.shape[0]
    shape = jax.ShapeDtypeStruct

    def across(x, j):
        return lax.ppermute(x, "pcol", [(c, c ^ j) for c in range(pcol)])

    def along(x, t):
        return lax.ppermute(x, "prow", [(r, r ^ t) for r in range(prow)])

    def gather(x):
        held = {0: x}
        for j in range(2, pcol, 2):
            held[j] = across(x, j)
        for j in range(1, pcol, 2):
            held[j] = across(held[j - 1], 1)
        return [held[j] for j in range(pcol)]

    def turned(x):
        moved = []
        for p in range(columns):
            pairs = []
            for a in range(prow):
                for b in range(pcol):
                    pairs.append((a * pcol + b, (b * columns + (a + p) % columns) * pcol + a // columns))
            piece = x
            if columns > 1:
                first = (lax.axis_index("prow") + p) % columns
                piece = lax.dynamic_slice_in_dim(x, first, 1, 1)
            moved.append(lax.ppermute(piece, ("prow", "pcol"), pairs))
        return moved

    slots = jnp.concatenate([upper_slots, lower_slots], axis=0)
    upper_all = gather(upper_panel)
    lower_all = gather(lower_panel)
    slots_all = gather(slots)
    upper_turned = turned(upper_panel)
    lower_turned = turned(lower_panel)
    slots_turned = turned(slots)

    def partial(panels, slot_start, with_parent):
        outs = [shape((side, width), F32)] + [shape((side, width), BF)] * (prow - 1)
        if with_parent:
            outs.append(shape((side, side), BF))
        return call(
            functools.partial(partial_kernel, prow, pcol, columns, slot_start, with_parent),
            tuple(outs),
            [VMEM] * pcol + [SMEM] * pcol + [VMEM],
            [pltpu.VMEM((prow * extent, side), BF)],
        )(*panels, *slots_all, known_inverse)

    upper_parts = partial(upper_all, 0, False)
    lower_parts = partial(lower_all, AR, True)
    parent = lower_parts[-1]
    upper_sent = [upper_parts[0]] + [along(upper_parts[t], t) for t in range(1, prow)]
    lower_sent = [lower_parts[0]] + [along(lower_parts[t], t) for t in range(1, prow)]
    outs = [shape((side, width), BF)] * 2 + [shape((2, share, side), F32)]
    outs += [shape((2, share, side), BF)] * (pcol - 1)
    finished = call(
        functools.partial(finish_kernel, prow, pcol, columns),
        tuple(outs),
        [VMEM] * (2 * prow + 2 * columns) + [SMEM] * columns + [VMEM] * 2,
        [pltpu.VMEM((2, width, side), BF), pltpu.VMEM((2, side, side), F32)],
    )(*upper_sent, *lower_sent, *upper_turned, *lower_turned, *slots_turned, parent, upper_pivots)
    upper_rows, lower_rows = finished[:2]
    pieces = [finished[2]] + [across(finished[2 + s], s) for s in range(1, pcol)]
    upper_diagonal, lower_diagonal = call(
        functools.partial(sum_kernel, pcol),
        (shape((share, side), F32), shape((share, side), F32)),
        [VMEM] * (pcol + 2),
    )(*pieces, upper_pivots, lower_pivots)
    return upper_rows, upper_diagonal, lower_rows, lower_diagonal


def solution(mesh):
    placed = (
        P(("pole", "prow"), "pcol"),
        P(("pole", "prow"), "pcol", None, None),
        P("prow", "pcol"),
        P(("pole", "prow", "pcol"), None),
        P(("pole", "prow"), "pcol", None, None),
        P("prow", "pcol"),
        P(("pole", "prow", "pcol"), None),
    )
    return jax.shard_map(
        per_device,
        mesh=mesh,
        in_specs=placed,
        out_specs=(
            P(("pole", "prow"), "pcol"),
            P(("pole", "prow", "pcol"), None),
            P(("pole", "prow"), "pcol"),
            P(("pole", "prow", "pcol"), None),
        ),
        check_vma=False,
    )
```

time: 165 us -> 63.5 us (0.38)
  waiting for transfers between devices: 72.4 us -> 22.8 us
  blocking collectives: 47.4 us -> 0 us
  starting transfers between devices: 13.3 us -> 30.8 us
  between operations: 13.9 us -> 0.7 us
  matrix products: 11 us -> 0 us
  Pallas kernels: 0 us -> 5.49 us
  other arithmetic: 4.6 us -> 0.75 us
    reduce_scatter x4 -> x0, waiting for transfers between devices: 59.9 us -> none  [the longest x1 28.6 us: per_device(): lax.psum_scatter(lax.dot_general(selected, extended, numbers, preferred_e...]
    ppermute x0 -> x21, starting transfers between devices: none -> 30.8 us  [the longest x6 19.4 us: along(): return lax.ppermute(x, 'prow', [(r, r ^ t) for r in range(prow)])]
    all_gather x4 -> x0, blocking collectives: 27.8 us -> none  [the longest x1 10.1 us: per_device(): lax.all_gather(upper_panel, 'pcol', axis=1, tiled=True)]
    ppermute x0 -> x21, waiting for transfers between devices: none -> 22.8 us  [the longest x6 11.6 us: along(): return lax.ppermute(x, 'prow', [(r, r ^ t) for r in range(prow)])]
    all_to_all x1 -> x0, blocking collectives: 19.6 us -> none  [per_device(): lax.all_to_all(lower_gathered, 'prow', split_axis=1, concat_axis=0, tiled...]
    all_to_all x3 -> x0, starting transfers between devices: 13.1 us -> none  [the longest x1 5.02 us: per_device(): lax.all_to_all(upper_chosen, 'prow', split_axis=1, concat_axis=0, tiled=T...]
    all_to_all x3 -> x0, waiting for transfers between devices: 12.5 us -> none  [the longest x1 12 us: per_device(): lax.all_to_all(upper_gathered, 'prow', split_axis=1, concat_axis=0, tiled...]
    dot_general x12 -> x0, matrix products: 11 us -> none  [the longest x4 3.6 us: spread_local(): jnp.einsum('ska,skij->aikj', selector, blocks, preferred_element_type=jnp...]
  transfers between devices with their start and end apart: 7 -> 21, of which waited for: 5 -> 9; matrix products, arithmetic and copies ran while one was open for 5% -> 1% of each run, Pallas kernels for 0% -> 5%
where the time goes in v1:
time: 63.5 us; the launch traced here: 62.6 us
  starting transfers between devices  30.8 us (49%)
  waiting for transfers between devices  22.8 us (36%)
  Pallas kernels  5.49 us (9%)
  local copies, waits for them, and re-layouts  2.04 us (3%)
  other arithmetic  0.75 us (1%)
  between operations  0.7 us (1%)
    ppermute x6, starting transfers between devices, along(): return lax.ppermute(x, 'prow', [(r, r ^ t) for r in range(prow)])  19.4 us
    ppermute x6, waiting for transfers between devices, along(): return lax.ppermute(x, 'prow', [(r, r ^ t) for r in range(prow)])  11.6 us
    ppermute x12, waiting for transfers between devices, across(): return lax.ppermute(x, 'pcol', [(c, c ^ j) for c in range(pcol)])  11.2 us
    ppermute x12, starting transfers between devices, across(): return lax.ppermute(x, 'pcol', [(c, c ^ j) for c in range(pcol)])  7.69 us
    ppermute x3, starting transfers between devices, turned(): moved.append(lax.ppermute(piece, ('prow', 'pcol'), pairs))  3.76 us
    pallas_call x2, Pallas kernels, partial(): call(functools.partial(partial_kernel, prow, pcol, columns, slot_start, w...  2.96 us
    unnamed x12, local copies, waits for them, and re-layouts  1.96 us
    pallas_call x1, Pallas kernels, per_device(): call(functools.partial(finish_kernel, prow, pcol, columns), tuple(outs),...  1.9 us
  transfers between devices with their start and end apart: 21, of which 9 were waited for; matrix products, arithmetic and copies ran while one was open for 1% of the time, Pallas kernels for 5%

profile of v1, /device:TPU:0, one launch (start us, length us, event | category | flops | bytes accessed | tf_op | source)
XLA Modules:
  0.0 62.6 jit_solution(1539833040505894098)
XLA Ops:
  0.6 3.0 %collective-permute-start.10 = (bf16[4,1,128,128]{3,2,1,0:T(8,128)(2,1)}, bf16[4,1,128,128]{3,2,1,0:T(8,128)(2,1)S(1)}, u32[]{:S(2)}, u32[]{:S(2)}) collective-permute-start(bf16[4,1,128,128]{3,2,1,0:T(8,128)(2,1)} %refs_0_.3), channel_id=1, source_target_pairs={{0,2},{1,3},{2,0},{3,1},{4,6},{5,7},{6,4},{7,5},{8,10},{9,11},{10,... | collective-permute-start | bytes 393224 | tf_op jit(solution)/shard_map/ppermute | solution.py:150
  3.7 4.5 %collective-permute-done.10.refs_2_ = bf16[4,1,128,128]{3,2,1,0:T(8,128)(2,1)S(1)} collective-permute-done((bf16[4,1,128,128]{3,2,1,0:T(8,128)(2,1)}, bf16[4,1,128,128]{3,2,1,0:T(8,128)(2,1)S(1)}, u32[]{:S(2)}, u32[]{:S(2)}) %collective-permute-start.10) | collective-permute-done | bytes 131104 | tf_op jit(solution)/shard_map/ppermute | solution.py:150
  8.7 0.7 %pad_add_fusion = s32[8,1]{0,1:T(1,128)S(1)} fusion(s32[4,1]{0,1:T(1,128)} %param.12, s32[4,1]{0,1:T(1,128)} %param.9), kind=kLoop, calls=%fused_computation | loop fusion | flops 8 | bytes 64 | tf_op jit(solution)/shard_map/concatenate | solution.py:177
  9.5 2.1 %collective-permute-start.4 = (s32[8,1]{1,0:T(8,128)S(1)}, s32[8,1]{1,0:T(8,128)S(1)}, u32[]{:S(2)}, u32[]{:S(2)}) collective-permute-start(s32[8,1]{1,0:T(8,128)S(1)} %copy.15.refs_4_), channel_id=1, source_target_pairs={{0,2},{1,3},{2,0},{3,1},{4,6},{5,7},{6,4},{7,5},{8,10},{9,11},{10,... | collective-permute-start | bytes 104 | tf_op jit(solution)/shard_map/ppermute | solution.py:150
  11.6 1.6 %collective-permute-done.4.refs_6_ = s32[8,1]{1,0:T(8,128)S(1)} collective-permute-done((s32[8,1]{1,0:T(8,128)S(1)}, s32[8,1]{1,0:T(8,128)S(1)}, u32[]{:S(2)}, u32[]{:S(2)}) %collective-permute-start.4) | collective-permute-done | bytes 64 | tf_op jit(solution)/shard_map/ppermute | solution.py:150
  13.2 1.2 %collective-permute-done.3.refs_5_ = s32[8,1]{1,0:T(8,128)S(1)} collective-permute-done((s32[8,1]{1,0:T(8,128)S(1)}, s32[8,1]{1,0:T(8,128)S(1)}, u32[]{:S(2)}, u32[]{:S(2)}) %collective-permute-start.3) | collective-permute-done | bytes 64 | tf_op jit(solution)/shard_map/ppermute | solution.py:150
  14.5 1.0 %collective-permute-done.5.refs_7_ = s32[8,1]{1,0:T(8,128)S(1)} collective-permute-done((s32[8,1]{1,0:T(8,128)S(1)}, s32[8,1]{1,0:T(8,128)S(1)}, u32[]{:S(2)}, u32[]{:S(2)}) %collective-permute-start.5) | collective-permute-done | bytes 64 | tf_op jit(solution)/shard_map/ppermute | solution.py:150
  15.5 1.6 %collective-permute-start.15 = (bf16[4,1,128,128]{3,2,1,0:T(8,128)(2,1)}, bf16[4,1,128,128]{3,2,1,0:T(8,128)(2,1)S(1)}, u32[]{:S(2)}, u32[]{:S(2)}) collective-permute-start(bf16[4,1,128,128]{3,2,1,0:T(8,128)(2,1)} %refs_0_.2), channel_id=1, source_target_pairs={{0,0},{1,4},{2,8},{3,12},{4,1},{5,5},{6,9},{7,13},{8,2},{9,6},{10,... | collective-permute-start | bytes 393224 | tf_op jit(solution)/shard_map/ppermute | solution.py:174
  17.0 1.6 %collective-permute-start.16 = (bf16[4,1,128,128]{3,2,1,0:T(8,128)(2,1)}, bf16[4,1,128,128]{3,2,1,0:T(8,128)(2,1)S(1)}, u32[]{:S(2)}, u32[]{:S(2)}) collective-permute-start(bf16[4,1,128,128]{3,2,1,0:T(8,128)(2,1)} %refs_0_.3), channel_id=1, source_target_pairs={{0,0},{1,4},{2,8},{3,12},{4,1},{5,5},{6,9},{7,13},{8,2},{9,6},{10,... | collective-permute-start | bytes 393224 | tf_op jit(solution)/shard_map/ppermute | solution.py:174
  18.6 1.0 %copy-done = bf16[512,512]{1,0:T(8,128)(2,1)S(1)} copy-done((bf16[512,512]{1,0:T(8,128)(2,1)S(1)}, bf16[512,512]{1,0:T(8,128)(2,1)}, u32[]{:S(2)}) %copy-start) | copy-done | bytes 524312
  19.6 0.9 %copy-done.3 = bf16[4,1,128,128]{3,2,1,0:T(8,128)(2,1)S(1)} copy-done((bf16[4,1,128,128]{3,2,1,0:T(8,128)(2,1)S(1)}, bf16[4,1,128,128]{3,2,1,0:T(8,128)(2,1)}, u32[]{:S(2)}) %copy-start.3) | copy-done | bytes 131096
  20.6 1.5 %shard_map.103 = (f32[128,512]{1,0:T(8,128)S(1)}, bf16[128,512]{1,0:T(8,128)(2,1)S(1)}, bf16[128,512]{1,0:T(8,128)(2,1)S(1)}, bf16[128,512]{1,0:T(8,128)(2,1)S(1)}, bf16[128,128]{1,0:T(8,128)(2,1)S(1)}) custom-call(bf16[4,1,128,128]{3,2,1,0:T(8,128)(2,1)S(1)} %copy-done.3, bf16[4,1,128,128]{3,2,1,0:T(8,128)(2,1)S(1)} %collective-permute-done.9.refs_1_, ...), custom_call_target="tpu_custom_call" | custom-call | tf_op jit(solution)/shard_map/pallas_call | solution.py:189
  22.1 4.7 %collective-permute-start.12 = (bf16[128,512]{1,0:T(8,128)(2,1)S(1)}, bf16[128,512]{1,0:T(8,128)(2,1)S(1)}, u32[]{:S(2)}, u32[]{:S(2)}) collective-permute-start(bf16[128,512]{1,0:T(8,128)(2,1)S(1)} %get-tuple-element.26), channel_id=1, source_target_pairs={{0,4},{4,0},{8,12},{12,8},{1,5},{5,1},{9,13},{13,9},{2,6},{6,2},{1... | collective-permute-start | bytes 393224 | tf_op jit(solution)/shard_map/ppermute | solution.py:153
  27.4 6.6 %collective-permute-start.13 = (bf16[128,512]{1,0:T(8,128)(2,1)S(1)}, bf16[128,512]{1,0:T(8,128)(2,1)S(1)}, u32[]{:S(2)}, u32[]{:S(2)}) collective-permute-start(bf16[128,512]{1,0:T(8,128)(2,1)S(1)} %get-tuple-element.27), channel_id=1, source_target_pairs={{0,8},{4,12},{8,0},{12,4},{1,9},{5,13},{9,1},{13,5},{2,10},{6,14},... | collective-permute-start | bytes 393224 | tf_op jit(solution)/shard_map/ppermute | solution.py:153
  34.0 1.5 %shard_map.102 = (f32[128,512]{1,0:T(8,128)S(1)}, bf16[128,512]{1,0:T(8,128)(2,1)S(1)}, bf16[128,512]{1,0:T(8,128)(2,1)S(1)}, bf16[128,512]{1,0:T(8,128)(2,1)S(1)}) custom-call(bf16[4,1,128,128]{3,2,1,0:T(8,128)(2,1)S(1)} %copy-done.2, bf16[4,1,128,128]{3,2,1,0:T(8,128)(2,1)S(1)} %collective-permute-done.refs_1_, ...), custom_call_target="tpu_custom_call" | custom-call | tf_op jit(solution)/shard_map/pallas_call | solution.py:189
  35.5 3.8 %collective-permute-start.14 = (bf16[128,512]{1,0:T(8,128)(2,1)S(1)}, bf16[128,512]{1,0:T(8,128)(2,1)S(1)}, u32[]{:S(2)}, u32[]{:S(2)}) collective-permute-start(bf16[128,512]{1,0:T(8,128)(2,1)S(1)} %get-tuple-element.28), channel_id=1, source_target_pairs={{0,12},{4,8},{8,4},{12,0},{1,13},{5,9},{9,5},{13,1},{2,14},{6,10},... | collective-permute-start | bytes 393224 | tf_op jit(solution)/shard_map/ppermute | solution.py:153
  39.9 3.7 %collective-permute-start.8 = (bf16[128,512]{1,0:T(8,128)(2,1)S(1)}, bf16[128,512]{1,0:T(8,128)(2,1)S(1)}, u32[]{:S(2)}, u32[]{:S(2)}) collective-permute-start(bf16[128,512]{1,0:T(8,128)(2,1)S(1)} %get-tuple-element.24), channel_id=1, source_target_pairs={{0,12},{4,8},{8,4},{12,0},{1,13},{5,9},{9,5},{13,1},{2,14},{6,10},... | collective-permute-start | bytes 393224 | tf_op jit(solution)/shard_map/ppermute | solution.py:153
  43.6 0.9 %collective-permute-done.13.refs_6_ = bf16[128,512]{1,0:T(8,128)(2,1)S(1)} collective-permute-done((bf16[128,512]{1,0:T(8,128)(2,1)S(1)}, bf16[128,512]{1,0:T(8,128)(2,1)S(1)}, u32[]{:S(2)}, u32[]{:S(2)}) %collective-permute-start.13) | collective-permute-done | bytes 131104 | tf_op jit(solution)/shard_map/ppermute | solution.py:153
  44.5 1.4 %collective-permute-done.6.refs_1_ = bf16[128,512]{1,0:T(8,128)(2,1)S(1)} collective-permute-done((bf16[128,512]{1,0:T(8,128)(2,1)S(1)}, bf16[128,512]{1,0:T(8,128)(2,1)S(1)}, u32[]{:S(2)}, u32[]{:S(2)}) %collective-permute-start.6) | collective-permute-done | bytes 131104 | tf_op jit(solution)/shard_map/ppermute | solution.py:153
  45.9 9.3 %collective-permute-done.7.refs_2_ = bf16[128,512]{1,0:T(8,128)(2,1)S(1)} collective-permute-done((bf16[128,512]{1,0:T(8,128)(2,1)S(1)}, bf16[128,512]{1,0:T(8,128)(2,1)S(1)}, u32[]{:S(2)}, u32[]{:S(2)}) %collective-permute-start.7) | collective-permute-done | bytes 131104 | tf_op jit(solution)/shard_map/ppermute | solution.py:153
  55.3 1.9 %shard_map.104 = (bf16[128,512]{1,0:T(8,128)(2,1)}, bf16[128,512]{1,0:T(8,128)(2,1)}, f32[2,32,128]{2,1,0:T(8,128)S(1)}, bf16[2,32,128]{2,1,0:T(8,128)(2,1)S(1)}...) custom-call(f32[128,512]{1,0:T(8,128)S(1)} %get-tuple-element.21.refs_0_, ...), custom_call_target="tpu_custom_call" | custom-call | tf_op jit(solution)/shard_map/pallas_call | solution.py:203
  57.2 1.6 %collective-permute-start.19 = (bf16[2,32,128]{2,1,0:T(8,128)(2,1)S(1)}, bf16[2,32,128]{2,1,0:T(8,128)(2,1)S(1)}, u32[]{:S(2)}, u32[]{:S(2)}) collective-permute-start(bf16[2,32,128]{2,1,0:T(8,128)(2,1)S(1)} %get-tuple-element.33), channel_id=1, source_target_pairs={{0,2},{1,3},{2,0},{3,1},{4,6},{5,7},{6,4},{7,5},{8,10},{9,11},{10,... | collective-permute-start | bytes 49160 | tf_op jit(solution)/shard_map/ppermute | solution.py:150
  59.0 1.9 %collective-permute-done.19.refs_2_ = bf16[2,32,128]{2,1,0:T(8,128)(2,1)S(1)} collective-permute-done((bf16[2,32,128]{2,1,0:T(8,128)(2,1)S(1)}, bf16[2,32,128]{2,1,0:T(8,128)(2,1)S(1)}, u32[]{:S(2)}, u32[]{:S(2)}) %collective-permute-start.19) | collective-permute-done | bytes 16416 | tf_op jit(solution)/shard_map/ppermute | solution.py:150
  60.9 1.1 %collective-permute-done.20.refs_3_ = bf16[2,32,128]{2,1,0:T(8,128)(2,1)S(1)} collective-permute-done((bf16[2,32,128]{2,1,0:T(8,128)(2,1)S(1)}, bf16[2,32,128]{2,1,0:T(8,128)(2,1)S(1)}, u32[]{:S(2)}, u32[]{:S(2)}) %collective-permute-start.20) | collective-permute-done | bytes 16416 | tf_op jit(solution)/shard_map/ppermute | solution.py:150
  (36 shorter events, 3.1 us)
Async XLA Ops:
  0.6 7.5 %collective-permute-start.10 = (bf16[4,1,128,128]{3,2,1,0:T(8,128)(2,1)}, bf16[4,1,128,128]{3,2,1,0:T(8,128)(2,1)S(1)}, u32[]{:S(2)}, u32[]{:S(2)}) collective-permute-start(bf16[4,1,128,128]{3,2,1,0:T(8,128)(2,1)} %refs_0_.3), channel_id=1, source_target_pairs={{0,2},{1,3},{2,0},{3,1},{4,6},{5,7},{6,4},{7,5},{8,10},{9,11},{10,... | collective-permute-start | bytes 393224 | tf_op jit(solution)/shard_map/ppermute | solution.py:150
  3.6 7.9 %collective-permute-start.1 = (bf16[4,1,128,128]{3,2,1,0:T(8,128)(2,1)}, bf16[4,1,128,128]{3,2,1,0:T(8,128)(2,1)S(1)}, u32[]{:S(2)}, u32[]{:S(2)}) collective-permute-start(bf16[4,1,128,128]{3,2,1,0:T(8,128)(2,1)} %refs_0_.2), channel_id=1, source_target_pairs={{0,2},{1,3},{2,0},{3,1},{4,6},{5,7},{6,4},{7,5},{8,10},{9,11},{10,... | collective-permute-start | bytes 393224 | tf_op jit(solution)/shard_map/ppermute | solution.py:150
  3.7 13.3 %collective-permute-start.9 = (bf16[4,1,128,128]{3,2,1,0:T(8,128)(2,1)}, bf16[4,1,128,128]{3,2,1,0:T(8,128)(2,1)S(1)}, u32[]{:S(2)}, u32[]{:S(2)}) collective-permute-start(bf16[4,1,128,128]{3,2,1,0:T(8,128)(2,1)} %refs_0_.3), channel_id=1, source_target_pairs={{0,1},{1,0},{2,3},{3,2},{4,5},{5,4},{6,7},{7,6},{8,9},{9,8},{10,11... | collective-permute-start | bytes 393224 | tf_op jit(solution)/shard_map/ppermute | solution.py:150
  8.2 10.4 %collective-permute-start.11 = (bf16[4,1,128,128]{3,2,1,0:T(8,128)(2,1)S(1)}, bf16[4,1,128,128]{3,2,1,0:T(8,128)(2,1)S(1)}, u32[]{:S(2)}, u32[]{:S(2)}) collective-permute-start(bf16[4,1,128,128]{3,2,1,0:T(8,128)(2,1)S(1)} %collective-permute-done.10.refs_2_), channel_id=1, source_target_pairs={{0,1},{1,0},{2,3},{3,2},{4,5},{5,4},{6,7},{7,6},{8,9},{9,8},{10,11... | collective-permute-start | bytes 393224 | tf_op jit(solution)/shard_map/ppermute | solution.py:150
  8.2 18.5 %collective-permute-start = (bf16[4,1,128,128]{3,2,1,0:T(8,128)(2,1)}, bf16[4,1,128,128]{3,2,1,0:T(8,128)(2,1)S(1)}, u32[]{:S(2)}, u32[]{:S(2)}) collective-permute-start(bf16[4,1,128,128]{3,2,1,0:T(8,128)(2,1)} %refs_0_.2), channel_id=1, source_target_pairs={{0,1},{1,0},{2,3},{3,2},{4,5},{5,4},{6,7},{7,6},{8,9},{9,8},{10,11... | collective-permute-start | bytes 393224 | tf_op jit(solution)/shard_map/ppermute | solution.py:150
  9.5 3.6 %collective-permute-start.4 = (s32[8,1]{1,0:T(8,128)S(1)}, s32[8,1]{1,0:T(8,128)S(1)}, u32[]{:S(2)}, u32[]{:S(2)}) collective-permute-start(s32[8,1]{1,0:T(8,128)S(1)} %copy.15.refs_4_), channel_id=1, source_target_pairs={{0,2},{1,3},{2,0},{3,1},{4,6},{5,7},{6,4},{7,5},{8,10},{9,11},{10,... | collective-permute-start | bytes 104 | tf_op jit(solution)/shard_map/ppermute | solution.py:150
  11.6 15.8 %collective-permute-start.2 = (bf16[4,1,128,128]{3,2,1,0:T(8,128)(2,1)S(1)}, bf16[4,1,128,128]{3,2,1,0:T(8,128)(2,1)S(1)}, u32[]{:S(2)}, u32[]{:S(2)}) collective-permute-start(bf16[4,1,128,128]{3,2,1,0:T(8,128)(2,1)S(1)} %collective-permute-done.1.refs_2_), channel_id=1, source_target_pairs={{0,1},{1,0},{2,3},{3,2},{4,5},{5,4},{6,7},{7,6},{8,9},{9,8},{10,11... | collective-permute-start | bytes 393224 | tf_op jit(solution)/shard_map/ppermute | solution.py:150
  13.2 1.2 %collective-permute-start.3 = (s32[8,1]{1,0:T(8,128)S(1)}, s32[8,1]{1,0:T(8,128)S(1)}, u32[]{:S(2)}, u32[]{:S(2)}) collective-permute-start(s32[8,1]{1,0:T(8,128)S(1)} %copy.15.refs_4_), channel_id=1, source_target_pairs={{0,1},{1,0},{2,3},{3,2},{4,5},{5,4},{6,7},{7,6},{8,9},{9,8},{10,11... | collective-permute-start | bytes 104 | tf_op jit(solution)/shard_map/ppermute | solution.py:150
  14.3 1.2 %collective-permute-start.5 = (s32[8,1]{1,0:T(8,128)S(1)}, s32[8,1]{1,0:T(8,128)S(1)}, u32[]{:S(2)}, u32[]{:S(2)}) collective-permute-start(s32[8,1]{1,0:T(8,128)S(1)} %collective-permute-done.4.refs_6_), channel_id=1, source_target_pairs={{0,1},{1,0},{2,3},{3,2},{4,5},{5,4},{6,7},{7,6},{8,9},{9,8},{10,11... | collective-permute-start | bytes 104 | tf_op jit(solution)/shard_map/ppermute | solution.py:150
  15.5 23.8 %collective-permute-start.15 = (bf16[4,1,128,128]{3,2,1,0:T(8,128)(2,1)}, bf16[4,1,128,128]{3,2,1,0:T(8,128)(2,1)S(1)}, u32[]{:S(2)}, u32[]{:S(2)}) collective-permute-start(bf16[4,1,128,128]{3,2,1,0:T(8,128)(2,1)} %refs_0_.2), channel_id=1, source_target_pairs={{0,0},{1,4},{2,8},{3,12},{4,1},{5,5},{6,9},{7,13},{8,2},{9,6},{10,... | collective-permute-start | bytes 393224 | tf_op jit(solution)/shard_map/ppermute | solution.py:174
  17.0 22.9 %collective-permute-start.16 = (bf16[4,1,128,128]{3,2,1,0:T(8,128)(2,1)}, bf16[4,1,128,128]{3,2,1,0:T(8,128)(2,1)S(1)}, u32[]{:S(2)}, u32[]{:S(2)}) collective-permute-start(bf16[4,1,128,128]{3,2,1,0:T(8,128)(2,1)} %refs_0_.3), channel_id=1, source_target_pairs={{0,0},{1,4},{2,8},{3,12},{4,1},{5,5},{6,9},{7,13},{8,2},{9,6},{10,... | collective-permute-start | bytes 393224 | tf_op jit(solution)/shard_map/ppermute | solution.py:174
  20.5 13.4 %copy-start.1 = (bf16[512,512]{1,0:T(8,128)(2,1)S(1)}, bf16[512,512]{1,0:T(8,128)(2,1)}, u32[]{:S(2)}) copy-start(bf16[512,512]{1,0:T(8,128)(2,1)} %refs_8_.3) | copy-start | bytes 1572868
  20.6 13.4 %copy-start.2 = (bf16[4,1,128,128]{3,2,1,0:T(8,128)(2,1)S(1)}, bf16[4,1,128,128]{3,2,1,0:T(8,128)(2,1)}, u32[]{:S(2)}) copy-start(bf16[4,1,128,128]{3,2,1,0:T(8,128)(2,1)} %refs_0_.2) | copy-start | bytes 393220
  22.1 17.9 %collective-permute-start.12 = (bf16[128,512]{1,0:T(8,128)(2,1)S(1)}, bf16[128,512]{1,0:T(8,128)(2,1)S(1)}, u32[]{:S(2)}, u32[]{:S(2)}) collective-permute-start(bf16[128,512]{1,0:T(8,128)(2,1)S(1)} %get-tuple-element.26), channel_id=1, source_target_pairs={{0,4},{4,0},{8,12},{12,8},{1,5},{5,1},{9,13},{13,9},{2,6},{6,2},{1... | collective-permute-start | bytes 393224 | tf_op jit(solution)/shard_map/ppermute | solution.py:153
  26.7 8.8 %collective-permute-start.17 = (s32[8,1]{1,0:T(8,128)S(1)}, s32[8,1]{1,0:T(8,128)S(1)}, u32[]{:S(2)}, u32[]{:S(2)}) collective-permute-start(s32[8,1]{1,0:T(8,128)S(1)} %copy.15.refs_4_), channel_id=1, source_target_pairs={{0,0},{1,4},{2,8},{3,12},{4,1},{5,5},{6,9},{7,13},{8,2},{9,6},{10,... | collective-permute-start | bytes 104 | tf_op jit(solution)/shard_map/ppermute | solution.py:174
  27.4 17.1 %collective-permute-start.13 = (bf16[128,512]{1,0:T(8,128)(2,1)S(1)}, bf16[128,512]{1,0:T(8,128)(2,1)S(1)}, u32[]{:S(2)}, u32[]{:S(2)}) collective-permute-start(bf16[128,512]{1,0:T(8,128)(2,1)S(1)} %get-tuple-element.27), channel_id=1, source_target_pairs={{0,8},{4,12},{8,0},{12,4},{1,9},{5,13},{9,1},{13,5},{2,10},{6,14},... | collective-permute-start | bytes 393224 | tf_op jit(solution)/shard_map/ppermute | solution.py:153
  34.0 21.3 %copy-start.4 = (f32[32,128]{1,0:T(8,128)S(1)}, f32[32,128]{1,0:T(8,128)}, u32[]{:S(2)}) copy-start(f32[32,128]{1,0:T(8,128)} %refs_4_.1) | copy-start | bytes 49156
  35.5 9.0 %collective-permute-start.14 = (bf16[128,512]{1,0:T(8,128)(2,1)S(1)}, bf16[128,512]{1,0:T(8,128)(2,1)S(1)}, u32[]{:S(2)}, u32[]{:S(2)}) collective-permute-start(bf16[128,512]{1,0:T(8,128)(2,1)S(1)} %get-tuple-element.28), channel_id=1, source_target_pairs={{0,12},{4,8},{8,4},{12,0},{1,13},{5,9},{9,5},{13,1},{2,14},{6,10},... | collective-permute-start | bytes 393224 | tf_op jit(solution)/shard_map/ppermute | solution.py:153
  39.2 6.7 %collective-permute-start.6 = (bf16[128,512]{1,0:T(8,128)(2,1)S(1)}, bf16[128,512]{1,0:T(8,128)(2,1)S(1)}, u32[]{:S(2)}, u32[]{:S(2)}) collective-permute-start(bf16[128,512]{1,0:T(8,128)(2,1)S(1)} %get-tuple-element.22), channel_id=1, source_target_pairs={{0,4},{4,0},{8,12},{12,8},{1,5},{5,1},{9,13},{13,9},{2,6},{6,2},{1... | collective-permute-start | bytes 393224 | tf_op jit(solution)/shard_map/ppermute | solution.py:153
  39.9 15.3 %collective-permute-start.7 = (bf16[128,512]{1,0:T(8,128)(2,1)S(1)}, bf16[128,512]{1,0:T(8,128)(2,1)S(1)}, u32[]{:S(2)}, u32[]{:S(2)}) collective-permute-start(bf16[128,512]{1,0:T(8,128)(2,1)S(1)} %get-tuple-element.23), channel_id=1, source_target_pairs={{0,8},{4,12},{8,0},{12,4},{1,9},{5,13},{9,1},{13,5},{2,10},{6,14},... | collective-permute-start | bytes 393224 | tf_op jit(solution)/shard_map/ppermute | solution.py:153
  39.9 15.3 %collective-permute-start.8 = (bf16[128,512]{1,0:T(8,128)(2,1)S(1)}, bf16[128,512]{1,0:T(8,128)(2,1)S(1)}, u32[]{:S(2)}, u32[]{:S(2)}) collective-permute-start(bf16[128,512]{1,0:T(8,128)(2,1)S(1)} %get-tuple-element.24), channel_id=1, source_target_pairs={{0,12},{4,8},{8,4},{12,0},{1,13},{5,9},{9,5},{13,1},{2,14},{6,10},... | collective-permute-start | bytes 393224 | tf_op jit(solution)/shard_map/ppermute | solution.py:153
  57.2 1.9 %collective-permute-start.18 = (bf16[2,32,128]{2,1,0:T(8,128)(2,1)S(1)}, bf16[2,32,128]{2,1,0:T(8,128)(2,1)S(1)}, u32[]{:S(2)}, u32[]{:S(2)}) collective-permute-start(bf16[2,32,128]{2,1,0:T(8,128)(2,1)S(1)} %get-tuple-element.32), channel_id=1, source_target_pairs={{0,1},{1,0},{2,3},{3,2},{4,5},{5,4},{6,7},{7,6},{8,9},{9,8},{10,11... | collective-permute-start | bytes 49160 | tf_op jit(solution)/shard_map/ppermute | solution.py:150
  57.2 3.7 %collective-permute-start.19 = (bf16[2,32,128]{2,1,0:T(8,128)(2,1)S(1)}, bf16[2,32,128]{2,1,0:T(8,128)(2,1)S(1)}, u32[]{:S(2)}, u32[]{:S(2)}) collective-permute-start(bf16[2,32,128]{2,1,0:T(8,128)(2,1)S(1)} %get-tuple-element.33), channel_id=1, source_target_pairs={{0,2},{1,3},{2,0},{3,1},{4,6},{5,7},{6,4},{7,5},{8,10},{9,11},{10,... | collective-permute-start | bytes 49160 | tf_op jit(solution)/shard_map/ppermute | solution.py:150
  58.8 3.2 %collective-permute-start.20 = (bf16[2,32,128]{2,1,0:T(8,128)(2,1)S(1)}, bf16[2,32,128]{2,1,0:T(8,128)(2,1)S(1)}, u32[]{:S(2)}, u32[]{:S(2)}) collective-permute-start(bf16[2,32,128]{2,1,0:T(8,128)(2,1)S(1)} %get-tuple-element.34), channel_id=1, source_target_pairs={{0,3},{1,2},{2,1},{3,0},{4,7},{5,6},{6,5},{7,4},{8,11},{9,10},{10,... | collective-permute-start | bytes 49160 | tf_op jit(solution)/shard_map/ppermute | solution.py:150
  (3 other events, 8.7 us)

commit v2 on v1

v2 whole, which is shorter than its diff:
```python
import functools

import jax
import jax.numpy as jnp
from jax import lax
from jax.experimental import pallas as pl
from jax.experimental.pallas import tpu as pltpu
from jax.sharding import PartitionSpec as P

AR = 4
BF = jnp.bfloat16
F32 = jnp.float32
VMEM = pl.BlockSpec(memory_space=pltpu.VMEM)
HBM = pl.BlockSpec(memory_space=pltpu.HBM)
SMEM = pl.BlockSpec(memory_space=pltpu.SMEM)


def tdot(a, b):
    return lax.dot_general(a, b, (((0,), (0,)), ((), ())), preferred_element_type=F32)


def ndot(a, b):
    return lax.dot_general(a, b, (((1,), (0,)), ((), ())), preferred_element_type=F32)


def split(x):
    hi = x.astype(BF)
    return hi, (x - hi.astype(F32)).astype(BF)


def place(dense, panel, column, slots):
    for s in range(AR):
        v = slots[column, s]

        @pl.when((v >= 0) & (v < AR))
        def _():
            dense[v] = panel[s, column]


def pack_kernel(
    columns, upper_far, lower_far, upper_slots, lower_slots, packed, turned, upper, lower, arrived
):
    copies = [
        pltpu.make_async_copy(upper_far, upper, arrived.at[0]),
        pltpu.make_async_copy(lower_far, lower, arrived.at[1]),
    ]
    for copy in copies:
        copy.start()
    packed[...] = jnp.zeros_like(packed)
    for copy in copies:
        copy.wait()
    for i in range(columns):
        place(packed.at[i, :AR], upper, i, upper_slots)
        place(packed.at[i, AR : 2 * AR], lower, i, lower_slots)
        packed[i, 2 * AR] = lower[0, i]
        turned[i] = packed[i, : 2 * AR]


def holder(k, columns):
    return (k // columns) % 2


def rounds(prow, columns):
    sends = [(t, e) for t in range(prow) for e in range(2) if (t, e) != (0, 0)]
    lists = {}
    for t, e in sends:
        lists.setdefault(((t // columns) % 2, e), []).append((t, e))
    out = []
    for e in range(2):
        even, odd = lists[0, e][::-1], lists[1, 1 - e][::-1]
        for n in range(max(len(even), len(odd))):
            out.append((even[n] if n < len(even) else None, odd[n] if n < len(odd) else None))
    return out


def partial_kernel(plan, columns, halves, *refs):
    packed, refs = refs[:halves], refs[halves:]
    own_known, other_known, refs = refs[0], refs[1], refs[2:]
    own, refs = refs[0], refs[1:]
    outs, refs = refs[: len(plan)], refs[len(plan) :]
    parent, dense, known = refs
    r = lax.axis_index("prow")
    c = lax.axis_index("pcol")
    side = parent.shape[0]
    extent = AR * side
    holds = c % 2 == holder(r, columns)

    def slot(k):
        return k // (2 * columns) * columns + k % columns

    known[0] = own_known[...]
    known[1] = other_known[...]
    for j in range(halves):
        for i in range(columns):
            k = (c ^ (2 * j)) * columns + i
            for level in range(2):
                blocks = packed[j][i, level * AR : (level + 1) * AR]
                dense[slot(k), :, level * side : (level + 1) * side] = blocks.reshape(extent, side)

            @pl.when(k == r)
            def _():
                parent[...] = packed[j][i, 2 * AR]

    for n, (even, odd) in enumerate(plan):

        def put(t, e):
            outs[n][...] = tdot(dense[slot(r ^ t)], known[e]).astype(BF)

        if even is None or odd is None:

            @pl.when(holds if odd is None else jnp.logical_not(holds))
            def _():
                put(*(even or odd))

        else:
            put(jnp.where(holds, even[0], odd[0]), jnp.where(holds, even[1], odd[1]))

    @pl.when(holds)
    def _():
        own[...] = tdot(dense[slot(r)], own_known[...])

    @pl.when(jnp.logical_not(holds))
    def _():
        own[...] = jnp.zeros_like(own)
        parent[...] = jnp.zeros_like(parent)


def finish_kernel(count, pcol, columns, *refs):
    sums, refs = refs[:count], refs[count:]
    turned, refs = refs[:columns], refs[columns:]
    parent_ref, parent_other, pivots, refs = refs[0], refs[1], refs[2], refs[3:]
    upper_rows, lower_rows, refs = refs[0], refs[1], refs[2:]
    pieces, refs = refs[:pcol], refs[pcol:]
    dense, parts = refs
    r = lax.axis_index("prow")
    c = lax.axis_index("pcol")
    side = parent_ref.shape[0]
    extent = AR * side
    share = pivots.shape[0]
    for p in range(columns):
        q = (r - p) % columns if columns > 1 else 0
        for level in range(2):
            rows = pl.ds(pl.multiple_of(q * extent, extent), extent)
            blocks = turned[p][0, level * AR : (level + 1) * AR]
            dense[level, rows, :] = blocks.reshape(extent, side)
    parent = parent_ref[...] + parent_other[...]
    upper_sum = sums[0][:side]
    lower_sum = sums[0][side:]
    for t in range(1, count):
        upper_sum += sums[t][:side].astype(F32)
        lower_sum += sums[t][side:].astype(F32)
    hi, lo = split(upper_sum)
    rows = -hi
    upper_rows[...] = rows
    upper_part = ndot(hi, dense[0]) + ndot(lo, dense[0])
    parts[0] = upper_part
    parts[1] = upper_part
    own = pl.ds(pl.multiple_of(c * share, share), share)
    parts[1, own, :] += pivots[...]
    lower_sum += tdot(parent, rows)
    hi, lo = split(lower_sum)
    lower_rows[...] = -hi
    lower_part = ndot(hi, dense[1]) + ndot(lo, dense[1])
    coupling_hi, coupling_lo = split(ndot(rows, dense[1]))
    lower_part += tdot(coupling_hi, parent) + tdot(coupling_lo, parent)
    hi, lo = split(parts[1])
    hi, lo = split(ndot(hi, parent) + ndot(lo, parent))
    parts[1] = lower_part + tdot(parent, hi) + tdot(parent, lo)
    for s in range(pcol):
        theirs = pl.ds(pl.multiple_of((c ^ s) * share, share), share)
        pieces[s][0] = parts[0, theirs, :].astype(pieces[s].dtype)
        pieces[s][1] = parts[1, theirs, :].astype(pieces[s].dtype)


def sum_kernel(pcol, *refs):
    pieces, refs = refs[:pcol], refs[pcol:]
    upper_pivots, lower_pivots, upper_diagonal, lower_diagonal = refs
    total = pieces[0][...]
    for s in range(1, pcol):
        total += pieces[s][...].astype(F32)
    upper_diagonal[...] = upper_pivots[...] + total[0]
    lower_diagonal[...] = lower_pivots[...] + total[1]


def call(kernel, outs, specs, scratch=(), room=32):
    return pl.pallas_call(
        kernel,
        out_shape=outs,
        in_specs=specs,
        out_specs=tuple(VMEM for _ in outs),
        scratch_shapes=scratch,
        cost_estimate=pl.CostEstimate(flops=0, bytes_accessed=0, transcendentals=0),
        compiler_params=pltpu.CompilerParams(vmem_limit_bytes=room << 20),
    )


def per_device(
    known_inverse, upper_panel, upper_slots, upper_pivots, lower_panel, lower_slots, lower_pivots
):
    prow = lax.axis_size("prow")
    pcol = lax.axis_size("pcol")
    columns = upper_panel.shape[1]
    side = upper_panel.shape[2]
    width = known_inverse.shape[1]
    extent = AR * side
    share = upper_pivots.shape[0]
    shape = jax.ShapeDtypeStruct

    def across(x, j):
        return lax.ppermute(x, "pcol", [(c, c ^ j) for c in range(pcol)])

    def flat(r, c):
        return r * pcol + c

    def send(x, even, odd):
        pairs = []
        for r in range(prow):
            for c in range(pcol):
                step = even if c % 2 == holder(r, columns) else odd
                if step is not None:
                    pairs.append((flat(r, c), flat(r ^ step[0], c ^ step[1])))
        return lax.ppermute(x, ("prow", "pcol"), pairs)

    def turned(x):
        moved = []
        for p in range(columns):
            pairs = []
            for a in range(prow):
                for b in range(pcol):
                    pairs.append((a * pcol + b, (b * columns + (a + p) % columns) * pcol + a // columns))
            piece = x
            if columns > 1:
                first = (lax.axis_index("prow") + p) % columns
                piece = lax.dynamic_slice_in_dim(x, first, 1, 0)
            moved.append(lax.ppermute(piece, ("prow", "pcol"), pairs))
        return moved

    packed, packed_own = call(
        functools.partial(pack_kernel, columns),
        (
            shape((columns, 2 * AR + 1, side, side), BF),
            shape((columns, 2 * AR, side, side), BF),
        ),
        [HBM] * 2 + [SMEM] * 2,
        [pltpu.VMEM(upper_panel.shape, BF)] * 2 + [pltpu.SemaphoreType.DMA((2,))],
        60,
    )(upper_panel, lower_panel, upper_slots.T, lower_slots.T)
    packed_all = [packed] + [across(packed, j) for j in range(2, pcol, 2)]
    other_known = across(known_inverse, 1)
    packed_turned = turned(packed_own)
    plan = rounds(prow, columns)
    outs = [shape((2 * side, width), F32)] + [shape((2 * side, width), BF)] * len(plan)
    *sums, parent = call(
        functools.partial(partial_kernel, plan, columns, pcol // 2),
        tuple(outs) + (shape((side, side), BF),),
        [VMEM] * (pcol // 2 + 2),
        [
            pltpu.VMEM((prow // 2, extent, 2 * side), BF),
            pltpu.VMEM((2,) + known_inverse.shape, BF),
        ],
    )(*packed_all, known_inverse, other_known)
    sums = [sums[0]] + [send(x, *steps) for x, steps in zip(sums[1:], plan)]
    parent_other = across(parent, 1)
    outs = [shape((side, width), BF)] * 2 + [shape((2, share, side), F32)]
    outs += [shape((2, share, side), BF)] * (pcol - 1)
    finished = call(
        functools.partial(finish_kernel, len(sums), pcol, columns),
        tuple(outs),
        [VMEM] * (len(sums) + columns + 3),
        [pltpu.VMEM((2, width, side), BF), pltpu.VMEM((2, side, side), F32)],
    )(*sums, *packed_turned, parent, parent_other, upper_pivots)
    upper_rows, lower_rows = finished[:2]
    pieces = [finished[2]] + [across(finished[2 + s], s) for s in range(1, pcol)]
    upper_diagonal, lower_diagonal = call(
        functools.partial(sum_kernel, pcol),
        (shape((share, side), F32), shape((share, side), F32)),
        [VMEM] * (pcol + 2),
    )(*pieces, upper_pivots, lower_pivots)
    return upper_rows, upper_diagonal, lower_rows, lower_diagonal


def solution(mesh):
    placed = (
        P(("pole", "prow"), "pcol"),
        P(("pole", "prow"), "pcol", None, None),
        P("prow", "pcol"),
        P(("pole", "prow", "pcol"), None),
        P(("pole", "prow"), "pcol", None, None),
        P("prow", "pcol"),
        P(("pole", "prow", "pcol"), None),
    )
    return jax.shard_map(
        per_device,
        mesh=mesh,
        in_specs=placed,
        out_specs=(
            P(("pole", "prow"), "pcol"),
            P(("pole", "prow", "pcol"), None),
            P(("pole", "prow"), "pcol"),
            P(("pole", "prow", "pcol"), None),
        ),
        check_vma=False,
    )
```

time: 63.5 us -> 52.5 us (0.83); the launches traced: 62.6 us -> 52.3 us
  starting transfers between devices: 30.8 us -> 20.1 us
  waiting for transfers between devices: 22.8 us -> 24.1 us
  other arithmetic: 0.75 us -> 0 us
    ppermute x6 -> x4, starting transfers between devices: 19.4 us -> 6.66 us  [send(): return lax.ppermute(x, ('prow', 'pcol'), pairs)]
    ppermute x12 -> x6, starting transfers between devices: 7.69 us -> 11.9 us  [across(): return lax.ppermute(x, 'pcol', [(c, c ^ j) for c in range(pcol)])]
    ppermute x3 -> x1, starting transfers between devices: 3.76 us -> 1.6 us  [turned(): moved.append(lax.ppermute(piece, ('prow', 'pcol'), pairs))]
    ppermute x6 -> x4, waiting for transfers between devices: 11.6 us -> 12.8 us  [send(): return lax.ppermute(x, ('prow', 'pcol'), pairs)]
    concatenate x1 -> x0, other arithmetic: 0.75 us -> none  [per_device(): slots = jnp.concatenate([upper_slots, lower_slots], axis=0)]
    ppermute x12 -> x6, waiting for transfers between devices: 11.2 us -> 11.2 us  [across(): return lax.ppermute(x, 'pcol', [(c, c ^ j) for c in range(pcol)])]
    unnamed x12 -> x8, local copies, waits for them, and re-layouts: 1.96 us -> 2.01 us
  transfers between devices with their start and end apart: 21 -> 11, of which waited for: 9 -> 5; matrix products, arithmetic and copies ran while one was open for 1% -> 0% of each run, Pallas kernels for 5% -> 7%
where the time goes in v2:
time: 52.5 us; the launch traced here: 52.3 us
  waiting for transfers between devices  24.1 us (46%)
  starting transfers between devices  20.1 us (38%)
  Pallas kernels  5.45 us (10%)
  local copies, waits for them, and re-layouts  2.01 us (4%)
  between operations  0.69 us (1%)
    ppermute x4, waiting for transfers between devices, send(): return lax.ppermute(x, ('prow', 'pcol'), pairs)  12.8 us
    ppermute x6, starting transfers between devices, across(): return lax.ppermute(x, 'pcol', [(c, c ^ j) for c in range(pcol)])  11.9 us
    ppermute x6, waiting for transfers between devices, across(): return lax.ppermute(x, 'pcol', [(c, c ^ j) for c in range(pcol)])  11.2 us
    ppermute x4, starting transfers between devices, send(): return lax.ppermute(x, ('prow', 'pcol'), pairs)  6.66 us
    pallas_call x1, Pallas kernels, per_device(): call(functools.partial(pack_kernel, columns), (shape((columns, 2 * AR + 1...  2.51 us
    unnamed x8, local copies, waits for them, and re-layouts  2.01 us
    ppermute x1, starting transfers between devices, turned(): moved.append(lax.ppermute(piece, ('prow', 'pcol'), pairs))  1.6 us
    pallas_call x1, Pallas kernels, per_device(): call(functools.partial(partial_kernel, plan, columns, pcol // 2), tuple(o...  1.28 us
  transfers between devices with their start and end apart: 11, of which 5 were waited for; matrix products, arithmetic and copies ran while one was open for 0% of the time, Pallas kernels for 7%

profile of v2, /device:TPU:0, one launch (start us, length us, event | category | flops | bytes accessed | tf_op | source)
XLA Modules:
  0.0 52.3 jit_solution(2654439615514666975)
XLA Ops:
  0.6 0.5 collective-permute-start.1
  1.1 2.5 %shard_map.102 = (bf16[1,9,128,128]{3,2,1,0:T(8,128)(2,1)}, bf16[1,8,128,128]{3,2,1,0:T(8,128)(2,1)}) custom-call(bf16[4,1,128,128]{3,2,1,0:T(8,128)(2,1)} %upper_far.1, bf16[4,1,128,128]{3,2,1,0:T(8,128)(2,1)} %lower_far.1, s32[1,4]{1,0:T(1,128)} %bitcast.2, s32[1,4]{1,0:T(1,128)} %bitcast.3), custom_call_target="tpu_custom_call" | custom-call | tf_op jit(solution)/shard_map/pallas_call | solution.py:238
  3.7 2.5 %collective-permute-start = (bf16[1,9,128,128]{3,2,1,0:T(8,128)(2,1)}, bf16[1,9,128,128]{3,2,1,0:T(8,128)(2,1)S(1)}, u32[]{:S(2)}, u32[]{:S(2)}) collective-permute-start(bf16[1,9,128,128]{3,2,1,0:T(8,128)(2,1)} %get-tuple-element.20.refs_0_), channel_id=1, source_target_pairs={{0,2},{1,3},{2,0},{3,1},{4,6},{5,7},{6,4},{7,5},{8,10},{9,11},{10,... | collective-permute-start | bytes 884744 | tf_op jit(solution)/shard_map/ppermute | solution.py:210
  6.2 1.6 %collective-permute-start.6 = (bf16[1,8,128,128]{3,2,1,0:T(8,128)(2,1)}, bf16[1,8,128,128]{3,2,1,0:T(8,128)(2,1)S(1)}, u32[]{:S(2)}, u32[]{:S(2)}) collective-permute-start(bf16[1,8,128,128]{3,2,1,0:T(8,128)(2,1)} %get-tuple-element.26), channel_id=1, source_target_pairs={{0,0},{1,4},{2,8},{3,12},{4,1},{5,5},{6,9},{7,13},{8,2},{9,6},{10,... | collective-permute-start | bytes 786440 | tf_op jit(solution)/shard_map/ppermute | solution.py:235
  7.8 7.1 %collective-permute-done.refs_1_ = bf16[1,9,128,128]{3,2,1,0:T(8,128)(2,1)S(1)} collective-permute-done((bf16[1,9,128,128]{3,2,1,0:T(8,128)(2,1)}, bf16[1,9,128,128]{3,2,1,0:T(8,128)(2,1)S(1)}, u32[]{:S(2)}, u32[]{:S(2)}) %collective-permute-start) | collective-permute-done | bytes 294944 | tf_op jit(solution)/shard_map/ppermute | solution.py:210
  14.9 0.0 collective-permute-done.1.refs_3_
  14.9 1.0 %copy-done = bf16[512,512]{1,0:T(8,128)(2,1)S(1)} copy-done((bf16[512,512]{1,0:T(8,128)(2,1)S(1)}, bf16[512,512]{1,0:T(8,128)(2,1)}, u32[]{:S(2)}) %copy-start) | copy-done | bytes 524312
  16.0 1.0 %copy-done.1 = bf16[1,9,128,128]{3,2,1,0:T(8,128)(2,1)S(1)} copy-done((bf16[1,9,128,128]{3,2,1,0:T(8,128)(2,1)S(1)}, bf16[1,9,128,128]{3,2,1,0:T(8,128)(2,1)}, u32[]{:S(2)}) %copy-start.1) | copy-done | bytes 294936
  16.9 1.3 %shard_map.103 = (f32[256,512]{1,0:T(8,128)S(1)}, bf16[256,512]{1,0:T(8,128)(2,1)S(1)}, bf16[256,512]{1,0:T(8,128)(2,1)S(1)}, bf16[256,512]{1,0:T(8,128)(2,1)S(1...) custom-call(bf16[1,9,128,128]{3,2,1,0:T(8,128)(2,1)S(1)} %copy-done.1, ...), custom_call_target="tpu_custom_call" | custom-call | tf_op jit(solution)/shard_map/pallas_call | solution.py:253
  18.2 4.6 %collective-permute-start.2 = (bf16[256,512]{1,0:T(8,128)(2,1)S(1)}, bf16[256,512]{1,0:T(8,128)(2,1)S(1)}, u32[]{:S(2)}, u32[]{:S(2)}) collective-permute-start(bf16[256,512]{1,0:T(8,128)(2,1)S(1)} %get-tuple-element.22), channel_id=1, source_target_pairs={{0,8},{1,12},{2,10},{3,14},{4,9},{5,13},{6,11},{7,15},{8,0},{9,4},... | collective-permute-start | bytes 786440 | tf_op jit(solution)/shard_map/ppermute | solution.py:222
  22.9 0.7 %collective-permute-start.3 = (bf16[256,512]{1,0:T(8,128)(2,1)S(1)}, bf16[256,512]{1,0:T(8,128)(2,1)S(1)}, u32[]{:S(2)}, u32[]{:S(2)}) collective-permute-start(bf16[256,512]{1,0:T(8,128)(2,1)S(1)} %get-tuple-element.23), channel_id=1, source_target_pairs={{1,4},{3,6},{4,1},{6,3},{9,12},{11,14},{12,9},{14,11},{17,20},{19,... | collective-permute-start | bytes 786440 | tf_op jit(solution)/shard_map/ppermute | solution.py:222
  23.5 1.4 %collective-permute-start.4 = (bf16[256,512]{1,0:T(8,128)(2,1)S(1)}, bf16[256,512]{1,0:T(8,128)(2,1)S(1)}, u32[]{:S(2)}, u32[]{:S(2)}) collective-permute-start(bf16[256,512]{1,0:T(8,128)(2,1)S(1)} %get-tuple-element.24), channel_id=1, source_target_pairs={{0,9},{1,13},{2,11},{3,15},{4,8},{5,12},{6,10},{7,14},{8,1},{9,5},... | collective-permute-start | bytes 786440 | tf_op jit(solution)/shard_map/ppermute | solution.py:222
  24.9 0.0 collective-permute-start.5
  24.9 1.8 %collective-permute-start.7 = (bf16[128,128]{1,0:T(8,128)(2,1)S(1)}, bf16[128,128]{1,0:T(8,128)(2,1)S(1)}, u32[]{:S(2)}, u32[]{:S(2)}) collective-permute-start(bf16[128,128]{1,0:T(8,128)(2,1)S(1)} %get-tuple-element.27.refs_6_), channel_id=1, source_target_pairs={{0,1},{1,0},{2,3},{3,2},{4,5},{5,4},{6,7},{7,6},{8,9},{9,8},{10,11... | collective-permute-start | bytes 98312 | tf_op jit(solution)/shard_map/ppermute | solution.py:210
  26.7 0.9 %collective-permute-done.7.refs_7_ = bf16[128,128]{1,0:T(8,128)(2,1)S(1)} collective-permute-done((bf16[128,128]{1,0:T(8,128)(2,1)S(1)}, bf16[128,128]{1,0:T(8,128)(2,1)S(1)}, u32[]{:S(2)}, u32[]{:S(2)}) %collective-permute-start.7) | collective-permute-done | bytes 32800 | tf_op jit(solution)/shard_map/ppermute | solution.py:210
  27.6 12.8 %collective-permute-done.2.refs_1_ = bf16[256,512]{1,0:T(8,128)(2,1)S(1)} collective-permute-done((bf16[256,512]{1,0:T(8,128)(2,1)S(1)}, bf16[256,512]{1,0:T(8,128)(2,1)S(1)}, u32[]{:S(2)}, u32[]{:S(2)}) %collective-permute-start.2) | collective-permute-done | bytes 262176 | tf_op jit(solution)/shard_map/ppermute | solution.py:222
  40.4 0.0 collective-permute-done.3.refs_2_
  40.4 0.0 copy-start.3
  40.5 1.0 %shard_map.104 = (bf16[128,512]{1,0:T(8,128)(2,1)}, bf16[128,512]{1,0:T(8,128)(2,1)}, f32[2,32,128]{2,1,0:T(8,128)S(1)}, bf16[2,32,128]{2,1,0:T(8,128)(2,1)S(1)}...) custom-call(f32[256,512]{1,0:T(8,128)S(1)} %get-tuple-element.21.refs_0_, ...), custom_call_target="tpu_custom_call" | custom-call | tf_op jit(solution)/shard_map/pallas_call | solution.py:266
  41.5 5.4 %collective-permute-start.8 = (bf16[2,32,128]{2,1,0:T(8,128)(2,1)S(1)}, bf16[2,32,128]{2,1,0:T(8,128)(2,1)S(1)}, u32[]{:S(2)}, u32[]{:S(2)}) collective-permute-start(bf16[2,32,128]{2,1,0:T(8,128)(2,1)S(1)} %get-tuple-element.30), channel_id=1, source_target_pairs={{0,1},{1,0},{2,3},{3,2},{4,5},{5,4},{6,7},{7,6},{8,9},{9,8},{10,11... | collective-permute-start | bytes 49160 | tf_op jit(solution)/shard_map/ppermute | solution.py:210
  46.9 1.6 %collective-permute-start.9 = (bf16[2,32,128]{2,1,0:T(8,128)(2,1)S(1)}, bf16[2,32,128]{2,1,0:T(8,128)(2,1)S(1)}, u32[]{:S(2)}, u32[]{:S(2)}) collective-permute-start(bf16[2,32,128]{2,1,0:T(8,128)(2,1)S(1)} %get-tuple-element.31), channel_id=1, source_target_pairs={{0,2},{1,3},{2,0},{3,1},{4,6},{5,7},{6,4},{7,5},{8,10},{9,11},{10,... | collective-permute-start | bytes 49160 | tf_op jit(solution)/shard_map/ppermute | solution.py:210
  48.5 2.1 %collective-permute-done.9.refs_2_ = bf16[2,32,128]{2,1,0:T(8,128)(2,1)S(1)} collective-permute-done((bf16[2,32,128]{2,1,0:T(8,128)(2,1)S(1)}, bf16[2,32,128]{2,1,0:T(8,128)(2,1)S(1)}, u32[]{:S(2)}, u32[]{:S(2)}) %collective-permute-start.9) | collective-permute-done | bytes 16416 | tf_op jit(solution)/shard_map/ppermute | solution.py:210
  50.6 1.1 %collective-permute-done.10.refs_3_ = bf16[2,32,128]{2,1,0:T(8,128)(2,1)S(1)} collective-permute-done((bf16[2,32,128]{2,1,0:T(8,128)(2,1)S(1)}, bf16[2,32,128]{2,1,0:T(8,128)(2,1)S(1)}, u32[]{:S(2)}, u32[]{:S(2)}) %collective-permute-start.10) | collective-permute-done | bytes 16416 | tf_op jit(solution)/shard_map/ppermute | solution.py:210
  51.7 0.6 %shard_map.105 = (f32[32,128]{1,0:T(8,128)}, f32[32,128]{1,0:T(8,128)}) custom-call(f32[2,32,128]{2,1,0:T(8,128)S(1)} %get-tuple-element.29.refs_0_, bf16[2,32,128]{2,1,0:T(8,128)(2,1)S(1)} %collective-permute-done.8.refs_1_, bf16[2,32,128]{2,1,0:T(8,128)(2,1)S(1)} %collective-permute-done.9.refs_2_, ...), custom_call_target="tpu_custom_call" | custom-call | tf_op jit(solution)/shard_map/pallas_call | solution.py:274
  (10 shorter events, 0.0 us)
Async XLA Ops:
  0.6 14.3 %collective-permute-start.1 = (bf16[512,512]{1,0:T(8,128)(2,1)}, bf16[512,512]{1,0:T(8,128)(2,1)S(1)}, u32[]{:S(2)}, u32[]{:S(2)}) collective-permute-start(bf16[512,512]{1,0:T(8,128)(2,1)} %refs_2_.1), channel_id=1, source_target_pairs={{0,1},{1,0},{2,3},{3,2},{4,5},{5,4},{6,7},{7,6},{8,9},{9,8},{10,11... | collective-permute-start | bytes 1572872 | tf_op jit(solution)/shard_map/ppermute | solution.py:210
  3.7 11.3 %collective-permute-start = (bf16[1,9,128,128]{3,2,1,0:T(8,128)(2,1)}, bf16[1,9,128,128]{3,2,1,0:T(8,128)(2,1)S(1)}, u32[]{:S(2)}, u32[]{:S(2)}) collective-permute-start(bf16[1,9,128,128]{3,2,1,0:T(8,128)(2,1)} %get-tuple-element.20.refs_0_), channel_id=1, source_target_pairs={{0,2},{1,3},{2,0},{3,1},{4,6},{5,7},{6,4},{7,5},{8,10},{9,11},{10,... | collective-permute-start | bytes 884744 | tf_op jit(solution)/shard_map/ppermute | solution.py:210
  6.2 18.7 %collective-permute-start.6 = (bf16[1,8,128,128]{3,2,1,0:T(8,128)(2,1)}, bf16[1,8,128,128]{3,2,1,0:T(8,128)(2,1)S(1)}, u32[]{:S(2)}, u32[]{:S(2)}) collective-permute-start(bf16[1,8,128,128]{3,2,1,0:T(8,128)(2,1)} %get-tuple-element.26), channel_id=1, source_target_pairs={{0,0},{1,4},{2,8},{3,12},{4,1},{5,5},{6,9},{7,13},{8,2},{9,6},{10,... | collective-permute-start | bytes 786440 | tf_op jit(solution)/shard_map/ppermute | solution.py:235
  14.9 1.0 %copy-start = (bf16[512,512]{1,0:T(8,128)(2,1)S(1)}, bf16[512,512]{1,0:T(8,128)(2,1)}, u32[]{:S(2)}) copy-start(bf16[512,512]{1,0:T(8,128)(2,1)} %refs_2_.1) | copy-start | bytes 1572868
  16.0 1.0 %copy-start.1 = (bf16[1,9,128,128]{3,2,1,0:T(8,128)(2,1)S(1)}, bf16[1,9,128,128]{3,2,1,0:T(8,128)(2,1)}, u32[]{:S(2)}) copy-start(bf16[1,9,128,128]{3,2,1,0:T(8,128)(2,1)} %get-tuple-element.20.refs_0_) | copy-start | bytes 884740
  16.9 23.5 %copy-start.2 = (f32[32,128]{1,0:T(8,128)S(1)}, f32[32,128]{1,0:T(8,128)}, u32[]{:S(2)}) copy-start(f32[32,128]{1,0:T(8,128)} %refs_4_.1) | copy-start | bytes 49156
  18.2 22.2 %collective-permute-start.2 = (bf16[256,512]{1,0:T(8,128)(2,1)S(1)}, bf16[256,512]{1,0:T(8,128)(2,1)S(1)}, u32[]{:S(2)}, u32[]{:S(2)}) collective-permute-start(bf16[256,512]{1,0:T(8,128)(2,1)S(1)} %get-tuple-element.22), channel_id=1, source_target_pairs={{0,8},{1,12},{2,10},{3,14},{4,9},{5,13},{6,11},{7,15},{8,0},{9,4},... | collective-permute-start | bytes 786440 | tf_op jit(solution)/shard_map/ppermute | solution.py:222
  22.9 17.6 %collective-permute-start.3 = (bf16[256,512]{1,0:T(8,128)(2,1)S(1)}, bf16[256,512]{1,0:T(8,128)(2,1)S(1)}, u32[]{:S(2)}, u32[]{:S(2)}) collective-permute-start(bf16[256,512]{1,0:T(8,128)(2,1)S(1)} %get-tuple-element.23), channel_id=1, source_target_pairs={{1,4},{3,6},{4,1},{6,3},{9,12},{11,14},{12,9},{14,11},{17,20},{19,... | collective-permute-start | bytes 786440 | tf_op jit(solution)/shard_map/ppermute | solution.py:222
  23.5 16.9 %collective-permute-start.4 = (bf16[256,512]{1,0:T(8,128)(2,1)S(1)}, bf16[256,512]{1,0:T(8,128)(2,1)S(1)}, u32[]{:S(2)}, u32[]{:S(2)}) collective-permute-start(bf16[256,512]{1,0:T(8,128)(2,1)S(1)} %get-tuple-element.24), channel_id=1, source_target_pairs={{0,9},{1,13},{2,11},{3,15},{4,8},{5,12},{6,10},{7,14},{8,1},{9,5},... | collective-permute-start | bytes 786440 | tf_op jit(solution)/shard_map/ppermute | solution.py:222
  24.9 15.5 %collective-permute-start.5 = (bf16[256,512]{1,0:T(8,128)(2,1)S(1)}, bf16[256,512]{1,0:T(8,128)(2,1)S(1)}, u32[]{:S(2)}, u32[]{:S(2)}) collective-permute-start(bf16[256,512]{1,0:T(8,128)(2,1)S(1)} %get-tuple-element.25), channel_id=1, source_target_pairs={{0,1},{1,5},{2,3},{3,7},{4,0},{5,4},{6,2},{7,6},{8,9},{9,13},{10,1... | collective-permute-start | bytes 786440 | tf_op jit(solution)/shard_map/ppermute | solution.py:222
  24.9 2.7 %collective-permute-start.7 = (bf16[128,128]{1,0:T(8,128)(2,1)S(1)}, bf16[128,128]{1,0:T(8,128)(2,1)S(1)}, u32[]{:S(2)}, u32[]{:S(2)}) collective-permute-start(bf16[128,128]{1,0:T(8,128)(2,1)S(1)} %get-tuple-element.27.refs_6_), channel_id=1, source_target_pairs={{0,1},{1,0},{2,3},{3,2},{4,5},{5,4},{6,7},{7,6},{8,9},{9,8},{10,11... | collective-permute-start | bytes 98312 | tf_op jit(solution)/shard_map/ppermute | solution.py:210
  40.4 11.3 %copy-start.3 = (f32[32,128]{1,0:T(8,128)S(1)}, f32[32,128]{1,0:T(8,128)}, u32[]{:S(2)}) copy-start(f32[32,128]{1,0:T(8,128)} %refs_5_.1) | copy-start | bytes 49156
  41.5 7.0 %collective-permute-start.8 = (bf16[2,32,128]{2,1,0:T(8,128)(2,1)S(1)}, bf16[2,32,128]{2,1,0:T(8,128)(2,1)S(1)}, u32[]{:S(2)}, u32[]{:S(2)}) collective-permute-start(bf16[2,32,128]{2,1,0:T(8,128)(2,1)S(1)} %get-tuple-element.30), channel_id=1, source_target_pairs={{0,1},{1,0},{2,3},{3,2},{4,5},{5,4},{6,7},{7,6},{8,9},{9,8},{10,11... | collective-permute-start | bytes 49160 | tf_op jit(solution)/shard_map/ppermute | solution.py:210
  46.9 3.7 %collective-permute-start.9 = (bf16[2,32,128]{2,1,0:T(8,128)(2,1)S(1)}, bf16[2,32,128]{2,1,0:T(8,128)(2,1)S(1)}, u32[]{:S(2)}, u32[]{:S(2)}) collective-permute-start(bf16[2,32,128]{2,1,0:T(8,128)(2,1)S(1)} %get-tuple-element.31), channel_id=1, source_target_pairs={{0,2},{1,3},{2,0},{3,1},{4,6},{5,7},{6,4},{7,5},{8,10},{9,11},{10,... | collective-permute-start | bytes 49160 | tf_op jit(solution)/shard_map/ppermute | solution.py:210
  48.5 3.2 %collective-permute-start.10 = (bf16[2,32,128]{2,1,0:T(8,128)(2,1)S(1)}, bf16[2,32,128]{2,1,0:T(8,128)(2,1)S(1)}, u32[]{:S(2)}, u32[]{:S(2)}) collective-permute-start(bf16[2,32,128]{2,1,0:T(8,128)(2,1)S(1)} %get-tuple-element.32), channel_id=1, source_target_pairs={{0,3},{1,2},{2,1},{3,0},{4,7},{5,6},{6,5},{7,4},{8,11},{9,10},{10,... | collective-permute-start | bytes 49160 | tf_op jit(solution)/shard_map/ppermute | solution.py:210

commit v3 on v2

--- a/solution.py
+++ b/solution.py
@@ -8,6 +8,7 @@
 from jax.sharding import PartitionSpec as P
 
 AR = 4
+TURN_FLOPS = 4 << 30
 BF = jnp.bfloat16
 F32 = jnp.float32
 VMEM = pl.BlockSpec(memory_space=pltpu.VMEM)
@@ -125,30 +126,95 @@
         parent[...] = jnp.zeros_like(parent)
 
 
-def finish_kernel(count, pcol, columns, *refs):
-    sums, refs = refs[:count], refs[count:]
-    turned, refs = refs[:columns], refs[columns:]
-    parent_ref, parent_other, pivots, refs = refs[0], refs[1], refs[2], refs[3:]
-    upper_rows, lower_rows, refs = refs[0], refs[1], refs[2:]
-    pieces, refs = refs[:pcol], refs[pcol:]
-    dense, parts = refs
+def halving_kernel(columns, halves, *refs):
+    packed, refs = refs[:halves], refs[halves:]
+    own_known, other_known, first, second, third, fourth, own, parent, dense = refs
     r = lax.axis_index("prow")
     c = lax.axis_index("pcol")
-    side = parent_ref.shape[0]
+    side = parent.shape[0]
     extent = AR * side
-    share = pivots.shape[0]
+    holds = c % 2 == holder(r, columns)
+
+    def slot(k):
+        return k // (2 * columns) * columns + k % columns
+
+    for j in range(halves):
+        for i in range(columns):
+            k = (c ^ (2 * j)) * columns + i
+            for level in range(2):
+                blocks = packed[j][i, level * AR : (level + 1) * AR]
+                dense[slot(k), :, level * side : (level + 1) * side] = blocks.reshape(extent, side)
+
+            @pl.when(k == r)
+            def _():
+                parent[...] = packed[j][i, 2 * AR]
+
+    @pl.when(holds)
+    def _():
+        panel = dense[slot(r)]
+        first[...] = tdot(panel, other_known[...]).astype(BF)
+        own[...] = tdot(panel, own_known[...])
+        second[:side, :side] = parent[...]
+        panel = dense[slot(r ^ 2)]
+        third[...] = tdot(panel, own_known[...])
+        fourth[...] = tdot(panel, other_known[...])
+
+    @pl.when(jnp.logical_not(holds))
+    def _():
+        panel = dense[slot(r ^ 3)]
+        first[...] = tdot(panel, own_known[...]).astype(BF)
+        second[...] = tdot(panel, other_known[...]).astype(BF)
+        panel = dense[slot(r ^ 1)]
+        third[...] = tdot(panel, other_known[...])
+        fourth[...] = tdot(panel, own_known[...])
+
+
+def add_kernel(columns, kept, arrived, total):
+    holds = lax.axis_index("pcol") % 2 == holder(lax.axis_index("prow"), columns)
+
+    @pl.when(holds)
+    def _():
+        total[...] = (kept[...] + arrived[...].astype(F32)).astype(BF)
+
+    @pl.when(jnp.logical_not(holds))
+    def _():
+        total[...] = kept[...].astype(BF)
+
+
+def turn_kernel(columns, *refs):
+    turned, dense = refs[:-1], refs[-1]
+    r = lax.axis_index("prow")
+    side = dense.shape[2]
+    extent = AR * side
     for p in range(columns):
         q = (r - p) % columns if columns > 1 else 0
         for level in range(2):
             rows = pl.ds(pl.multiple_of(q * extent, extent), extent)
             blocks = turned[p][0, level * AR : (level + 1) * AR]
             dense[level, rows, :] = blocks.reshape(extent, side)
-    parent = parent_ref[...] + parent_other[...]
-    upper_sum = sums[0][:side]
-    lower_sum = sums[0][side:]
-    for t in range(1, count):
-        upper_sum += sums[t][:side].astype(F32)
-        lower_sum += sums[t][side:].astype(F32)
+
+
+def finish_kernel(halving, count, pcol, columns, *refs):
+    sums, refs = refs[:count], refs[count:]
+    dense, parent_ref, parent_other, pivots, refs = refs[0], refs[1], refs[2], refs[3], refs[4:]
+    upper_rows, lower_rows, refs = refs[0], refs[1], refs[2:]
+    pieces, refs = refs[:pcol], refs[pcol:]
+    parts = refs[0]
+    r = lax.axis_index("prow")
+    c = lax.axis_index("pcol")
+    side = parent_ref.shape[0]
+    share = pivots.shape[0]
+    if halving:
+        holds = c % 2 == holder(r, columns)
+        parent = jnp.where(holds, parent_ref[...], parent_other[:side, :side])
+        total = jnp.where(holds, sums[0][...], sums[1][...].astype(F32))
+        total += sums[2][...].astype(F32) + sums[3][...].astype(F32)
+    else:
+        parent = parent_ref[...] + parent_other[...]
+        total = sums[0][...]
+        for t in range(1, count):
+            total += sums[t][...].astype(F32)
+    upper_sum, lower_sum = total[:side], total[side:]
     hi, lo = split(upper_sum)
     rows = -hi
     upper_rows[...] = rows
@@ -182,14 +248,14 @@
     lower_diagonal[...] = lower_pivots[...] + total[1]
 
 
-def call(kernel, outs, specs, scratch=(), room=32):
+def call(kernel, outs, specs, scratch=(), room=32, flops=0):
     return pl.pallas_call(
         kernel,
         out_shape=outs,
         in_specs=specs,
         out_specs=tuple(VMEM for _ in outs),
         scratch_shapes=scratch,
-        cost_estimate=pl.CostEstimate(flops=0, bytes_accessed=0, transcendentals=0),
+        cost_estimate=pl.CostEstimate(flops=flops, bytes_accessed=0, transcendentals=0),
         compiler_params=pltpu.CompilerParams(vmem_limit_bytes=room << 20),
     )
 
@@ -220,6 +286,28 @@
                 if step is not None:
                     pairs.append((flat(r, c), flat(r ^ step[0], c ^ step[1])))
         return lax.ppermute(x, ("prow", "pcol"), pairs)
+
+    def trade(x, held_step, held_other, step, other):
+        pairs = []
+        for r in range(prow):
+            for c in range(pcol):
+                if c % 2 == holder(r, columns):
+                    pairs.append((flat(r, c), flat(r ^ held_step, c ^ held_other)))
+                else:
+                    pairs.append((flat(r, c), flat(r ^ step, c ^ other)))
+        return lax.ppermute(x, ("prow", "pcol"), pairs)
+
+    def add(kept, arrived):
+        out = (shape(arrived.shape, BF),)
+        return call(functools.partial(add_kernel, columns), out, [VMEM] * 2)(kept, arrived)[0]
+
+    def turn(moved):
+        return call(
+            functools.partial(turn_kernel, columns),
+            (shape((2, width, side), BF),),
+            [VMEM] * columns,
+            flops=TURN_FLOPS,
+        )(*moved)[0]
 
     def turned(x):
         moved = []
@@ -248,27 +336,46 @@
     packed_all = [packed] + [across(packed, j) for j in range(2, pcol, 2)]
     other_known = across(known_inverse, 1)
     packed_turned = turned(packed_own)
-    plan = rounds(prow, columns)
-    outs = [shape((2 * side, width), F32)] + [shape((2 * side, width), BF)] * len(plan)
-    *sums, parent = call(
-        functools.partial(partial_kernel, plan, columns, pcol // 2),
-        tuple(outs) + (shape((side, side), BF),),
-        [VMEM] * (pcol // 2 + 2),
-        [
-            pltpu.VMEM((prow // 2, extent, 2 * side), BF),
-            pltpu.VMEM((2,) + known_inverse.shape, BF),
-        ],
-    )(*packed_all, known_inverse, other_known)
-    sums = [sums[0]] + [send(x, *steps) for x, steps in zip(sums[1:], plan)]
-    parent_other = across(parent, 1)
+    part = (2 * side, width)
+    halving = prow == 4 and columns == 1
+    if halving:
+        first, second, third, fourth, own, parent = call(
+            functools.partial(halving_kernel, columns, pcol // 2),
+            (shape(part, BF), shape(part, BF), shape(part, F32), shape(part, F32))
+            + (shape(part, F32), shape((side, side), BF)),
+            [VMEM] * (pcol // 2 + 2),
+            [pltpu.VMEM((prow // 2, extent, 2 * side), BF)],
+        )(*packed_all, known_inverse, other_known)
+        first = trade(first, 0, 1, 1, 0)
+        parent_other = trade(second, 0, 1, 1, 0)
+        dense_turned = turn(packed_turned)
+        first, dense_turned = lax.optimization_barrier((first, dense_turned))
+        third = trade(add(third, first), 2, 0, 1, 1)
+        fourth = trade(add(fourth, parent_other), 2, 1, 1, 0)
+        sums = [own, first, third, fourth]
+    else:
+        plan = rounds(prow, columns)
+        outs = [shape((2 * side, width), F32)] + [shape((2 * side, width), BF)] * len(plan)
+        *sums, parent = call(
+            functools.partial(partial_kernel, plan, columns, pcol // 2),
+            tuple(outs) + (shape((side, side), BF),),
+            [VMEM] * (pcol // 2 + 2),
+            [
+                pltpu.VMEM((prow // 2, extent, 2 * side), BF),
+                pltpu.VMEM((2,) + known_inverse.shape, BF),
+            ],
+        )(*packed_all, known_inverse, other_known)
+        sums = [sums[0]] + [send(x, *steps) for x, steps in zip(sums[1:], plan)]
+        parent_other = across(parent, 1)
+        dense_turned = turn(packed_turned)
     outs = [shape((side, width), BF)] * 2 + [shape((2, share, side), F32)]
     outs += [shape((2, share, side), BF)] * (pcol - 1)
     finished = call(
-        functools.partial(finish_kernel, len(sums), pcol, columns),
+        functools.partial(finish_kernel, halving, len(sums), pcol, columns),
         tuple(outs),
-        [VMEM] * (len(sums) + columns + 3),
-        [pltpu.VMEM((2, width, side), BF), pltpu.VMEM((2, side, side), F32)],
-    )(*sums, *packed_turned, parent, parent_other, upper_pivots)
+        [VMEM] * (len(sums) + 4),
+        [pltpu.VMEM((2, side, side), F32)],
+    )(*sums, dense_turned, parent, parent_other, upper_pivots)
     upper_rows, lower_rows = finished[:2]
     pieces = [finished[2]] + [across(finished[2 + s], s) for s in range(1, pcol)]
     upper_diagonal, lower_diagonal = call(

time: 52.5 us -> 48.3 us (0.920)
  starting transfers between devices: 20.1 us -> 15 us
  waiting for transfers between devices: 24.1 us -> 25.3 us
    ppermute x6 -> x5, starting transfers between devices: 11.9 us -> 7.96 us  [across(): return lax.ppermute(x, 'pcol', [(c, c ^ j) for c in range(pcol)])]
    ppermute x4, waiting for transfers between devices: 12.8 us -> 15.1 us  [trade(): return lax.ppermute(x, ('prow', 'pcol'), pairs)]
    ppermute x4, starting transfers between devices: 6.66 us -> 5.41 us  [trade(): return lax.ppermute(x, ('prow', 'pcol'), pairs)]
    ppermute x6 -> x5, waiting for transfers between devices: 11.2 us -> 10.2 us  [across(): return lax.ppermute(x, 'pcol', [(c, c ^ j) for c in range(pcol)])]
    pallas_call x2 -> x5, Pallas kernels: 2.32 us -> 1.95 us  [the longest x1 1 us: per_device(): call(functools.partial(finish_kernel, halving, len(sums), pcol, columns),...]
  transfers between devices with their start and end apart: 11 -> 10, of which waited for: 5 -> 6; matrix products, arithmetic and copies ran while one was open for 0% -> 0% of each run, Pallas kernels for 7% -> 7%
where the time goes in v3:
time: 48.3 us; the launch traced here: 48.1 us
  waiting for transfers between devices  25.3 us (52%)
  starting transfers between devices  15 us (31%)
  Pallas kernels  5.08 us (11%)
  local copies, waits for them, and re-layouts  2.01 us (4%)
  between operations  0.7 us (1%)
    ppermute x4, waiting for transfers between devices, trade(): return lax.ppermute(x, ('prow', 'pcol'), pairs)  15.1 us
    ppermute x5, waiting for transfers between devices, across(): return lax.ppermute(x, 'pcol', [(c, c ^ j) for c in range(pcol)])  10.2 us
    ppermute x5, starting transfers between devices, across(): return lax.ppermute(x, 'pcol', [(c, c ^ j) for c in range(pcol)])  7.96 us
    ppermute x4, starting transfers between devices, trade(): return lax.ppermute(x, ('prow', 'pcol'), pairs)  5.41 us
    pallas_call x1, Pallas kernels, per_device(): call(functools.partial(pack_kernel, columns), (shape((columns, 2 * AR + 1...  2.51 us
    unnamed x8, local copies, waits for them, and re-layouts  2.01 us
    ppermute x1, starting transfers between devices, turned(): moved.append(lax.ppermute(piece, ('prow', 'pcol'), pairs))  1.6 us
    pallas_call x1, Pallas kernels, per_device(): call(functools.partial(finish_kernel, halving, len(sums), pcol, columns),...  1 us
  transfers between devices with their start and end apart: 10, of which 6 were waited for; matrix products, arithmetic and copies ran while one was open for 0% of the time, Pallas kernels for 7%

profile of v3, /device:TPU:0, one launch (start us, length us, event | category | flops | bytes accessed | tf_op | source)
XLA Modules:
  0.0 48.1 jit_solution(12875896198664116166)
XLA Ops:
  0.6 0.5 %collective-permute-start.1 = (bf16[512,512]{1,0:T(8,128)(2,1)}, bf16[512,512]{1,0:T(8,128)(2,1)S(1)}, u32[]{:S(2)}, u32[]{:S(2)}) collective-permute-start(bf16[512,512]{1,0:T(8,128)(2,1)} %refs_2_.1), channel_id=1, source_target_pairs={{0,1},{1,0},{2,3},{3,2},{4,5},{5,4},{6,7},{7,6},{8,9},{9,8},{10,11... | collective-permute-start | bytes 1572872 | tf_op jit(solution)/shard_map/ppermute | solution.py:276
  1.1 2.5 %shard_map.102 = (bf16[1,9,128,128]{3,2,1,0:T(8,128)(2,1)}, bf16[1,8,128,128]{3,2,1,0:T(8,128)(2,1)}) custom-call(bf16[4,1,128,128]{3,2,1,0:T(8,128)(2,1)} %upper_far.1, bf16[4,1,128,128]{3,2,1,0:T(8,128)(2,1)} %lower_far.1, s32[1,4]{1,0:T(1,128)} %bitcast.2, s32[1,4]{1,0:T(1,128)} %bitcast.3), custom_call_target="tpu_custom_call" | custom-call | tf_op jit(solution)/shard_map/pallas_call | solution.py:326
  3.7 2.6 %collective-permute-start = (bf16[1,9,128,128]{3,2,1,0:T(8,128)(2,1)}, bf16[1,9,128,128]{3,2,1,0:T(8,128)(2,1)S(1)}, u32[]{:S(2)}, u32[]{:S(2)}) collective-permute-start(bf16[1,9,128,128]{3,2,1,0:T(8,128)(2,1)} %get-tuple-element.22.refs_0_), channel_id=1, source_target_pairs={{0,2},{1,3},{2,0},{3,1},{4,6},{5,7},{6,4},{7,5},{8,10},{9,11},{10,... | collective-permute-start | bytes 884744 | tf_op jit(solution)/shard_map/ppermute | solution.py:276
  6.2 1.6 %collective-permute-start.3 = (bf16[1,8,128,128]{3,2,1,0:T(8,128)(2,1)}, bf16[1,8,128,128]{3,2,1,0:T(8,128)(2,1)S(1)}, u32[]{:S(2)}, u32[]{:S(2)}) collective-permute-start(bf16[1,8,128,128]{3,2,1,0:T(8,128)(2,1)} %get-tuple-element.25), channel_id=1, source_target_pairs={{0,0},{1,4},{2,8},{3,12},{4,1},{5,5},{6,9},{7,13},{8,2},{9,6},{10,... | collective-permute-start | bytes 786440 | tf_op jit(solution)/shard_map/ppermute | solution.py:323
  7.8 6.9 %collective-permute-done.refs_1_ = bf16[1,9,128,128]{3,2,1,0:T(8,128)(2,1)S(1)} collective-permute-done((bf16[1,9,128,128]{3,2,1,0:T(8,128)(2,1)}, bf16[1,9,128,128]{3,2,1,0:T(8,128)(2,1)S(1)}, u32[]{:S(2)}, u32[]{:S(2)}) %collective-permute-start) | collective-permute-done | bytes 294944 | tf_op jit(solution)/shard_map/ppermute | solution.py:276
  14.8 0.0 collective-permute-done.1.refs_3_
  14.8 1.0 %copy-done = bf16[512,512]{1,0:T(8,128)(2,1)S(1)} copy-done((bf16[512,512]{1,0:T(8,128)(2,1)S(1)}, bf16[512,512]{1,0:T(8,128)(2,1)}, u32[]{:S(2)}) %copy-start) | copy-done | bytes 524312
  15.8 1.0 %copy-done.1 = bf16[1,9,128,128]{3,2,1,0:T(8,128)(2,1)S(1)} copy-done((bf16[1,9,128,128]{3,2,1,0:T(8,128)(2,1)S(1)}, bf16[1,9,128,128]{3,2,1,0:T(8,128)(2,1)}, u32[]{:S(2)}) %copy-start.1) | copy-done | bytes 294936
  16.8 0.8 %shard_map.103 = (bf16[256,512]{1,0:T(8,128)(2,1)S(1)}, bf16[256,512]{1,0:T(8,128)(2,1)S(1)}, f32[256,512]{1,0:T(8,128)S(1)}, f32[256,512]{1,0:T(8,128)S(1)}, f3...) custom-call(bf16[1,9,128,128]{3,2,1,0:T(8,128)(2,1)S(1)} %copy-done.1, ...), custom_call_target="tpu_custom_call" | custom-call | tf_op jit(solution)/shard_map/pallas_call | solution.py:342
  17.6 0.1 collective-permute-start.2
  17.7 2.5 %collective-permute-start.5 = (bf16[256,512]{1,0:T(8,128)(2,1)S(1)}, bf16[256,512]{1,0:T(8,128)(2,1)S(1)}, u32[]{:S(2)}, u32[]{:S(2)}) collective-permute-start(bf16[256,512]{1,0:T(8,128)(2,1)S(1)} %get-tuple-element.29), channel_id=1, source_target_pairs={{0,1},{1,5},{2,3},{3,7},{4,0},{5,4},{6,2},{7,6},{8,9},{9,13},{10,1... | collective-permute-start | bytes 786440 | tf_op jit(solution)/shard_map/ppermute | solution.py:298
  20.2 5.8 %collective-permute-done.2.arrived.refs_1_ = bf16[256,512]{1,0:T(8,128)(2,1)S(1)} collective-permute-done((bf16[256,512]{1,0:T(8,128)(2,1)S(1)}, bf16[256,512]{1,0:T(8,128)(2,1)S(1)}, u32[]{:S(2)}, u32[]{:S(2)}) %collective-permute-start.2) | collective-permute-done | bytes 262176 | tf_op jit(solution)/shard_map/ppermute | solution.py:298
  26.1 2.8 %collective-permute-start.4 = (bf16[256,512]{1,0:T(8,128)(2,1)S(1)}, bf16[256,512]{1,0:T(8,128)(2,1)S(1)}, u32[]{:S(2)}, u32[]{:S(2)}) collective-permute-start(bf16[256,512]{1,0:T(8,128)(2,1)S(1)} %shard_map.105), channel_id=1, source_target_pairs={{0,8},{1,4},{2,10},{3,6},{4,1},{5,13},{6,3},{7,15},{8,0},{9,12},{1... | collective-permute-start | bytes 786440 | tf_op jit(solution)/shard_map/ppermute | solution.py:298
  29.0 0.1 collective-permute-start.6
  29.0 7.2 %collective-permute-done.4.refs_2_ = bf16[256,512]{1,0:T(8,128)(2,1)S(1)} collective-permute-done((bf16[256,512]{1,0:T(8,128)(2,1)S(1)}, bf16[256,512]{1,0:T(8,128)(2,1)S(1)}, u32[]{:S(2)}, u32[]{:S(2)}) %collective-permute-start.4) | collective-permute-done | bytes 262176 | tf_op jit(solution)/shard_map/ppermute | solution.py:298
  36.3 2.1 %collective-permute-done.6.refs_3_ = bf16[256,512]{1,0:T(8,128)(2,1)S(1)} collective-permute-done((bf16[256,512]{1,0:T(8,128)(2,1)S(1)}, bf16[256,512]{1,0:T(8,128)(2,1)S(1)}, u32[]{:S(2)}, u32[]{:S(2)}) %collective-permute-start.6) | collective-permute-done | bytes 262176 | tf_op jit(solution)/shard_map/ppermute | solution.py:298
  38.3 1.0 %shard_map.107 = (bf16[128,512]{1,0:T(8,128)(2,1)}, bf16[128,512]{1,0:T(8,128)(2,1)}, f32[2,32,128]{2,1,0:T(8,128)S(1)}, bf16[2,32,128]{2,1,0:T(8,128)(2,1)S(1)}...) custom-call(f32[256,512]{1,0:T(8,128)S(1)} %get-tuple-element.23.refs_0_, ...), custom_call_target="tpu_custom_call" | custom-call | tf_op jit(solution)/shard_map/pallas_call | solution.py:373
  39.3 2.5 %collective-permute-start.7 = (bf16[2,32,128]{2,1,0:T(8,128)(2,1)S(1)}, bf16[2,32,128]{2,1,0:T(8,128)(2,1)S(1)}, u32[]{:S(2)}, u32[]{:S(2)}) collective-permute-start(bf16[2,32,128]{2,1,0:T(8,128)(2,1)S(1)} %get-tuple-element.34), channel_id=1, source_target_pairs={{0,1},{1,0},{2,3},{3,2},{4,5},{5,4},{6,7},{7,6},{8,9},{9,8},{10,11... | collective-permute-start | bytes 49160 | tf_op jit(solution)/shard_map/ppermute | solution.py:276
  41.8 2.4 %collective-permute-start.8 = (bf16[2,32,128]{2,1,0:T(8,128)(2,1)S(1)}, bf16[2,32,128]{2,1,0:T(8,128)(2,1)S(1)}, u32[]{:S(2)}, u32[]{:S(2)}) collective-permute-start(bf16[2,32,128]{2,1,0:T(8,128)(2,1)S(1)} %get-tuple-element.35), channel_id=1, source_target_pairs={{0,2},{1,3},{2,0},{3,1},{4,6},{5,7},{6,4},{7,5},{8,10},{9,11},{10,... | collective-permute-start | bytes 49160 | tf_op jit(solution)/shard_map/ppermute | solution.py:276
  44.2 0.0 collective-permute-start.9
  44.2 0.0 collective-permute-done.7.refs_1_
  44.2 1.7 %collective-permute-done.8.refs_2_ = bf16[2,32,128]{2,1,0:T(8,128)(2,1)S(1)} collective-permute-done((bf16[2,32,128]{2,1,0:T(8,128)(2,1)S(1)}, bf16[2,32,128]{2,1,0:T(8,128)(2,1)S(1)}, u32[]{:S(2)}, u32[]{:S(2)}) %collective-permute-start.8) | collective-permute-done | bytes 16416 | tf_op jit(solution)/shard_map/ppermute | solution.py:276
  45.9 1.5 %collective-permute-done.9.refs_3_ = bf16[2,32,128]{2,1,0:T(8,128)(2,1)S(1)} collective-permute-done((bf16[2,32,128]{2,1,0:T(8,128)(2,1)S(1)}, bf16[2,32,128]{2,1,0:T(8,128)(2,1)S(1)}, u32[]{:S(2)}, u32[]{:S(2)}) %collective-permute-start.9) | collective-permute-done | bytes 16416 | tf_op jit(solution)/shard_map/ppermute | solution.py:276
  47.4 0.6 %shard_map.108 = (f32[32,128]{1,0:T(8,128)}, f32[32,128]{1,0:T(8,128)}) custom-call(f32[2,32,128]{2,1,0:T(8,128)S(1)} %get-tuple-element.33.refs_0_, bf16[2,32,128]{2,1,0:T(8,128)(2,1)S(1)} %collective-permute-done.7.refs_1_, bf16[2,32,128]{2,1,0:T(8,128)(2,1)S(1)} %collective-permute-done.8.refs_2_, bf16[2,32,128]{2,1,0:T(8,128)(2,1)S(1)} %collective-permute-done.9.refs_3_, ...), custom_call_target="tpu_custom_call" | custom-call | tf_op jit(solution)/shard_map/pallas_call | solution.py:381
  (11 shorter events, 0.1 us)
Async XLA Ops:
  0.6 14.2 %collective-permute-start.1 = (bf16[512,512]{1,0:T(8,128)(2,1)}, bf16[512,512]{1,0:T(8,128)(2,1)S(1)}, u32[]{:S(2)}, u32[]{:S(2)}) collective-permute-start(bf16[512,512]{1,0:T(8,128)(2,1)} %refs_2_.1), channel_id=1, source_target_pairs={{0,1},{1,0},{2,3},{3,2},{4,5},{5,4},{6,7},{7,6},{8,9},{9,8},{10,11... | collective-permute-start | bytes 1572872 | tf_op jit(solution)/shard_map/ppermute | solution.py:276
  3.7 11.1 %collective-permute-start = (bf16[1,9,128,128]{3,2,1,0:T(8,128)(2,1)}, bf16[1,9,128,128]{3,2,1,0:T(8,128)(2,1)S(1)}, u32[]{:S(2)}, u32[]{:S(2)}) collective-permute-start(bf16[1,9,128,128]{3,2,1,0:T(8,128)(2,1)} %get-tuple-element.22.refs_0_), channel_id=1, source_target_pairs={{0,2},{1,3},{2,0},{3,1},{4,6},{5,7},{6,4},{7,5},{8,10},{9,11},{10,... | collective-permute-start | bytes 884744 | tf_op jit(solution)/shard_map/ppermute | solution.py:276
  6.2 14.0 %collective-permute-start.3 = (bf16[1,8,128,128]{3,2,1,0:T(8,128)(2,1)}, bf16[1,8,128,128]{3,2,1,0:T(8,128)(2,1)S(1)}, u32[]{:S(2)}, u32[]{:S(2)}) collective-permute-start(bf16[1,8,128,128]{3,2,1,0:T(8,128)(2,1)} %get-tuple-element.25), channel_id=1, source_target_pairs={{0,0},{1,4},{2,8},{3,12},{4,1},{5,5},{6,9},{7,13},{8,2},{9,6},{10,... | collective-permute-start | bytes 786440 | tf_op jit(solution)/shard_map/ppermute | solution.py:323
  14.8 1.0 %copy-start = (bf16[512,512]{1,0:T(8,128)(2,1)S(1)}, bf16[512,512]{1,0:T(8,128)(2,1)}, u32[]{:S(2)}) copy-start(bf16[512,512]{1,0:T(8,128)(2,1)} %refs_2_.1) | copy-start | bytes 1572868
  15.8 1.0 %copy-start.1 = (bf16[1,9,128,128]{3,2,1,0:T(8,128)(2,1)S(1)}, bf16[1,9,128,128]{3,2,1,0:T(8,128)(2,1)}, u32[]{:S(2)}) copy-start(bf16[1,9,128,128]{3,2,1,0:T(8,128)(2,1)} %get-tuple-element.22.refs_0_) | copy-start | bytes 884740
  17.6 8.4 %collective-permute-start.2 = (bf16[256,512]{1,0:T(8,128)(2,1)S(1)}, bf16[256,512]{1,0:T(8,128)(2,1)S(1)}, u32[]{:S(2)}, u32[]{:S(2)}) collective-permute-start(bf16[256,512]{1,0:T(8,128)(2,1)S(1)} %get-tuple-element.24), channel_id=1, source_target_pairs={{0,1},{1,5},{2,3},{3,7},{4,0},{5,4},{6,2},{7,6},{8,9},{9,13},{10,1... | collective-permute-start | bytes 786440 | tf_op jit(solution)/shard_map/ppermute | solution.py:298
  17.7 11.2 %collective-permute-start.5 = (bf16[256,512]{1,0:T(8,128)(2,1)S(1)}, bf16[256,512]{1,0:T(8,128)(2,1)S(1)}, u32[]{:S(2)}, u32[]{:S(2)}) collective-permute-start(bf16[256,512]{1,0:T(8,128)(2,1)S(1)} %get-tuple-element.29), channel_id=1, source_target_pairs={{0,1},{1,5},{2,3},{3,7},{4,0},{5,4},{6,2},{7,6},{8,9},{9,13},{10,1... | collective-permute-start | bytes 786440 | tf_op jit(solution)/shard_map/ppermute | solution.py:298
  26.1 10.1 %collective-permute-start.4 = (bf16[256,512]{1,0:T(8,128)(2,1)S(1)}, bf16[256,512]{1,0:T(8,128)(2,1)S(1)}, u32[]{:S(2)}, u32[]{:S(2)}) collective-permute-start(bf16[256,512]{1,0:T(8,128)(2,1)S(1)} %shard_map.105), channel_id=1, source_target_pairs={{0,8},{1,4},{2,10},{3,6},{4,1},{5,13},{6,3},{7,15},{8,0},{9,12},{1... | collective-permute-start | bytes 786440 | tf_op jit(solution)/shard_map/ppermute | solution.py:298
  28.9 9.4 %copy-start.2 = (f32[32,128]{1,0:T(8,128)S(1)}, f32[32,128]{1,0:T(8,128)}, u32[]{:S(2)}) copy-start(f32[32,128]{1,0:T(8,128)} %refs_4_.1) | copy-start | bytes 49156
  29.0 9.4 %collective-permute-start.6 = (bf16[256,512]{1,0:T(8,128)(2,1)S(1)}, bf16[256,512]{1,0:T(8,128)(2,1)S(1)}, u32[]{:S(2)}, u32[]{:S(2)}) collective-permute-start(bf16[256,512]{1,0:T(8,128)(2,1)S(1)} %shard_map.106), channel_id=1, source_target_pairs={{0,9},{1,5},{2,11},{3,7},{4,0},{5,12},{6,2},{7,14},{8,1},{9,13},{1... | collective-permute-start | bytes 786440 | tf_op jit(solution)/shard_map/ppermute | solution.py:298
  38.3 9.1 %copy-start.3 = (f32[32,128]{1,0:T(8,128)S(1)}, f32[32,128]{1,0:T(8,128)}, u32[]{:S(2)}) copy-start(f32[32,128]{1,0:T(8,128)} %refs_5_.1) | copy-start | bytes 49156
  39.3 4.9 %collective-permute-start.7 = (bf16[2,32,128]{2,1,0:T(8,128)(2,1)S(1)}, bf16[2,32,128]{2,1,0:T(8,128)(2,1)S(1)}, u32[]{:S(2)}, u32[]{:S(2)}) collective-permute-start(bf16[2,32,128]{2,1,0:T(8,128)(2,1)S(1)} %get-tuple-element.34), channel_id=1, source_target_pairs={{0,1},{1,0},{2,3},{3,2},{4,5},{5,4},{6,7},{7,6},{8,9},{9,8},{10,11... | collective-permute-start | bytes 49160 | tf_op jit(solution)/shard_map/ppermute | solution.py:276
  41.8 4.1 %collective-permute-start.8 = (bf16[2,32,128]{2,1,0:T(8,128)(2,1)S(1)}, bf16[2,32,128]{2,1,0:T(8,128)(2,1)S(1)}, u32[]{:S(2)}, u32[]{:S(2)}) collective-permute-start(bf16[2,32,128]{2,1,0:T(8,128)(2,1)S(1)} %get-tuple-element.35), channel_id=1, source_target_pairs={{0,2},{1,3},{2,0},{3,1},{4,6},{5,7},{6,4},{7,5},{8,10},{9,11},{10,... | collective-permute-start | bytes 49160 | tf_op jit(solution)/shard_map/ppermute | solution.py:276
  44.2 3.2 %collective-permute-start.9 = (bf16[2,32,128]{2,1,0:T(8,128)(2,1)S(1)}, bf16[2,32,128]{2,1,0:T(8,128)(2,1)S(1)}, u32[]{:S(2)}, u32[]{:S(2)}) collective-permute-start(bf16[2,32,128]{2,1,0:T(8,128)(2,1)S(1)} %get-tuple-element.36), channel_id=1, source_target_pairs={{0,3},{1,2},{2,1},{3,0},{4,7},{5,6},{6,5},{7,4},{8,11},{9,10},{10,... | collective-permute-start | bytes 49160 | tf_op jit(solution)/shard_map/ppermute | solution.py:276

commit v4 on v3

--- a/solution.py
+++ b/solution.py
@@ -8,7 +8,8 @@
 from jax.sharding import PartitionSpec as P
 
 AR = 4
-TURN_FLOPS = 4 << 30
+TURN_FLOPS = 1 << 28
+NEAR_FLOPS = 1 << 30
 BF = jnp.bfloat16
 F32 = jnp.float32
 VMEM = pl.BlockSpec(memory_space=pltpu.VMEM)
@@ -29,32 +30,21 @@
     return hi, (x - hi.astype(F32)).astype(BF)
 
 
-def place(dense, panel, column, slots):
-    for s in range(AR):
-        v = slots[column, s]
-
-        @pl.when((v >= 0) & (v < AR))
-        def _():
-            dense[v] = panel[s, column]
-
-
-def pack_kernel(
-    columns, upper_far, lower_far, upper_slots, lower_slots, packed, turned, upper, lower, arrived
-):
-    copies = [
-        pltpu.make_async_copy(upper_far, upper, arrived.at[0]),
-        pltpu.make_async_copy(lower_far, lower, arrived.at[1]),
-    ]
-    for copy in copies:
-        copy.start()
-    packed[...] = jnp.zeros_like(packed)
-    for copy in copies:
-        copy.wait()
-    for i in range(columns):
-        place(packed.at[i, :AR], upper, i, upper_slots)
-        place(packed.at[i, AR : 2 * AR], lower, i, lower_slots)
-        packed[i, 2 * AR] = lower[0, i]
-        turned[i] = packed[i, : 2 * AR]
+def lay(dense, panel, slots_ref, level):
+    side = panel.shape[-1]
+    slots = slots_ref[...].astype(F32)
+    for v in range(AR):
+        total = None
+        for s in range(AR):
+            index = level * AR + s
+            chosen = (slots[index : index + 1] == v).astype(BF)
+            term = panel[s * side : (s + 1) * side, :] * chosen
+            total = term if total is None else total + term
+        dense[v * side : (v + 1) * side, :] = total
+
+
+def copy_kernel(known, near):
+    near[...] = known[...]
 
 
 def holder(k, columns):
@@ -75,7 +65,8 @@
 
 
 def partial_kernel(plan, columns, halves, *refs):
-    packed, refs = refs[:halves], refs[halves:]
+    panels = refs[:halves], refs[halves : 2 * halves]
+    slots, refs = refs[2 * halves : 3 * halves], refs[3 * halves :]
     own_known, other_known, refs = refs[0], refs[1], refs[2:]
     own, refs = refs[0], refs[1:]
     outs, refs = refs[: len(plan)], refs[len(plan) :]
@@ -95,12 +86,12 @@
         for i in range(columns):
             k = (c ^ (2 * j)) * columns + i
             for level in range(2):
-                blocks = packed[j][i, level * AR : (level + 1) * AR]
-                dense[slot(k), :, level * side : (level + 1) * side] = blocks.reshape(extent, side)
+                columns_of = pl.ds(level * side, side)
+                lay(dense.at[slot(k), :, columns_of], panels[level][j].at[i], slots[j].at[i], level)
 
             @pl.when(k == r)
             def _():
-                parent[...] = packed[j][i, 2 * AR]
+                parent[...] = panels[1][j][i, :side]
 
     for n, (even, odd) in enumerate(plan):
 
@@ -127,7 +118,8 @@
 
 
 def halving_kernel(columns, halves, *refs):
-    packed, refs = refs[:halves], refs[halves:]
+    panels = refs[:halves], refs[halves : 2 * halves]
+    slots, refs = refs[2 * halves : 3 * halves], refs[3 * halves :]
     own_known, other_known, first, second, third, fourth, own, parent, dense = refs
     r = lax.axis_index("prow")
     c = lax.axis_index("pcol")
@@ -142,12 +134,12 @@
         for i in range(columns):
             k = (c ^ (2 * j)) * columns + i
             for level in range(2):
-                blocks = packed[j][i, level * AR : (level + 1) * AR]
-                dense[slot(k), :, level * side : (level + 1) * side] = blocks.reshape(extent, side)
+                columns_of = pl.ds(level * side, side)
+                lay(dense.at[slot(k), :, columns_of], panels[level][j].at[i], slots[j].at[i], level)
 
             @pl.when(k == r)
             def _():
-                parent[...] = packed[j][i, 2 * AR]
+                parent[...] = panels[1][j][i, :side]
 
     @pl.when(holds)
     def _():
@@ -190,8 +182,9 @@
         q = (r - p) % columns if columns > 1 else 0
         for level in range(2):
             rows = pl.ds(pl.multiple_of(q * extent, extent), extent)
-            blocks = turned[p][0, level * AR : (level + 1) * AR]
-            dense[level, rows, :] = blocks.reshape(extent, side)
+            panel = turned[p].at[0, pl.ds(level * extent, extent), :]
+            slots = turned[p].at[0, pl.ds(2 * extent, 4 * AR), :]
+            lay(dense.at[level, rows, :], panel, slots, level)
 
 
 def finish_kernel(halving, count, pcol, columns, *refs):
@@ -287,6 +280,14 @@
                     pairs.append((flat(r, c), flat(r ^ step[0], c ^ step[1])))
         return lax.ppermute(x, ("prow", "pcol"), pairs)
 
+    def swing(x):
+        pairs = []
+        for a in range(prow):
+            for b in range(pcol):
+                c = a ^ 2 if a // 2 == b // 2 else b // 2 * 2 + a % 2
+                pairs.append((flat(a, b), flat(b, c)))
+        return lax.ppermute(x, ("prow", "pcol"), pairs)
+
     def trade(x, held_step, held_other, step, other):
         pairs = []
         for r in range(prow):
@@ -323,33 +324,34 @@
             moved.append(lax.ppermute(piece, ("prow", "pcol"), pairs))
         return moved
 
-    packed, packed_own = call(
-        functools.partial(pack_kernel, columns),
-        (
-            shape((columns, 2 * AR + 1, side, side), BF),
-            shape((columns, 2 * AR, side, side), BF),
-        ),
-        [HBM] * 2 + [SMEM] * 2,
-        [pltpu.VMEM(upper_panel.shape, BF)] * 2 + [pltpu.SemaphoreType.DMA((2,))],
-        60,
-    )(upper_panel, lower_panel, upper_slots.T, lower_slots.T)
-    packed_all = [packed] + [across(packed, j) for j in range(2, pcol, 2)]
+    slots = jnp.concatenate([upper_slots, lower_slots, lower_slots, lower_slots], axis=0).T
+    packed = [
+        jnp.swapaxes(upper_panel, 0, 1).reshape(columns, extent, side),
+        jnp.swapaxes(lower_panel, 0, 1).reshape(columns, extent, side),
+        jnp.broadcast_to(slots[:, :, None].astype(BF), (columns, 4 * AR, side)),
+    ]
+    packed_all = []
+    for x in packed:
+        packed_all += [x] + [across(x, j) for j in range(2, pcol, 2)]
     other_known = across(known_inverse, 1)
-    packed_turned = turned(packed_own)
+    near = call(copy_kernel, (shape(known_inverse.shape, BF),), [VMEM], flops=NEAR_FLOPS)(known_inverse)[0]
+    halving = prow == 4 and columns == 1
+    whole = jnp.concatenate(packed, axis=1)
+    packed_turned = [swing(whole)] if halving else turned(whole)
     part = (2 * side, width)
-    halving = prow == 4 and columns == 1
     if halving:
         first, second, third, fourth, own, parent = call(
             functools.partial(halving_kernel, columns, pcol // 2),
             (shape(part, BF), shape(part, BF), shape(part, F32), shape(part, F32))
             + (shape(part, F32), shape((side, side), BF)),
-            [VMEM] * (pcol // 2 + 2),
+            [VMEM] * (3 * pcol // 2 + 2),
             [pltpu.VMEM((prow // 2, extent, 2 * side), BF)],
-        )(*packed_all, known_inverse, other_known)
+        )(*packed_all, near, other_known)
         first = trade(first, 0, 1, 1, 0)
         parent_other = trade(second, 0, 1, 1, 0)
         dense_turned = turn(packed_turned)
         first, dense_turned = lax.optimization_barrier((first, dense_turned))
+        dense_turned = across(dense_turned, 2)
         third = trade(add(third, first), 2, 0, 1, 1)
         fourth = trade(add(fourth, parent_other), 2, 1, 1, 0)
         sums = [own, first, third, fourth]
@@ -359,12 +361,12 @@
         *sums, parent = call(
             functools.partial(partial_kernel, plan, columns, pcol // 2),
             tuple(outs) + (shape((side, side), BF),),
-            [VMEM] * (pcol // 2 + 2),
+            [VMEM] * (3 * pcol // 2 + 2),
             [
                 pltpu.VMEM((prow // 2, extent, 2 * side), BF),
                 pltpu.VMEM((2,) + known_inverse.shape, BF),
             ],
-        )(*packed_all, known_inverse, other_known)
+        )(*packed_all, near, other_known)
         sums = [sums[0]] + [send(x, *steps) for x, steps in zip(sums[1:], plan)]
         parent_other = across(parent, 1)
         dense_turned = turn(packed_turned)

time: 48.3 us -> 44.1 us (0.913)
  starting transfers between devices: 15 us -> 10.5 us
  other arithmetic: 0 us -> 2.38 us
  Pallas kernels: 5.08 us -> 3 us
  local copies, waits for them, and re-layouts: 2.01 us -> 0.1 us
  waiting for transfers between devices: 25.3 us -> 27.2 us
    ppermute x1, waiting for transfers between devices: 0.01 us -> 12 us  [swing(): return lax.ppermute(x, ('prow', 'pcol'), pairs)]
    ppermute x5 -> x8, waiting for transfers between devices: 10.2 us -> 4.39 us  [across(): return lax.ppermute(x, 'pcol', [(c, c ^ j) for c in range(pcol)])]
    ppermute x4, waiting for transfers between devices: 15.1 us -> 10.8 us  [trade(): return lax.ppermute(x, ('prow', 'pcol'), pairs)]
    ppermute x4, starting transfers between devices: 5.41 us -> 1.42 us  [trade(): return lax.ppermute(x, ('prow', 'pcol'), pairs)]
    pallas_call x1, Pallas kernels: 2.51 us -> 0.03 us  [per_device(): call(copy_kernel, (shape(known_inverse.shape, BF),), [VMEM], flops=NEAR_F...]
    unnamed x8 -> x10, local copies, waits for them, and re-layouts: 2.01 us -> 0.02 us
    ppermute x1, starting transfers between devices: 1.6 us -> 0.15 us  [swing(): return lax.ppermute(x, ('prow', 'pcol'), pairs)]
    another operation x0 -> x2, other arithmetic: none -> 1.32 us
  transfers between devices with their start and end apart: 10 -> 13, of which waited for: 6 -> 6; matrix products, arithmetic and copies ran while one was open for 0% -> 6% of each run, Pallas kernels for 7% -> 3%
where the time goes in v4:
time: 44.1 us; the launch traced here: 43.9 us
  waiting for transfers between devices  27.2 us (62%)
  starting transfers between devices  10.5 us (24%)
  Pallas kernels  3 us (7%)
  other arithmetic  2.38 us (5%)
  between operations  0.76 us (2%)
    ppermute x1, waiting for transfers between devices, swing(): return lax.ppermute(x, ('prow', 'pcol'), pairs)  12 us
    ppermute x4, waiting for transfers between devices, trade(): return lax.ppermute(x, ('prow', 'pcol'), pairs)  10.8 us
    ppermute x8, starting transfers between devices, across(): return lax.ppermute(x, 'pcol', [(c, c ^ j) for c in range(pcol)])  8.91 us
    ppermute x8, waiting for transfers between devices, across(): return lax.ppermute(x, 'pcol', [(c, c ^ j) for c in range(pcol)])  4.39 us
    ppermute x4, starting transfers between devices, trade(): return lax.ppermute(x, ('prow', 'pcol'), pairs)  1.42 us
    another operation x2, other arithmetic  1.32 us
    pallas_call x1, Pallas kernels, per_device(): call(functools.partial(halving_kernel, columns, pcol // 2), (shape(part,...  1.03 us
    pallas_call x1, Pallas kernels, per_device(): call(functools.partial(finish_kernel, halving, len(sums), pcol, columns),...  1.01 us
  transfers between devices with their start and end apart: 13, of which 6 were waited for; matrix products, arithmetic and copies ran while one was open for 6% of the time, Pallas kernels for 3%

profile of v4, /device:TPU:0, one launch (start us, length us, event | category | flops | bytes accessed | tf_op | source)
XLA Modules:
  0.0 43.9 jit_solution(6671204832381012073)
XLA Ops:
  0.6 0.5 %collective-permute-start.3 = (bf16[512,512]{1,0:T(8,128)(2,1)}, bf16[512,512]{1,0:T(8,128)(2,1)S(1)}, u32[]{:S(2)}, u32[]{:S(2)}) collective-permute-start(bf16[512,512]{1,0:T(8,128)(2,1)} %known.1), channel_id=1, source_target_pairs={{0,1},{1,0},{2,3},{3,2},{4,5},{5,4},{6,7},{7,6},{8,9},{9,8},{10,11... | collective-permute-start | bytes 1572872 | tf_op jit(solution)/shard_map/ppermute | solution.py:269
  1.2 2.6 %collective-permute-start = (bf16[1,512,128]{2,1,0:T(8,128)(2,1)}, bf16[1,512,128]{2,1,0:T(8,128)(2,1)S(1)}, u32[]{:S(2)}, u32[]{:S(2)}) collective-permute-start(bf16[1,512,128]{2,1,0:T(8,128)(2,1)} %bitcast.4), channel_id=1, source_target_pairs={{0,2},{1,3},{2,0},{3,1},{4,6},{5,7},{6,4},{7,5},{8,10},{9,11},{10,... | collective-permute-start | bytes 393224 | tf_op jit(solution)/shard_map/ppermute | solution.py:269
  3.7 0.1 collective-permute-start.1
  3.8 0.7 %convert.8 = bf16[4,1]{0,1:T(2,128)(2,1)S(1)} convert(s32[4,1]{0,1:T(1,128)} %param.9) | non-fusion elementwise | flops 4 | bytes 24 | tf_op jit(solution)/shard_map/convert
  4.5 0.7 %convert.9 = bf16[4,1]{0,1:T(2,128)(2,1)S(1)} convert(s32[4,1]{0,1:T(1,128)} %param.12) | non-fusion elementwise | flops 4 | bytes 24 | tf_op jit(solution)/shard_map/convert.1
  5.1 0.1 maximum_bitcast_fusion
  5.2 0.1 broadcast_in_dim.2.refs_4_
  5.3 1.9 %collective-permute-start.2 = (bf16[1,16,128]{2,1,0:T(8,128)(2,1)S(1)}, bf16[1,16,128]{2,1,0:T(8,128)(2,1)S(1)}, u32[]{:S(2)}, u32[]{:S(2)}) collective-permute-start(bf16[1,16,128]{2,1,0:T(8,128)(2,1)S(1)} %broadcast_in_dim.2.refs_4_), channel_id=1, source_target_pairs={{0,2},{1,3},{2,0},{3,1},{4,6},{5,7},{6,4},{7,5},{8,10},{9,11},{10,... | collective-permute-start | bytes 12296 | tf_op jit(solution)/shard_map/ppermute | solution.py:269
  7.2 1.0 %pad_maximum_fusion = bf16[1,1040,128]{2,1,0:T(8,128)(2,1)S(1)} fusion(bf16[1,16,128]{2,1,0:T(8,128)(2,1)S(1)} %broadcast_in_dim.2.refs_4_, bf16[1,512,128]{2,1,0:T(8,128)(2,1)} %bitcast.8, bf16[1,512,128]{2,1,0:T(8,128)(2,1)} %bitcast.5), kind=kLoop, calls=%fused_computation | loop fusion | flops 798720 | bytes 532480 | tf_op jit(solution)/shard_map/concatenate | solution.py:339
  8.2 0.1 collective-permute-start.5
  8.4 2.5 %collective-permute-done.2.refs_5_ = bf16[1,16,128]{2,1,0:T(8,128)(2,1)S(1)} collective-permute-done((bf16[1,16,128]{2,1,0:T(8,128)(2,1)S(1)}, bf16[1,16,128]{2,1,0:T(8,128)(2,1)S(1)}, u32[]{:S(2)}, u32[]{:S(2)}) %collective-permute-start.2) | collective-permute-done | bytes 4128 | tf_op jit(solution)/shard_map/ppermute | solution.py:269
  11.0 1.0 %shard_map.103 = (bf16[256,512]{1,0:T(8,128)(2,1)S(1)}, bf16[256,512]{1,0:T(8,128)(2,1)S(1)}, f32[256,512]{1,0:T(8,128)S(1)}, f32[256,512]{1,0:T(8,128)S(1)}, f3...) custom-call(bf16[1,512,128]{2,1,0:T(8,128)(2,1)S(1)} %bitcast.6, ...), custom_call_target="tpu_custom_call" | custom-call | tf_op jit(solution)/shard_map/pallas_call | solution.py:343
  12.1 1.2 %collective-permute-start.7 = (bf16[256,512]{1,0:T(8,128)(2,1)S(1)}, bf16[256,512]{1,0:T(8,128)(2,1)S(1)}, u32[]{:S(2)}, u32[]{:S(2)}) collective-permute-start(bf16[256,512]{1,0:T(8,128)(2,1)S(1)} %get-tuple-element.25), channel_id=1, source_target_pairs={{0,1},{1,5},{2,3},{3,7},{4,0},{5,4},{6,2},{7,6},{8,9},{9,13},{10,1... | collective-permute-start | bytes 786440 | tf_op jit(solution)/shard_map/ppermute | solution.py:299
  13.3 12.0 %collective-permute-done.5.refs_0_ = bf16[1,1040,128]{2,1,0:T(8,128)(2,1)S(1)} collective-permute-done((bf16[1,1040,128]{2,1,0:T(8,128)(2,1)S(1)}, bf16[1,1040,128]{2,1,0:T(8,128)(2,1)S(1)}, u32[]{:S(2)}, u32[]{:S(2)}) %collective-permute-start.5) | collective-permute-done | bytes 266272 | tf_op jit(solution)/shard_map/ppermute | solution.py:289
  25.3 0.2 shard_map.104
  25.5 0.1 shard_map.105
  25.6 0.3 collective-permute-done.7.arrived.refs_6_
  26.0 1.9 %collective-permute-start.9 = (bf16[2,512,128]{2,1,0:T(8,128)(2,1)S(1)}, bf16[2,512,128]{2,1,0:T(8,128)(2,1)S(1)}, u32[]{:S(2)}, u32[]{:S(2)}) collective-permute-start(bf16[2,512,128]{2,1,0:T(8,128)(2,1)S(1)} %shard_map.104), channel_id=1, source_target_pairs={{0,2},{1,3},{2,0},{3,1},{4,6},{5,7},{6,4},{7,5},{8,10},{9,11},{10,... | collective-permute-start | bytes 786440 | tf_op jit(solution)/shard_map/ppermute | solution.py:269
  28.0 7.4 %collective-permute-done.6.refs_2_ = bf16[256,512]{1,0:T(8,128)(2,1)S(1)} collective-permute-done((bf16[256,512]{1,0:T(8,128)(2,1)S(1)}, bf16[256,512]{1,0:T(8,128)(2,1)S(1)}, u32[]{:S(2)}, u32[]{:S(2)}) %collective-permute-start.6) | collective-permute-done | bytes 262176 | tf_op jit(solution)/shard_map/ppermute | solution.py:299
  35.4 3.1 %collective-permute-done.8.refs_3_ = bf16[256,512]{1,0:T(8,128)(2,1)S(1)} collective-permute-done((bf16[256,512]{1,0:T(8,128)(2,1)S(1)}, bf16[256,512]{1,0:T(8,128)(2,1)S(1)}, u32[]{:S(2)}, u32[]{:S(2)}) %collective-permute-start.8) | collective-permute-done | bytes 262176 | tf_op jit(solution)/shard_map/ppermute | solution.py:299
  38.5 1.0 %shard_map.107 = (bf16[128,512]{1,0:T(8,128)(2,1)}, bf16[128,512]{1,0:T(8,128)(2,1)}, f32[2,32,128]{2,1,0:T(8,128)S(1)}, bf16[2,32,128]{2,1,0:T(8,128)(2,1)S(1)}...) custom-call(f32[256,512]{1,0:T(8,128)S(1)} %get-tuple-element.20.refs_0_, ...), custom_call_target="tpu_custom_call" | custom-call | tf_op jit(solution)/shard_map/pallas_call | solution.py:375
  39.5 1.9 %collective-permute-start.12 = (bf16[2,32,128]{2,1,0:T(8,128)(2,1)S(1)}, bf16[2,32,128]{2,1,0:T(8,128)(2,1)S(1)}, u32[]{:S(2)}, u32[]{:S(2)}) collective-permute-start(bf16[2,32,128]{2,1,0:T(8,128)(2,1)S(1)} %get-tuple-element.32), channel_id=1, source_target_pairs={{0,3},{1,2},{2,1},{3,0},{4,7},{5,6},{6,5},{7,4},{8,11},{9,10},{10,... | collective-permute-start | bytes 49160 | tf_op jit(solution)/shard_map/ppermute | solution.py:269
  41.4 1.9 %collective-permute-done.11.refs_2_ = bf16[2,32,128]{2,1,0:T(8,128)(2,1)S(1)} collective-permute-done((bf16[2,32,128]{2,1,0:T(8,128)(2,1)S(1)}, bf16[2,32,128]{2,1,0:T(8,128)(2,1)S(1)}, u32[]{:S(2)}, u32[]{:S(2)}) %collective-permute-start.11) | collective-permute-done | bytes 16416 | tf_op jit(solution)/shard_map/ppermute | solution.py:269
  43.3 0.6 %shard_map.108 = (f32[32,128]{1,0:T(8,128)}, f32[32,128]{1,0:T(8,128)}) custom-call(f32[2,32,128]{2,1,0:T(8,128)S(1)} %get-tuple-element.29.refs_0_, bf16[2,32,128]{2,1,0:T(8,128)(2,1)S(1)} %collective-permute-done.10.refs_1_, bf16[2,32,128]{2,1,0:T(8,128)(2,1)S(1)} %collective-permute-done.11.refs_2_, ...), custom_call_target="tpu_custom_call" | custom-call | tf_op jit(solution)/shard_map/pallas_call | solution.py:383
  (24 shorter events, 0.4 us)
Async XLA Ops:
  0.6 7.8 %copy-start.4 = (bf16[512,512]{1,0:T(8,128)(2,1)S(1)}, bf16[512,512]{1,0:T(8,128)(2,1)}, u32[]{:S(2)}) copy-start(bf16[512,512]{1,0:T(8,128)(2,1)} %known.1) | copy-start | bytes 1572868
  0.6 10.3 %collective-permute-start.3 = (bf16[512,512]{1,0:T(8,128)(2,1)}, bf16[512,512]{1,0:T(8,128)(2,1)S(1)}, u32[]{:S(2)}, u32[]{:S(2)}) collective-permute-start(bf16[512,512]{1,0:T(8,128)(2,1)} %known.1), channel_id=1, source_target_pairs={{0,1},{1,0},{2,3},{3,2},{4,5},{5,4},{6,7},{7,6},{8,9},{9,8},{10,11... | collective-permute-start | bytes 1572872 | tf_op jit(solution)/shard_map/ppermute | solution.py:269
  1.2 9.8 %collective-permute-start = (bf16[1,512,128]{2,1,0:T(8,128)(2,1)}, bf16[1,512,128]{2,1,0:T(8,128)(2,1)S(1)}, u32[]{:S(2)}, u32[]{:S(2)}) collective-permute-start(bf16[1,512,128]{2,1,0:T(8,128)(2,1)} %bitcast.4), channel_id=1, source_target_pairs={{0,2},{1,3},{2,0},{3,1},{4,6},{5,7},{6,4},{7,5},{8,10},{9,11},{10,... | collective-permute-start | bytes 393224 | tf_op jit(solution)/shard_map/ppermute | solution.py:269
  3.7 7.2 %collective-permute-start.1 = (bf16[1,512,128]{2,1,0:T(8,128)(2,1)}, bf16[1,512,128]{2,1,0:T(8,128)(2,1)S(1)}, u32[]{:S(2)}, u32[]{:S(2)}) collective-permute-start(bf16[1,512,128]{2,1,0:T(8,128)(2,1)} %bitcast.7), channel_id=1, source_target_pairs={{0,2},{1,3},{2,0},{3,1},{4,6},{5,7},{6,4},{7,5},{8,10},{9,11},{10,... | collective-permute-start | bytes 393224 | tf_op jit(solution)/shard_map/ppermute | solution.py:269
  5.3 5.6 %collective-permute-start.2 = (bf16[1,16,128]{2,1,0:T(8,128)(2,1)S(1)}, bf16[1,16,128]{2,1,0:T(8,128)(2,1)S(1)}, u32[]{:S(2)}, u32[]{:S(2)}) collective-permute-start(bf16[1,16,128]{2,1,0:T(8,128)(2,1)S(1)} %broadcast_in_dim.2.refs_4_), channel_id=1, source_target_pairs={{0,2},{1,3},{2,0},{3,1},{4,6},{5,7},{6,4},{7,5},{8,10},{9,11},{10,... | collective-permute-start | bytes 12296 | tf_op jit(solution)/shard_map/ppermute | solution.py:269
  8.2 2.7 %copy-start = (bf16[4,1,128,128]{3,2,1,0:T(8,128)(2,1)S(1)}, bf16[4,1,128,128]{3,2,1,0:T(8,128)(2,1)}, u32[]{:S(2)}) copy-start(bf16[4,1,128,128]{3,2,1,0:T(8,128)(2,1)} %param.8) | copy-start | bytes 393220
  8.2 2.7 %copy-start.1 = (bf16[4,1,128,128]{3,2,1,0:T(8,128)(2,1)S(1)}, bf16[4,1,128,128]{3,2,1,0:T(8,128)(2,1)}, u32[]{:S(2)}) copy-start(bf16[4,1,128,128]{3,2,1,0:T(8,128)(2,1)} %param.11) | copy-start | bytes 393220
  8.2 17.0 %collective-permute-start.5 = (bf16[1,1040,128]{2,1,0:T(8,128)(2,1)S(1)}, bf16[1,1040,128]{2,1,0:T(8,128)(2,1)S(1)}, u32[]{:S(2)}, u32[]{:S(2)}) collective-permute-start(bf16[1,1040,128]{2,1,0:T(8,128)(2,1)S(1)} %pad_maximum_fusion), channel_id=1, source_target_pairs={{0,2},{1,6},{2,10},{3,14},{4,3},{5,7},{6,11},{7,15},{8,0},{9,4},{1... | collective-permute-start | bytes 798728 | tf_op jit(solution)/shard_map/ppermute | solution.py:289
  12.0 13.5 %collective-permute-start.4 = (bf16[256,512]{1,0:T(8,128)(2,1)S(1)}, bf16[256,512]{1,0:T(8,128)(2,1)S(1)}, u32[]{:S(2)}, u32[]{:S(2)}) collective-permute-start(bf16[256,512]{1,0:T(8,128)(2,1)S(1)} %get-tuple-element.21), channel_id=1, source_target_pairs={{0,1},{1,5},{2,3},{3,7},{4,0},{5,4},{6,2},{7,6},{8,9},{9,13},{10,1... | collective-permute-start | bytes 786440 | tf_op jit(solution)/shard_map/ppermute | solution.py:299
  12.1 13.8 %collective-permute-start.7 = (bf16[256,512]{1,0:T(8,128)(2,1)S(1)}, bf16[256,512]{1,0:T(8,128)(2,1)S(1)}, u32[]{:S(2)}, u32[]{:S(2)}) collective-permute-start(bf16[256,512]{1,0:T(8,128)(2,1)S(1)} %get-tuple-element.25), channel_id=1, source_target_pairs={{0,1},{1,5},{2,3},{3,7},{4,0},{5,4},{6,2},{7,6},{8,9},{9,13},{10,1... | collective-permute-start | bytes 786440 | tf_op jit(solution)/shard_map/ppermute | solution.py:299
  25.5 9.8 %collective-permute-start.6 = (bf16[256,512]{1,0:T(8,128)(2,1)S(1)}, bf16[256,512]{1,0:T(8,128)(2,1)S(1)}, u32[]{:S(2)}, u32[]{:S(2)}) collective-permute-start(bf16[256,512]{1,0:T(8,128)(2,1)S(1)} %shard_map.105), channel_id=1, source_target_pairs={{0,8},{1,4},{2,10},{3,6},{4,1},{5,13},{6,3},{7,15},{8,0},{9,12},{1... | collective-permute-start | bytes 786440 | tf_op jit(solution)/shard_map/ppermute | solution.py:299
  25.9 12.6 %copy-start.2 = (f32[32,128]{1,0:T(8,128)S(1)}, f32[32,128]{1,0:T(8,128)}, u32[]{:S(2)}) copy-start(f32[32,128]{1,0:T(8,128)} %refs_4_.1) | copy-start | bytes 49156
  26.0 12.5 %collective-permute-start.8 = (bf16[256,512]{1,0:T(8,128)(2,1)S(1)}, bf16[256,512]{1,0:T(8,128)(2,1)S(1)}, u32[]{:S(2)}, u32[]{:S(2)}) collective-permute-start(bf16[256,512]{1,0:T(8,128)(2,1)S(1)} %shard_map.106), channel_id=1, source_target_pairs={{0,9},{1,5},{2,11},{3,7},{4,0},{5,12},{6,2},{7,14},{8,1},{9,13},{1... | collective-permute-start | bytes 786440 | tf_op jit(solution)/shard_map/ppermute | solution.py:299
  26.0 12.5 %collective-permute-start.9 = (bf16[2,512,128]{2,1,0:T(8,128)(2,1)S(1)}, bf16[2,512,128]{2,1,0:T(8,128)(2,1)S(1)}, u32[]{:S(2)}, u32[]{:S(2)}) collective-permute-start(bf16[2,512,128]{2,1,0:T(8,128)(2,1)S(1)} %shard_map.104), channel_id=1, source_target_pairs={{0,2},{1,3},{2,0},{3,1},{4,6},{5,7},{6,4},{7,5},{8,10},{9,11},{10,... | collective-permute-start | bytes 786440 | tf_op jit(solution)/shard_map/ppermute | solution.py:269
  38.5 4.8 %copy-start.3 = (f32[32,128]{1,0:T(8,128)S(1)}, f32[32,128]{1,0:T(8,128)}, u32[]{:S(2)}) copy-start(f32[32,128]{1,0:T(8,128)} %refs_5_.1) | copy-start | bytes 49156
  39.5 1.9 %collective-permute-start.10 = (bf16[2,32,128]{2,1,0:T(8,128)(2,1)S(1)}, bf16[2,32,128]{2,1,0:T(8,128)(2,1)S(1)}, u32[]{:S(2)}, u32[]{:S(2)}) collective-permute-start(bf16[2,32,128]{2,1,0:T(8,128)(2,1)S(1)} %get-tuple-element.30), channel_id=1, source_target_pairs={{0,1},{1,0},{2,3},{3,2},{4,5},{5,4},{6,7},{7,6},{8,9},{9,8},{10,11... | collective-permute-start | bytes 49160 | tf_op jit(solution)/shard_map/ppermute | solution.py:269
  39.5 3.7 %collective-permute-start.11 = (bf16[2,32,128]{2,1,0:T(8,128)(2,1)S(1)}, bf16[2,32,128]{2,1,0:T(8,128)(2,1)S(1)}, u32[]{:S(2)}, u32[]{:S(2)}) collective-permute-start(bf16[2,32,128]{2,1,0:T(8,128)(2,1)S(1)} %get-tuple-element.31), channel_id=1, source_target_pairs={{0,2},{1,3},{2,0},{3,1},{4,6},{5,7},{6,4},{7,5},{8,10},{9,11},{10,... | collective-permute-start | bytes 49160 | tf_op jit(solution)/shard_map/ppermute | solution.py:269
  39.5 3.7 %collective-permute-start.12 = (bf16[2,32,128]{2,1,0:T(8,128)(2,1)S(1)}, bf16[2,32,128]{2,1,0:T(8,128)(2,1)S(1)}, u32[]{:S(2)}, u32[]{:S(2)}) collective-permute-start(bf16[2,32,128]{2,1,0:T(8,128)(2,1)S(1)} %get-tuple-element.32), channel_id=1, source_target_pairs={{0,3},{1,2},{2,1},{3,0},{4,7},{5,6},{6,5},{7,4},{8,11},{9,10},{10,... | collective-permute-start | bytes 49160 | tf_op jit(solution)/shard_map/ppermute | solution.py:269

commit v5 on v4

--- a/solution.py
+++ b/solution.py
@@ -173,23 +173,23 @@
         total[...] = kept[...].astype(BF)
 
 
-def turn_kernel(columns, *refs):
+def turn_kernel(level, columns, *refs):
     turned, dense = refs[:-1], refs[-1]
     r = lax.axis_index("prow")
-    side = dense.shape[2]
+    side = dense.shape[1]
     extent = AR * side
     for p in range(columns):
         q = (r - p) % columns if columns > 1 else 0
-        for level in range(2):
-            rows = pl.ds(pl.multiple_of(q * extent, extent), extent)
-            panel = turned[p].at[0, pl.ds(level * extent, extent), :]
-            slots = turned[p].at[0, pl.ds(2 * extent, 4 * AR), :]
-            lay(dense.at[level, rows, :], panel, slots, level)
+        rows = pl.ds(pl.multiple_of(q * extent, extent), extent)
+        panel = turned[p].at[0, pl.ds(0, extent), :]
+        slots = turned[p].at[0, pl.ds(extent, 4 * AR), :]
+        lay(dense.at[rows, :], panel, slots, level)
 
 
 def finish_kernel(halving, count, pcol, columns, *refs):
     sums, refs = refs[:count], refs[count:]
-    dense, parent_ref, parent_other, pivots, refs = refs[0], refs[1], refs[2], refs[3], refs[4:]
+    dense, refs = (refs[0], refs[1]), refs[2:]
+    parent_ref, parent_other, pivots, refs = refs[0], refs[1], refs[2], refs[3:]
     upper_rows, lower_rows, refs = refs[0], refs[1], refs[2:]
     pieces, refs = refs[:pcol], refs[pcol:]
     parts = refs[0]
@@ -211,7 +211,7 @@
     hi, lo = split(upper_sum)
     rows = -hi
     upper_rows[...] = rows
-    upper_part = ndot(hi, dense[0]) + ndot(lo, dense[0])
+    upper_part = ndot(hi, dense[0][...]) + ndot(lo, dense[0][...])
     parts[0] = upper_part
     parts[1] = upper_part
     own = pl.ds(pl.multiple_of(c * share, share), share)
@@ -219,8 +219,8 @@
     lower_sum += tdot(parent, rows)
     hi, lo = split(lower_sum)
     lower_rows[...] = -hi
-    lower_part = ndot(hi, dense[1]) + ndot(lo, dense[1])
-    coupling_hi, coupling_lo = split(ndot(rows, dense[1]))
+    lower_part = ndot(hi, dense[1][...]) + ndot(lo, dense[1][...])
+    coupling_hi, coupling_lo = split(ndot(rows, dense[1][...]))
     lower_part += tdot(coupling_hi, parent) + tdot(coupling_lo, parent)
     hi, lo = split(parts[1])
     hi, lo = split(ndot(hi, parent) + ndot(lo, parent))
@@ -302,12 +302,12 @@
         out = (shape(arrived.shape, BF),)
         return call(functools.partial(add_kernel, columns), out, [VMEM] * 2)(kept, arrived)[0]
 
-    def turn(moved):
+    def turn(moved, level):
         return call(
-            functools.partial(turn_kernel, columns),
-            (shape((2, width, side), BF),),
+            functools.partial(turn_kernel, level, columns),
+            (shape((width, side), BF),),
             [VMEM] * columns,
-            flops=TURN_FLOPS,
+            flops=(2 << 30) if level == 0 else (3 << 30),
         )(*moved)[0]
 
     def turned(x):
@@ -336,8 +336,9 @@
     other_known = across(known_inverse, 1)
     near = call(copy_kernel, (shape(known_inverse.shape, BF),), [VMEM], flops=NEAR_FLOPS)(known_inverse)[0]
     halving = prow == 4 and columns == 1
-    whole = jnp.concatenate(packed, axis=1)
-    packed_turned = [swing(whole)] if halving else turned(whole)
+    upper_turned = jnp.concatenate([packed[0], packed[2]], axis=1)
+    upper_turned = [swing(upper_turned)] if halving else turned(upper_turned)
+    lower_turned = turned(jnp.concatenate([packed[1], packed[2]], axis=1))
     part = (2 * side, width)
     if halving:
         first, second, third, fourth, own, parent = call(
@@ -349,11 +350,12 @@
         )(*packed_all, near, other_known)
         first = trade(first, 0, 1, 1, 0)
         parent_other = trade(second, 0, 1, 1, 0)
-        dense_turned = turn(packed_turned)
-        first, dense_turned = lax.optimization_barrier((first, dense_turned))
-        dense_turned = across(dense_turned, 2)
+        swung = turn(upper_turned, 0)
+        first, swung = lax.optimization_barrier((first, swung))
+        upper_dense = across(swung, 2)
         third = trade(add(third, first), 2, 0, 1, 1)
         fourth = trade(add(fourth, parent_other), 2, 1, 1, 0)
+        lower_dense = turn(lower_turned, 1)
         sums = [own, first, third, fourth]
     else:
         plan = rounds(prow, columns)
@@ -369,15 +371,15 @@
         )(*packed_all, near, other_known)
         sums = [sums[0]] + [send(x, *steps) for x, steps in zip(sums[1:], plan)]
         parent_other = across(parent, 1)
-        dense_turned = turn(packed_turned)
+        upper_dense, lower_dense = turn(upper_turned, 0), turn(lower_turned, 1)
     outs = [shape((side, width), BF)] * 2 + [shape((2, share, side), F32)]
     outs += [shape((2, share, side), BF)] * (pcol - 1)
     finished = call(
         functools.partial(finish_kernel, halving, len(sums), pcol, columns),
         tuple(outs),
-        [VMEM] * (len(sums) + 4),
+        [VMEM] * (len(sums) + 5),
         [pltpu.VMEM((2, side, side), F32)],
-    )(*sums, dense_turned, parent, parent_other, upper_pivots)
+    )(*sums, upper_dense, lower_dense, parent, parent_other, upper_pivots)
     upper_rows, lower_rows = finished[:2]
     pieces = [finished[2]] + [across(finished[2 + s], s) for s in range(1, pcol)]
     upper_diagonal, lower_diagonal = call(

time: 44.1 us -> 43.7 us (level)
  waiting for transfers between devices: 27.2 us -> 24 us
  starting transfers between devices: 10.5 us -> 13.3 us
    ppermute x1, waiting for transfers between devices: 12 us -> 4.25 us  [swing(): return lax.ppermute(x, ('prow', 'pcol'), pairs)]
    ppermute x8, waiting for transfers between devices: 4.39 us -> 7.24 us  [across(): return lax.ppermute(x, 'pcol', [(c, c ^ j) for c in range(pcol)])]
    ppermute x4, waiting for transfers between devices: 10.8 us -> 12.5 us  [trade(): return lax.ppermute(x, ('prow', 'pcol'), pairs)]
    ppermute x4, starting transfers between devices: 1.42 us -> 2.94 us  [trade(): return lax.ppermute(x, ('prow', 'pcol'), pairs)]
    ppermute x8, starting transfers between devices: 8.91 us -> 9.58 us  [across(): return lax.ppermute(x, 'pcol', [(c, c ^ j) for c in range(pcol)])]
    ppermute x0 -> x1, starting transfers between devices: none -> 0.66 us  [turned(): moved.append(lax.ppermute(piece, ('prow', 'pcol'), pairs))]
  transfers between devices with their start and end apart: 13 -> 14, of which waited for: 6 -> 8; matrix products, arithmetic and copies ran while one was open for 6% -> 6% of each run, Pallas kernels for 3% -> 3%
where the time goes in v5:
time: 43.7 us; the launch traced here: 43.5 us
  waiting for transfers between devices  24 us (55%)
  starting transfers between devices  13.3 us (30%)
  Pallas kernels  2.99 us (7%)
  other arithmetic  2.38 us (5%)
  between operations  0.76 us (2%)
    ppermute x4, waiting for transfers between devices, trade(): return lax.ppermute(x, ('prow', 'pcol'), pairs)  12.5 us
    ppermute x8, starting transfers between devices, across(): return lax.ppermute(x, 'pcol', [(c, c ^ j) for c in range(pcol)])  9.58 us
    ppermute x8, waiting for transfers between devices, across(): return lax.ppermute(x, 'pcol', [(c, c ^ j) for c in range(pcol)])  7.24 us
    ppermute x1, waiting for transfers between devices, swing(): return lax.ppermute(x, ('prow', 'pcol'), pairs)  4.25 us
    ppermute x4, starting transfers between devices, trade(): return lax.ppermute(x, ('prow', 'pcol'), pairs)  2.94 us
    another operation x2, other arithmetic  1.32 us
    pallas_call x1, Pallas kernels, per_device(): call(functools.partial(halving_kernel, columns, pcol // 2), (shape(part,...  1.03 us
    pallas_call x1, Pallas kernels, per_device(): call(functools.partial(finish_kernel, halving, len(sums), pcol, columns),...  1.01 us
  transfers between devices with their start and end apart: 14, of which 8 were waited for; matrix products, arithmetic and copies ran while one was open for 6% of the time, Pallas kernels for 3%

profile of v5, /device:TPU:0, one launch (start us, length us, event | category | flops | bytes accessed | tf_op | source)
XLA Modules:
  0.0 43.5 jit_solution(6443580985822613060)
XLA Ops:
  0.6 0.5 %collective-permute-start.3 = (bf16[512,512]{1,0:T(8,128)(2,1)}, bf16[512,512]{1,0:T(8,128)(2,1)S(1)}, u32[]{:S(2)}, u32[]{:S(2)}) collective-permute-start(bf16[512,512]{1,0:T(8,128)(2,1)} %known.1), channel_id=1, source_target_pairs={{0,1},{1,0},{2,3},{3,2},{4,5},{5,4},{6,7},{7,6},{8,9},{9,8},{10,11... | collective-permute-start | bytes 1572872 | tf_op jit(solution)/shard_map/ppermute | solution.py:269
  1.2 2.6 %collective-permute-start = (bf16[1,512,128]{2,1,0:T(8,128)(2,1)}, bf16[1,512,128]{2,1,0:T(8,128)(2,1)S(1)}, u32[]{:S(2)}, u32[]{:S(2)}) collective-permute-start(bf16[1,512,128]{2,1,0:T(8,128)(2,1)} %bitcast.4), channel_id=1, source_target_pairs={{0,2},{1,3},{2,0},{3,1},{4,6},{5,7},{6,4},{7,5},{8,10},{9,11},{10,... | collective-permute-start | bytes 393224 | tf_op jit(solution)/shard_map/ppermute | solution.py:269
  3.7 0.1 collective-permute-start.1
  3.8 0.7 %convert.8 = bf16[4,1]{0,1:T(2,128)(2,1)S(1)} convert(s32[4,1]{0,1:T(1,128)} %param.9) | non-fusion elementwise | flops 4 | bytes 24 | tf_op jit(solution)/shard_map/convert
  4.5 0.7 %convert.9 = bf16[4,1]{0,1:T(2,128)(2,1)S(1)} convert(s32[4,1]{0,1:T(1,128)} %param.12) | non-fusion elementwise | flops 4 | bytes 24 | tf_op jit(solution)/shard_map/convert.1
  5.3 1.9 %collective-permute-start.2 = (bf16[1,16,128]{2,1,0:T(8,128)(2,1)S(1)}, bf16[1,16,128]{2,1,0:T(8,128)(2,1)S(1)}, u32[]{:S(2)}, u32[]{:S(2)}) collective-permute-start(bf16[1,16,128]{2,1,0:T(8,128)(2,1)S(1)} %broadcast_in_dim.2.refs_4_), channel_id=1, source_target_pairs={{0,2},{1,3},{2,0},{3,1},{4,6},{5,7},{6,4},{7,5},{8,10},{9,11},{10,... | collective-permute-start | bytes 12296 | tf_op jit(solution)/shard_map/ppermute | solution.py:269
  7.2 1.0 %pad_maximum_fusion = (bf16[1,528,128]{2,1,0:T(8,128)(2,1)S(1)}, bf16[1,528,128]{2,1,0:T(8,128)(2,1)S(1)}) fusion(bf16[1,16,128]{2,1,0:T(8,128)(2,1)S(1)} %broadcast_in_dim.2.refs_4_, bf16[1,512,128]{2,1,0:T(8,128)(2,1)} %bitcast.8, bf16[1,512,128]{2,1,0:T(8,128)(2,1)} %bitcast.5), kind=kLoop, calls=%fused_computation | loop fusion | flops 473088 | bytes 536576 | tf_op jit(solution)/shard_map/concatenate | solution.py:341
  8.2 0.1 collective-permute-start.5
  8.4 2.5 %collective-permute-done.2.refs_5_ = bf16[1,16,128]{2,1,0:T(8,128)(2,1)S(1)} collective-permute-done((bf16[1,16,128]{2,1,0:T(8,128)(2,1)S(1)}, bf16[1,16,128]{2,1,0:T(8,128)(2,1)S(1)}, u32[]{:S(2)}, u32[]{:S(2)}) %collective-permute-start.2) | collective-permute-done | bytes 4128 | tf_op jit(solution)/shard_map/ppermute | solution.py:269
  11.0 1.0 %shard_map.103 = (bf16[256,512]{1,0:T(8,128)(2,1)S(1)}, bf16[256,512]{1,0:T(8,128)(2,1)S(1)}, f32[256,512]{1,0:T(8,128)S(1)}, f32[256,512]{1,0:T(8,128)S(1)}, f3...) custom-call(bf16[1,512,128]{2,1,0:T(8,128)(2,1)S(1)} %bitcast.6, ...), custom_call_target="tpu_custom_call" | custom-call | tf_op jit(solution)/shard_map/pallas_call | solution.py:344
  12.1 1.2 %collective-permute-start.7 = (bf16[256,512]{1,0:T(8,128)(2,1)S(1)}, bf16[256,512]{1,0:T(8,128)(2,1)S(1)}, u32[]{:S(2)}, u32[]{:S(2)}) collective-permute-start(bf16[256,512]{1,0:T(8,128)(2,1)S(1)} %get-tuple-element.25), channel_id=1, source_target_pairs={{0,1},{1,5},{2,3},{3,7},{4,0},{5,4},{6,2},{7,6},{8,9},{9,13},{10,1... | collective-permute-start | bytes 786440 | tf_op jit(solution)/shard_map/ppermute | solution.py:299
  13.3 0.7 %collective-permute-start.10 = (bf16[1,528,128]{2,1,0:T(8,128)(2,1)S(1)}, bf16[1,528,128]{2,1,0:T(8,128)(2,1)S(1)}, u32[]{:S(2)}, u32[]{:S(2)}) collective-permute-start(bf16[1,528,128]{2,1,0:T(8,128)(2,1)S(1)} %get-tuple-element.36), channel_id=1, source_target_pairs={{0,0},{1,4},{2,8},{3,12},{4,1},{5,5},{6,9},{7,13},{8,2},{9,6},{10,... | collective-permute-start | bytes 405512 | tf_op jit(solution)/shard_map/ppermute | solution.py:324
  13.9 4.2 %collective-permute-done.5.refs_0_ = bf16[1,528,128]{2,1,0:T(8,128)(2,1)S(1)} collective-permute-done((bf16[1,528,128]{2,1,0:T(8,128)(2,1)S(1)}, bf16[1,528,128]{2,1,0:T(8,128)(2,1)S(1)}, u32[]{:S(2)}, u32[]{:S(2)}) %collective-permute-start.5) | collective-permute-done | bytes 135200 | tf_op jit(solution)/shard_map/ppermute | solution.py:289
  18.3 1.5 %collective-permute-done.4.arrived.refs_1_ = bf16[256,512]{1,0:T(8,128)(2,1)S(1)} collective-permute-done((bf16[256,512]{1,0:T(8,128)(2,1)S(1)}, bf16[256,512]{1,0:T(8,128)(2,1)S(1)}, u32[]{:S(2)}, u32[]{:S(2)}) %collective-permute-start.4) | collective-permute-done | bytes 262176 | tf_op jit(solution)/shard_map/ppermute | solution.py:299
  19.8 1.6 %collective-permute-start.6 = (bf16[256,512]{1,0:T(8,128)(2,1)S(1)}, bf16[256,512]{1,0:T(8,128)(2,1)S(1)}, u32[]{:S(2)}, u32[]{:S(2)}) collective-permute-start(bf16[256,512]{1,0:T(8,128)(2,1)S(1)} %shard_map.105), channel_id=1, source_target_pairs={{0,8},{1,4},{2,10},{3,6},{4,1},{5,13},{6,3},{7,15},{8,0},{9,12},{1... | collective-permute-start | bytes 786440 | tf_op jit(solution)/shard_map/ppermute | solution.py:299
  21.4 2.6 %collective-permute-done.7.arrived.refs_7_ = bf16[256,512]{1,0:T(8,128)(2,1)S(1)} collective-permute-done((bf16[256,512]{1,0:T(8,128)(2,1)S(1)}, bf16[256,512]{1,0:T(8,128)(2,1)S(1)}, u32[]{:S(2)}, u32[]{:S(2)}) %collective-permute-start.7) | collective-permute-done | bytes 262176 | tf_op jit(solution)/shard_map/ppermute | solution.py:299
  24.2 2.6 %collective-permute-start.9 = (bf16[512,128]{1,0:T(8,128)(2,1)S(1)}, bf16[512,128]{1,0:T(8,128)(2,1)S(1)}, u32[]{:S(2)}, u32[]{:S(2)}) collective-permute-start(bf16[512,128]{1,0:T(8,128)(2,1)S(1)} %shard_map.104), channel_id=1, source_target_pairs={{0,2},{1,3},{2,0},{3,1},{4,6},{5,7},{6,4},{7,5},{8,10},{9,11},{10,... | collective-permute-start | bytes 393224 | tf_op jit(solution)/shard_map/ppermute | solution.py:269
  26.9 2.9 %collective-permute-done.9.refs_4_ = bf16[512,128]{1,0:T(8,128)(2,1)S(1)} collective-permute-done((bf16[512,128]{1,0:T(8,128)(2,1)S(1)}, bf16[512,128]{1,0:T(8,128)(2,1)S(1)}, u32[]{:S(2)}, u32[]{:S(2)}) %collective-permute-start.9) | collective-permute-done | bytes 131104 | tf_op jit(solution)/shard_map/ppermute | solution.py:269
  29.7 3.4 %collective-permute-done.6.refs_2_ = bf16[256,512]{1,0:T(8,128)(2,1)S(1)} collective-permute-done((bf16[256,512]{1,0:T(8,128)(2,1)S(1)}, bf16[256,512]{1,0:T(8,128)(2,1)S(1)}, u32[]{:S(2)}, u32[]{:S(2)}) %collective-permute-start.6) | collective-permute-done | bytes 262176 | tf_op jit(solution)/shard_map/ppermute | solution.py:299
  33.2 5.0 %collective-permute-done.8.refs_3_ = bf16[256,512]{1,0:T(8,128)(2,1)S(1)} collective-permute-done((bf16[256,512]{1,0:T(8,128)(2,1)S(1)}, bf16[256,512]{1,0:T(8,128)(2,1)S(1)}, u32[]{:S(2)}, u32[]{:S(2)}) %collective-permute-start.8) | collective-permute-done | bytes 262176 | tf_op jit(solution)/shard_map/ppermute | solution.py:299
  38.2 1.0 %shard_map.108 = (bf16[128,512]{1,0:T(8,128)(2,1)}, bf16[128,512]{1,0:T(8,128)(2,1)}, f32[2,32,128]{2,1,0:T(8,128)S(1)}, bf16[2,32,128]{2,1,0:T(8,128)(2,1)S(1)}...) custom-call(f32[256,512]{1,0:T(8,128)S(1)} %get-tuple-element.20.refs_0_, ...), custom_call_target="tpu_custom_call" | custom-call | tf_op jit(solution)/shard_map/pallas_call | solution.py:377
  39.2 1.9 %collective-permute-start.13 = (bf16[2,32,128]{2,1,0:T(8,128)(2,1)S(1)}, bf16[2,32,128]{2,1,0:T(8,128)(2,1)S(1)}, u32[]{:S(2)}, u32[]{:S(2)}) collective-permute-start(bf16[2,32,128]{2,1,0:T(8,128)(2,1)S(1)} %get-tuple-element.32), channel_id=1, source_target_pairs={{0,3},{1,2},{2,1},{3,0},{4,7},{5,6},{6,5},{7,4},{8,11},{9,10},{10,... | collective-permute-start | bytes 49160 | tf_op jit(solution)/shard_map/ppermute | solution.py:269
  41.0 1.9 %collective-permute-done.12.refs_2_ = bf16[2,32,128]{2,1,0:T(8,128)(2,1)S(1)} collective-permute-done((bf16[2,32,128]{2,1,0:T(8,128)(2,1)S(1)}, bf16[2,32,128]{2,1,0:T(8,128)(2,1)S(1)}, u32[]{:S(2)}, u32[]{:S(2)}) %collective-permute-start.12) | collective-permute-done | bytes 16416 | tf_op jit(solution)/shard_map/ppermute | solution.py:269
  42.9 0.6 %shard_map.109 = (f32[32,128]{1,0:T(8,128)}, f32[32,128]{1,0:T(8,128)}) custom-call(f32[2,32,128]{2,1,0:T(8,128)S(1)} %get-tuple-element.29.refs_0_, bf16[2,32,128]{2,1,0:T(8,128)(2,1)S(1)} %collective-permute-done.11.refs_1_, bf16[2,32,128]{2,1,0:T(8,128)(2,1)S(1)} %collective-permute-done.12.refs_2_, ...), custom_call_target="tpu_custom_call" | custom-call | tf_op jit(solution)/shard_map/pallas_call | solution.py:385
  (27 shorter events, 0.7 us)
Async XLA Ops:
  0.6 7.8 %copy-start.4 = (bf16[512,512]{1,0:T(8,128)(2,1)S(1)}, bf16[512,512]{1,0:T(8,128)(2,1)}, u32[]{:S(2)}) copy-start(bf16[512,512]{1,0:T(8,128)(2,1)} %known.1) | copy-start | bytes 1572868
  0.6 10.3 %collective-permute-start.3 = (bf16[512,512]{1,0:T(8,128)(2,1)}, bf16[512,512]{1,0:T(8,128)(2,1)S(1)}, u32[]{:S(2)}, u32[]{:S(2)}) collective-permute-start(bf16[512,512]{1,0:T(8,128)(2,1)} %known.1), channel_id=1, source_target_pairs={{0,1},{1,0},{2,3},{3,2},{4,5},{5,4},{6,7},{7,6},{8,9},{9,8},{10,11... | collective-permute-start | bytes 1572872 | tf_op jit(solution)/shard_map/ppermute | solution.py:269
  1.2 9.8 %collective-permute-start = (bf16[1,512,128]{2,1,0:T(8,128)(2,1)}, bf16[1,512,128]{2,1,0:T(8,128)(2,1)S(1)}, u32[]{:S(2)}, u32[]{:S(2)}) collective-permute-start(bf16[1,512,128]{2,1,0:T(8,128)(2,1)} %bitcast.4), channel_id=1, source_target_pairs={{0,2},{1,3},{2,0},{3,1},{4,6},{5,7},{6,4},{7,5},{8,10},{9,11},{10,... | collective-permute-start | bytes 393224 | tf_op jit(solution)/shard_map/ppermute | solution.py:269
  3.7 7.2 %collective-permute-start.1 = (bf16[1,512,128]{2,1,0:T(8,128)(2,1)}, bf16[1,512,128]{2,1,0:T(8,128)(2,1)S(1)}, u32[]{:S(2)}, u32[]{:S(2)}) collective-permute-start(bf16[1,512,128]{2,1,0:T(8,128)(2,1)} %bitcast.7), channel_id=1, source_target_pairs={{0,2},{1,3},{2,0},{3,1},{4,6},{5,7},{6,4},{7,5},{8,10},{9,11},{10,... | collective-permute-start | bytes 393224 | tf_op jit(solution)/shard_map/ppermute | solution.py:269
  5.3 5.6 %collective-permute-start.2 = (bf16[1,16,128]{2,1,0:T(8,128)(2,1)S(1)}, bf16[1,16,128]{2,1,0:T(8,128)(2,1)S(1)}, u32[]{:S(2)}, u32[]{:S(2)}) collective-permute-start(bf16[1,16,128]{2,1,0:T(8,128)(2,1)S(1)} %broadcast_in_dim.2.refs_4_), channel_id=1, source_target_pairs={{0,2},{1,3},{2,0},{3,1},{4,6},{5,7},{6,4},{7,5},{8,10},{9,11},{10,... | collective-permute-start | bytes 12296 | tf_op jit(solution)/shard_map/ppermute | solution.py:269
  8.2 2.7 %copy-start = (bf16[4,1,128,128]{3,2,1,0:T(8,128)(2,1)S(1)}, bf16[4,1,128,128]{3,2,1,0:T(8,128)(2,1)}, u32[]{:S(2)}) copy-start(bf16[4,1,128,128]{3,2,1,0:T(8,128)(2,1)} %param.8) | copy-start | bytes 393220
  8.2 2.7 %copy-start.1 = (bf16[4,1,128,128]{3,2,1,0:T(8,128)(2,1)S(1)}, bf16[4,1,128,128]{3,2,1,0:T(8,128)(2,1)}, u32[]{:S(2)}) copy-start(bf16[4,1,128,128]{3,2,1,0:T(8,128)(2,1)} %param.11) | copy-start | bytes 393220
  8.2 10.0 %collective-permute-start.5 = (bf16[1,528,128]{2,1,0:T(8,128)(2,1)S(1)}, bf16[1,528,128]{2,1,0:T(8,128)(2,1)S(1)}, u32[]{:S(2)}, u32[]{:S(2)}) collective-permute-start(bf16[1,528,128]{2,1,0:T(8,128)(2,1)S(1)} %get-tuple-element.37), channel_id=1, source_target_pairs={{0,2},{1,6},{2,10},{3,14},{4,3},{5,7},{6,11},{7,15},{8,0},{9,4},{1... | collective-permute-start | bytes 405512 | tf_op jit(solution)/shard_map/ppermute | solution.py:289
  12.0 7.8 %collective-permute-start.4 = (bf16[256,512]{1,0:T(8,128)(2,1)S(1)}, bf16[256,512]{1,0:T(8,128)(2,1)S(1)}, u32[]{:S(2)}, u32[]{:S(2)}) collective-permute-start(bf16[256,512]{1,0:T(8,128)(2,1)S(1)} %get-tuple-element.21), channel_id=1, source_target_pairs={{0,1},{1,5},{2,3},{3,7},{4,0},{5,4},{6,2},{7,6},{8,9},{9,13},{10,1... | collective-permute-start | bytes 786440 | tf_op jit(solution)/shard_map/ppermute | solution.py:299
  12.1 12.0 %collective-permute-start.7 = (bf16[256,512]{1,0:T(8,128)(2,1)S(1)}, bf16[256,512]{1,0:T(8,128)(2,1)S(1)}, u32[]{:S(2)}, u32[]{:S(2)}) collective-permute-start(bf16[256,512]{1,0:T(8,128)(2,1)S(1)} %get-tuple-element.25), channel_id=1, source_target_pairs={{0,1},{1,5},{2,3},{3,7},{4,0},{5,4},{6,2},{7,6},{8,9},{9,13},{10,1... | collective-permute-start | bytes 786440 | tf_op jit(solution)/shard_map/ppermute | solution.py:299
  13.3 13.5 %collective-permute-start.10 = (bf16[1,528,128]{2,1,0:T(8,128)(2,1)S(1)}, bf16[1,528,128]{2,1,0:T(8,128)(2,1)S(1)}, u32[]{:S(2)}, u32[]{:S(2)}) collective-permute-start(bf16[1,528,128]{2,1,0:T(8,128)(2,1)S(1)} %get-tuple-element.36), channel_id=1, source_target_pairs={{0,0},{1,4},{2,8},{3,12},{4,1},{5,5},{6,9},{7,13},{8,2},{9,6},{10,... | collective-permute-start | bytes 405512 | tf_op jit(solution)/shard_map/ppermute | solution.py:324
  19.8 13.3 %collective-permute-start.6 = (bf16[256,512]{1,0:T(8,128)(2,1)S(1)}, bf16[256,512]{1,0:T(8,128)(2,1)S(1)}, u32[]{:S(2)}, u32[]{:S(2)}) collective-permute-start(bf16[256,512]{1,0:T(8,128)(2,1)S(1)} %shard_map.105), channel_id=1, source_target_pairs={{0,8},{1,4},{2,10},{3,6},{4,1},{5,13},{6,3},{7,15},{8,0},{9,12},{1... | collective-permute-start | bytes 786440 | tf_op jit(solution)/shard_map/ppermute | solution.py:299
  24.1 14.1 %copy-start.2 = (f32[32,128]{1,0:T(8,128)S(1)}, f32[32,128]{1,0:T(8,128)}, u32[]{:S(2)}) copy-start(f32[32,128]{1,0:T(8,128)} %refs_4_.1) | copy-start | bytes 49156
  24.1 14.0 %collective-permute-start.8 = (bf16[256,512]{1,0:T(8,128)(2,1)S(1)}, bf16[256,512]{1,0:T(8,128)(2,1)S(1)}, u32[]{:S(2)}, u32[]{:S(2)}) collective-permute-start(bf16[256,512]{1,0:T(8,128)(2,1)S(1)} %shard_map.106), channel_id=1, source_target_pairs={{0,9},{1,5},{2,11},{3,7},{4,0},{5,12},{6,2},{7,14},{8,1},{9,13},{1... | collective-permute-start | bytes 786440 | tf_op jit(solution)/shard_map/ppermute | solution.py:299
  24.2 5.5 %collective-permute-start.9 = (bf16[512,128]{1,0:T(8,128)(2,1)S(1)}, bf16[512,128]{1,0:T(8,128)(2,1)S(1)}, u32[]{:S(2)}, u32[]{:S(2)}) collective-permute-start(bf16[512,128]{1,0:T(8,128)(2,1)S(1)} %shard_map.104), channel_id=1, source_target_pairs={{0,2},{1,3},{2,0},{3,1},{4,6},{5,7},{6,4},{7,5},{8,10},{9,11},{10,... | collective-permute-start | bytes 393224 | tf_op jit(solution)/shard_map/ppermute | solution.py:269
  38.2 4.8 %copy-start.3 = (f32[32,128]{1,0:T(8,128)S(1)}, f32[32,128]{1,0:T(8,128)}, u32[]{:S(2)}) copy-start(f32[32,128]{1,0:T(8,128)} %refs_5_.1) | copy-start | bytes 49156
  39.2 1.9 %collective-permute-start.11 = (bf16[2,32,128]{2,1,0:T(8,128)(2,1)S(1)}, bf16[2,32,128]{2,1,0:T(8,128)(2,1)S(1)}, u32[]{:S(2)}, u32[]{:S(2)}) collective-permute-start(bf16[2,32,128]{2,1,0:T(8,128)(2,1)S(1)} %get-tuple-element.30), channel_id=1, source_target_pairs={{0,1},{1,0},{2,3},{3,2},{4,5},{5,4},{6,7},{7,6},{8,9},{9,8},{10,11... | collective-permute-start | bytes 49160 | tf_op jit(solution)/shard_map/ppermute | solution.py:269
  39.2 3.7 %collective-permute-start.12 = (bf16[2,32,128]{2,1,0:T(8,128)(2,1)S(1)}, bf16[2,32,128]{2,1,0:T(8,128)(2,1)S(1)}, u32[]{:S(2)}, u32[]{:S(2)}) collective-permute-start(bf16[2,32,128]{2,1,0:T(8,128)(2,1)S(1)} %get-tuple-element.31), channel_id=1, source_target_pairs={{0,2},{1,3},{2,0},{3,1},{4,6},{5,7},{6,4},{7,5},{8,10},{9,11},{10,... | collective-permute-start | bytes 49160 | tf_op jit(solution)/shard_map/ppermute | solution.py:269
  39.2 3.7 %collective-permute-start.13 = (bf16[2,32,128]{2,1,0:T(8,128)(2,1)S(1)}, bf16[2,32,128]{2,1,0:T(8,128)(2,1)S(1)}, u32[]{:S(2)}, u32[]{:S(2)}) collective-permute-start(bf16[2,32,128]{2,1,0:T(8,128)(2,1)S(1)} %get-tuple-element.32), channel_id=1, source_target_pairs={{0,3},{1,2},{2,1},{3,0},{4,7},{5,6},{6,5},{7,4},{8,11},{9,10},{10,... | collective-permute-start | bytes 49160 | tf_op jit(solution)/shard_map/ppermute | solution.py:269

commit v6 on v5

--- a/solution.py
+++ b/solution.py
@@ -117,48 +117,57 @@
         parent[...] = jnp.zeros_like(parent)
 
 
-def halving_kernel(columns, halves, *refs):
+def take(columns, halves, refs, k, dense, parent=None):
     panels = refs[:halves], refs[halves : 2 * halves]
-    slots, refs = refs[2 * halves : 3 * halves], refs[3 * halves :]
-    own_known, other_known, first, second, third, fourth, own, parent, dense = refs
-    r = lax.axis_index("prow")
-    c = lax.axis_index("pcol")
-    side = parent.shape[0]
-    extent = AR * side
-    holds = c % 2 == holder(r, columns)
-
-    def slot(k):
-        return k // (2 * columns) * columns + k % columns
-
+    slots = refs[2 * halves : 3 * halves]
+    side = dense.shape[1] // 2
     for j in range(halves):
         for i in range(columns):
-            k = (c ^ (2 * j)) * columns + i
-            for level in range(2):
-                columns_of = pl.ds(level * side, side)
-                lay(dense.at[slot(k), :, columns_of], panels[level][j].at[i], slots[j].at[i], level)
-
-            @pl.when(k == r)
+
+            @pl.when((lax.axis_index("pcol") ^ (2 * j)) * columns + i == k)
             def _():
-                parent[...] = panels[1][j][i, :side]
+                for level in range(2):
+                    columns_of = pl.ds(level * side, side)
+                    lay(dense.at[:, columns_of], panels[level][j].at[i], slots[j].at[i], level)
+                if parent is not None:
+                    parent[...] = panels[1][j][i, :side]
+
+
+def leading_kernel(columns, halves, *refs):
+    own_known, other_known, first, second, parent, dense = refs[3 * halves :]
+    r = lax.axis_index("prow")
+    side = parent.shape[0]
+    holds = lax.axis_index("pcol") % 2 == holder(r, columns)
+    take(columns, halves, refs, r ^ jnp.where(holds, 0, 3), dense, parent)
 
     @pl.when(holds)
     def _():
-        panel = dense[slot(r)]
-        first[...] = tdot(panel, other_known[...]).astype(BF)
-        own[...] = tdot(panel, own_known[...])
+        first[...] = tdot(dense[...], other_known[...]).astype(BF)
         second[:side, :side] = parent[...]
-        panel = dense[slot(r ^ 2)]
-        third[...] = tdot(panel, own_known[...])
-        fourth[...] = tdot(panel, other_known[...])
 
     @pl.when(jnp.logical_not(holds))
     def _():
-        panel = dense[slot(r ^ 3)]
-        first[...] = tdot(panel, own_known[...]).astype(BF)
-        second[...] = tdot(panel, other_known[...]).astype(BF)
-        panel = dense[slot(r ^ 1)]
-        third[...] = tdot(panel, other_known[...])
-        fourth[...] = tdot(panel, own_known[...])
+        first[...] = tdot(dense[...], other_known[...]).astype(BF)
+        second[...] = tdot(dense[...], own_known[...]).astype(BF)
+
+
+def trailing_kernel(columns, halves, *refs):
+    own_known, other_known, third, fourth, own, dense = refs[3 * halves :]
+    r = lax.axis_index("prow")
+    holds = lax.axis_index("pcol") % 2 == holder(r, columns)
+    take(columns, halves, refs, r ^ jnp.where(holds, 2, 1), dense)
+
+    @pl.when(holds)
+    def _():
+        third[...] = tdot(dense[...], other_known[...])
+        fourth[...] = tdot(dense[...], own_known[...])
+        take(columns, halves, refs, r, dense)
+        own[...] = tdot(dense[...], own_known[...])
+
+    @pl.when(jnp.logical_not(holds))
+    def _():
+        third[...] = tdot(dense[...], own_known[...])
+        fourth[...] = tdot(dense[...], other_known[...])
 
 
 def add_kernel(columns, kept, arrived, total):
@@ -186,39 +195,47 @@
         lay(dense.at[rows, :], panel, slots, level)
 
 
-def finish_kernel(halving, count, pcol, columns, *refs):
-    sums, refs = refs[:count], refs[count:]
-    dense, refs = (refs[0], refs[1]), refs[2:]
-    parent_ref, parent_other, pivots, refs = refs[0], refs[1], refs[2], refs[3:]
-    upper_rows, lower_rows, refs = refs[0], refs[1], refs[2:]
-    pieces, refs = refs[:pcol], refs[pcol:]
-    parts = refs[0]
-    r = lax.axis_index("prow")
-    c = lax.axis_index("pcol")
+def whole_sums(halving, columns, sums, parent_ref, parent_other):
     side = parent_ref.shape[0]
-    share = pivots.shape[0]
+    holds = lax.axis_index("pcol") % 2 == holder(lax.axis_index("prow"), columns)
     if halving:
-        holds = c % 2 == holder(r, columns)
         parent = jnp.where(holds, parent_ref[...], parent_other[:side, :side])
         total = jnp.where(holds, sums[0][...], sums[1][...].astype(F32))
         total += sums[2][...].astype(F32) + sums[3][...].astype(F32)
     else:
         parent = parent_ref[...] + parent_other[...]
         total = sums[0][...]
-        for t in range(1, count):
+        for t in range(1, len(sums)):
             total += sums[t][...].astype(F32)
-    upper_sum, lower_sum = total[:side], total[side:]
+    rows = -total[:side].astype(BF)
+    return parent, rows, total[:side], total[side:] + tdot(parent, rows)
+
+
+def rows_kernel(halving, count, columns, *refs):
+    sums, (parent_ref, parent_other, upper_rows, lower_rows) = refs[:count], refs[count:]
+    _, rows, _, lower_sum = whole_sums(halving, columns, sums, parent_ref, parent_other)
+    upper_rows[...] = rows
+    lower_rows[...] = -lower_sum.astype(BF)
+
+
+def finish_kernel(halving, count, pcol, columns, *refs):
+    sums, refs = refs[:count], refs[count:]
+    dense, refs = (refs[0], refs[1]), refs[2:]
+    parent_ref, parent_other, pivots, refs = refs[0], refs[1], refs[2], refs[3:]
+    pieces, refs = refs[:pcol], refs[pcol:]
+    parts = refs[0]
+    c = lax.axis_index("pcol")
+    share = pivots.shape[0]
+    parent, rows, upper_sum, lower_sum = whole_sums(
+        halving, columns, sums, parent_ref, parent_other
+    )
     hi, lo = split(upper_sum)
-    rows = -hi
-    upper_rows[...] = rows
     upper_part = ndot(hi, dense[0][...]) + ndot(lo, dense[0][...])
     parts[0] = upper_part
     parts[1] = upper_part
     own = pl.ds(pl.multiple_of(c * share, share), share)
     parts[1, own, :] += pivots[...]
-    lower_sum += tdot(parent, rows)
     hi, lo = split(lower_sum)
-    lower_rows[...] = -hi
     lower_part = ndot(hi, dense[1][...]) + ndot(lo, dense[1][...])
     coupling_hi, coupling_lo = split(ndot(rows, dense[1][...]))
     lower_part += tdot(coupling_hi, parent) + tdot(coupling_lo, parent)
@@ -341,20 +358,26 @@
     lower_turned = turned(jnp.concatenate([packed[1], packed[2]], axis=1))
     part = (2 * side, width)
     if halving:
-        first, second, third, fourth, own, parent = call(
-            functools.partial(halving_kernel, columns, pcol // 2),
-            (shape(part, BF), shape(part, BF), shape(part, F32), shape(part, F32))
-            + (shape(part, F32), shape((side, side), BF)),
+        operands = (*packed_all, near, other_known)
+        first, second, parent = call(
+            functools.partial(leading_kernel, columns, pcol // 2),
+            (shape(part, BF), shape(part, BF), shape((side, side), BF)),
             [VMEM] * (3 * pcol // 2 + 2),
-            [pltpu.VMEM((prow // 2, extent, 2 * side), BF)],
-        )(*packed_all, near, other_known)
+            [pltpu.VMEM((extent, 2 * side), BF)],
+        )(*operands)
+        third, fourth, own = call(
+            functools.partial(trailing_kernel, columns, pcol // 2),
+            (shape(part, F32), shape(part, F32), shape(part, F32)),
+            [VMEM] * (3 * pcol // 2 + 2),
+            [pltpu.VMEM((extent, 2 * side), BF)],
+        )(*operands)
         first = trade(first, 0, 1, 1, 0)
         parent_other = trade(second, 0, 1, 1, 0)
         swung = turn(upper_turned, 0)
         first, swung = lax.optimization_barrier((first, swung))
         upper_dense = across(swung, 2)
-        third = trade(add(third, first), 2, 0, 1, 1)
-        fourth = trade(add(fourth, parent_other), 2, 1, 1, 0)
+        third = trade(add(third, first), 2, 1, 1, 0)
+        fourth = trade(add(fourth, parent_other), 2, 0, 1, 1)
         lower_dense = turn(lower_turned, 1)
         sums = [own, first, third, fourth]
     else:
@@ -372,7 +395,7 @@
         sums = [sums[0]] + [send(x, *steps) for x, steps in zip(sums[1:], plan)]
         parent_other = across(parent, 1)
         upper_dense, lower_dense = turn(upper_turned, 0), turn(lower_turned, 1)
-    outs = [shape((side, width), BF)] * 2 + [shape((2, share, side), F32)]
+    outs = [shape((2, share, side), F32)]
     outs += [shape((2, share, side), BF)] * (pcol - 1)
     finished = call(
         functools.partial(finish_kernel, halving, len(sums), pcol, columns),
@@ -380,8 +403,12 @@
         [VMEM] * (len(sums) + 5),
         [pltpu.VMEM((2, side, side), F32)],
     )(*sums, upper_dense, lower_dense, parent, parent_other, upper_pivots)
-    upper_rows, lower_rows = finished[:2]
-    pieces = [finished[2]] + [across(finished[2 + s], s) for s in range(1, pcol)]
+    upper_rows, lower_rows = call(
+        functools.partial(rows_kernel, halving, len(sums), columns),
+        (shape((side, width), BF), shape((side, width), BF)),
+        [VMEM] * (len(sums) + 2),
+    )(*sums, parent, parent_other)
+    pieces = [finished[0]] + [across(finished[s], s) for s in range(1, pcol)]
     upper_diagonal, lower_diagonal = call(
         functools.partial(sum_kernel, pcol),
         (shape((share, side), F32), shape((share, side), F32)),

time: 43.7 us -> 43.2 us (0.989)
  starting transfers between devices: 13.3 us -> 10.9 us
  Pallas kernels: 2.99 us -> 4.16 us
  waiting for transfers between devices: 24 us -> 24.7 us
    ppermute x8, starting transfers between devices: 9.58 us -> 7.37 us  [across(): return lax.ppermute(x, 'pcol', [(c, c ^ j) for c in range(pcol)])]
    ppermute x8, waiting for transfers between devices: 7.24 us -> 8.78 us  [across(): return lax.ppermute(x, 'pcol', [(c, c ^ j) for c in range(pcol)])]
    pallas_call x1 -> x3, Pallas kernels: 1.03 us -> 2.51 us  [the longest x1 1.11 us: per_device(): call(functools.partial(trailing_kernel, columns, pcol // 2), (shape(part,...]
    ppermute x4, waiting for transfers between devices: 12.5 us -> 11.2 us  [trade(): return lax.ppermute(x, ('prow', 'pcol'), pairs)]
    ppermute x1, waiting for transfers between devices: 4.25 us -> 4.69 us  [swing(): return lax.ppermute(x, ('prow', 'pcol'), pairs)]
  transfers between devices with their start and end apart: 14 -> 14, of which waited for: 8 -> 8; matrix products, arithmetic and copies ran while one was open for 6% -> 6% of each run, Pallas kernels for 3% -> 7%
where the time goes in v6:
time: 43.2 us; the launch traced here: 43 us
  waiting for transfers between devices  24.7 us (57%)
  starting transfers between devices  10.9 us (25%)
  Pallas kernels  4.16 us (10%)
  other arithmetic  2.38 us (6%)
  between operations  0.77 us (2%)
    ppermute x4, waiting for transfers between devices, trade(): return lax.ppermute(x, ('prow', 'pcol'), pairs)  11.2 us
    ppermute x8, waiting for transfers between devices, across(): return lax.ppermute(x, 'pcol', [(c, c ^ j) for c in range(pcol)])  8.78 us
    ppermute x8, starting transfers between devices, across(): return lax.ppermute(x, 'pcol', [(c, c ^ j) for c in range(pcol)])  7.37 us
    ppermute x1, waiting for transfers between devices, swing(): return lax.ppermute(x, ('prow', 'pcol'), pairs)  4.69 us
    ppermute x4, starting transfers between devices, trade(): return lax.ppermute(x, ('prow', 'pcol'), pairs)  2.73 us
    another operation x2, other arithmetic  1.32 us
    pallas_call x1, Pallas kernels, per_device(): call(functools.partial(trailing_kernel, columns, pcol // 2), (shape(part,...  1.11 us
    concatenate x1, other arithmetic, per_device(): lower_turned = turned(jnp.concatenate([packed[1], packed[2]], axis=1))  0.99 us
  transfers between devices with their start and end apart: 14, of which 8 were waited for; matrix products, arithmetic and copies ran while one was open for 6% of the time, Pallas kernels for 7%

profile of v6, /device:TPU:0, one launch (start us, length us, event | category | flops | bytes accessed | tf_op | source)
XLA Modules:
  0.0 43.0 jit_solution(13698832521023764474)
XLA Ops:
  0.6 0.5 %collective-permute-start.3 = (bf16[512,512]{1,0:T(8,128)(2,1)}, bf16[512,512]{1,0:T(8,128)(2,1)S(1)}, u32[]{:S(2)}, u32[]{:S(2)}) collective-permute-start(bf16[512,512]{1,0:T(8,128)(2,1)} %known.1), channel_id=1, source_target_pairs={{0,1},{1,0},{2,3},{3,2},{4,5},{5,4},{6,7},{7,6},{8,9},{9,8},{10,11... | collective-permute-start | bytes 1572872 | tf_op jit(solution)/shard_map/ppermute | solution.py:286
  1.2 2.6 %collective-permute-start = (bf16[1,512,128]{2,1,0:T(8,128)(2,1)}, bf16[1,512,128]{2,1,0:T(8,128)(2,1)S(1)}, u32[]{:S(2)}, u32[]{:S(2)}) collective-permute-start(bf16[1,512,128]{2,1,0:T(8,128)(2,1)} %bitcast.4), channel_id=1, source_target_pairs={{0,2},{1,3},{2,0},{3,1},{4,6},{5,7},{6,4},{7,5},{8,10},{9,11},{10,... | collective-permute-start | bytes 393224 | tf_op jit(solution)/shard_map/ppermute | solution.py:286
  3.8 0.7 %convert.9 = bf16[4,1]{0,1:T(2,128)(2,1)S(1)} convert(s32[4,1]{0,1:T(1,128)} %param.12) | non-fusion elementwise | flops 4 | bytes 24 | tf_op jit(solution)/shard_map/convert.1
  4.5 0.7 %convert.8 = bf16[4,1]{0,1:T(2,128)(2,1)S(1)} convert(s32[4,1]{0,1:T(1,128)} %param.9) | non-fusion elementwise | flops 4 | bytes 24 | tf_op jit(solution)/shard_map/convert
  5.3 1.9 %collective-permute-start.2 = (bf16[1,16,128]{2,1,0:T(8,128)(2,1)S(1)}, bf16[1,16,128]{2,1,0:T(8,128)(2,1)S(1)}, u32[]{:S(2)}, u32[]{:S(2)}) collective-permute-start(bf16[1,16,128]{2,1,0:T(8,128)(2,1)S(1)} %broadcast_in_dim.2.refs_4_), channel_id=1, source_target_pairs={{0,2},{1,3},{2,0},{3,1},{4,6},{5,7},{6,4},{7,5},{8,10},{9,11},{10,... | collective-permute-start | bytes 12296 | tf_op jit(solution)/shard_map/ppermute | solution.py:286
  7.2 1.0 %pad_maximum_fusion = (bf16[1,528,128]{2,1,0:T(8,128)(2,1)S(1)}, bf16[1,528,128]{2,1,0:T(8,128)(2,1)S(1)}) fusion(bf16[1,16,128]{2,1,0:T(8,128)(2,1)S(1)} %broadcast_in_dim.2.refs_4_, bf16[1,512,128]{2,1,0:T(8,128)(2,1)} %bitcast.9, bf16[1,512,128]{2,1,0:T(8,128)(2,1)} %bitcast.5), kind=kLoop, calls=%fused_computation | loop fusion | flops 473088 | bytes 536576 | tf_op jit(solution)/shard_map/concatenate | solution.py:358
  8.4 2.5 %collective-permute-done.2.refs_5_ = bf16[1,16,128]{2,1,0:T(8,128)(2,1)S(1)} collective-permute-done((bf16[1,16,128]{2,1,0:T(8,128)(2,1)S(1)}, bf16[1,16,128]{2,1,0:T(8,128)(2,1)S(1)}, u32[]{:S(2)}, u32[]{:S(2)}) %collective-permute-start.2) | collective-permute-done | bytes 4128 | tf_op jit(solution)/shard_map/ppermute | solution.py:286
  11.0 0.5 %shard_map.104 = (bf16[256,512]{1,0:T(8,128)(2,1)S(1)}, bf16[256,512]{1,0:T(8,128)(2,1)S(1)}, bf16[128,128]{1,0:T(8,128)(2,1)S(1)}) custom-call(bf16[1,512,128]{2,1,0:T(8,128)(2,1)S(1)} %bitcast.6, bf16[1,512,128]{2,1,0:T(8,128)(2,1)S(1)} %collective-permute-done.refs_1_, bf16[1,512,128]{2,1,0:T(8,128)(2,1)S(1)} %bitcast.10, ...), custom_call_target="tpu_custom_call" | custom-call | tf_op jit(solution)/shard_map/pallas_call | solution.py:362
  11.5 1.2 %collective-permute-start.7 = (bf16[256,512]{1,0:T(8,128)(2,1)S(1)}, bf16[256,512]{1,0:T(8,128)(2,1)S(1)}, u32[]{:S(2)}, u32[]{:S(2)}) collective-permute-start(bf16[256,512]{1,0:T(8,128)(2,1)S(1)} %get-tuple-element.25), channel_id=1, source_target_pairs={{0,1},{1,5},{2,3},{3,7},{4,0},{5,4},{6,2},{7,6},{8,9},{9,13},{10,1... | collective-permute-start | bytes 786440 | tf_op jit(solution)/shard_map/ppermute | solution.py:316
  12.7 0.7 %collective-permute-start.10 = (bf16[1,528,128]{2,1,0:T(8,128)(2,1)S(1)}, bf16[1,528,128]{2,1,0:T(8,128)(2,1)S(1)}, u32[]{:S(2)}, u32[]{:S(2)}) collective-permute-start(bf16[1,528,128]{2,1,0:T(8,128)(2,1)S(1)} %get-tuple-element.36), channel_id=1, source_target_pairs={{0,0},{1,4},{2,8},{3,12},{4,1},{5,5},{6,9},{7,13},{8,2},{9,6},{10,... | collective-permute-start | bytes 405512 | tf_op jit(solution)/shard_map/ppermute | solution.py:341
  13.4 4.7 %collective-permute-done.5.refs_0_ = bf16[1,528,128]{2,1,0:T(8,128)(2,1)S(1)} collective-permute-done((bf16[1,528,128]{2,1,0:T(8,128)(2,1)S(1)}, bf16[1,528,128]{2,1,0:T(8,128)(2,1)S(1)}, u32[]{:S(2)}, u32[]{:S(2)}) %collective-permute-start.5) | collective-permute-done | bytes 135200 | tf_op jit(solution)/shard_map/ppermute | solution.py:306
  18.2 1.1 %shard_map.103 = (f32[256,512]{1,0:T(8,128)S(1)}, f32[256,512]{1,0:T(8,128)S(1)}, f32[256,512]{1,0:T(8,128)S(1)}) custom-call(bf16[1,512,128]{2,1,0:T(8,128)(2,1)S(1)} %bitcast.7, bf16[1,512,128]{2,1,0:T(8,128)(2,1)S(1)} %collective-permute-done.refs_1_, bf16[1,512,128]{2,1,0:T(8,128)(2,1)S(1)} %bitcast.11, ...), custom_call_target="tpu_custom_call" | custom-call | tf_op jit(solution)/shard_map/pallas_call | solution.py:368
  19.7 0.7 %collective-permute-start.6 = (bf16[256,512]{1,0:T(8,128)(2,1)S(1)}, bf16[256,512]{1,0:T(8,128)(2,1)S(1)}, u32[]{:S(2)}, u32[]{:S(2)}) collective-permute-start(bf16[256,512]{1,0:T(8,128)(2,1)S(1)} %shard_map.106), channel_id=1, source_target_pairs={{0,9},{1,5},{2,11},{3,7},{4,0},{5,12},{6,2},{7,14},{8,1},{9,13},{1... | collective-permute-start | bytes 786440 | tf_op jit(solution)/shard_map/ppermute | solution.py:316
  20.4 3.9 %collective-permute-done.7.arrived.refs_5_.refs_7_ = bf16[256,512]{1,0:T(8,128)(2,1)S(1)} collective-permute-done((bf16[256,512]{1,0:T(8,128)(2,1)S(1)}, bf16[256,512]{1,0:T(8,128)(2,1)S(1)}, u32[]{:S(2)}, u32[]{:S(2)}) %collective-permute-start.7) | collective-permute-done | bytes 262176 | tf_op jit(solution)/shard_map/ppermute | solution.py:316
  24.4 0.8 %collective-permute-start.8 = (bf16[256,512]{1,0:T(8,128)(2,1)S(1)}, bf16[256,512]{1,0:T(8,128)(2,1)S(1)}, u32[]{:S(2)}, u32[]{:S(2)}) collective-permute-start(bf16[256,512]{1,0:T(8,128)(2,1)S(1)} %shard_map.107), channel_id=1, source_target_pairs={{0,8},{1,4},{2,10},{3,6},{4,1},{5,13},{6,3},{7,15},{8,0},{9,12},{1... | collective-permute-start | bytes 786440 | tf_op jit(solution)/shard_map/ppermute | solution.py:316
  25.3 4.9 %collective-permute-done.9.refs_4_ = bf16[512,128]{1,0:T(8,128)(2,1)S(1)} collective-permute-done((bf16[512,128]{1,0:T(8,128)(2,1)S(1)}, bf16[512,128]{1,0:T(8,128)(2,1)S(1)}, u32[]{:S(2)}, u32[]{:S(2)}) %collective-permute-start.9) | collective-permute-done | bytes 131104 | tf_op jit(solution)/shard_map/ppermute | solution.py:286
  30.2 2.2 %collective-permute-done.6.refs_2_ = bf16[256,512]{1,0:T(8,128)(2,1)S(1)} collective-permute-done((bf16[256,512]{1,0:T(8,128)(2,1)S(1)}, bf16[256,512]{1,0:T(8,128)(2,1)S(1)}, u32[]{:S(2)}, u32[]{:S(2)}) %collective-permute-start.6) | collective-permute-done | bytes 262176 | tf_op jit(solution)/shard_map/ppermute | solution.py:316
  32.4 4.7 %collective-permute-done.8.refs_3_ = bf16[256,512]{1,0:T(8,128)(2,1)S(1)} collective-permute-done((bf16[256,512]{1,0:T(8,128)(2,1)S(1)}, bf16[256,512]{1,0:T(8,128)(2,1)S(1)}, u32[]{:S(2)}, u32[]{:S(2)}) %collective-permute-start.8) | collective-permute-done | bytes 262176 | tf_op jit(solution)/shard_map/ppermute | solution.py:316
  37.1 0.7 %shard_map.110 = (f32[2,32,128]{2,1,0:T(8,128)S(1)}, bf16[2,32,128]{2,1,0:T(8,128)(2,1)S(1)}, bf16[2,32,128]{2,1,0:T(8,128)(2,1)S(1)}, bf16[2,32,128]{2,1,0:T(8,128)(2,1)S(1)}) custom-call(f32[256,512]{1,0:T(8,128)S(1)} %get-tuple-element.20.refs_0_, bf16[256,512]{1,0:T(8,128)(2,1)S(1)} %collective-permute-done.4.arrived.refs_1_, ...), custom_call_target="tpu_custom_call" | custom-call | tf_op jit(solution)/shard_map/pallas_call | solution.py:400
  37.8 0.8 %collective-permute-start.11 = (bf16[2,32,128]{2,1,0:T(8,128)(2,1)S(1)}, bf16[2,32,128]{2,1,0:T(8,128)(2,1)S(1)}, u32[]{:S(2)}, u32[]{:S(2)}) collective-permute-start(bf16[2,32,128]{2,1,0:T(8,128)(2,1)S(1)} %get-tuple-element.30), channel_id=1, source_target_pairs={{0,1},{1,0},{2,3},{3,2},{4,5},{5,4},{6,7},{7,6},{8,9},{9,8},{10,11... | collective-permute-start | bytes 49160 | tf_op jit(solution)/shard_map/ppermute | solution.py:286
  38.7 1.4 %collective-permute-start.13 = (bf16[2,32,128]{2,1,0:T(8,128)(2,1)S(1)}, bf16[2,32,128]{2,1,0:T(8,128)(2,1)S(1)}, u32[]{:S(2)}, u32[]{:S(2)}) collective-permute-start(bf16[2,32,128]{2,1,0:T(8,128)(2,1)S(1)} %get-tuple-element.32), channel_id=1, source_target_pairs={{0,3},{1,2},{2,1},{3,0},{4,7},{5,6},{6,5},{7,4},{8,11},{9,10},{10,... | collective-permute-start | bytes 49160 | tf_op jit(solution)/shard_map/ppermute | solution.py:286
  40.1 0.9 %shard_map.108 = (bf16[128,512]{1,0:T(8,128)(2,1)}, bf16[128,512]{1,0:T(8,128)(2,1)}) custom-call(f32[256,512]{1,0:T(8,128)S(1)} %get-tuple-element.20.refs_0_, bf16[256,512]{1,0:T(8,128)(2,1)S(1)} %collective-permute-done.4.arrived.refs_1_, bf16[256,512]{1,0:T(8,128)(2,1)S(1)} %collective-permute-done.6.refs_2_, ...), custom_call_target="tpu_custom_call" | custom-call | tf_op jit(solution)/shard_map/pallas_call | solution.py:406
  41.0 1.4 %collective-permute-done.12.refs_2_ = bf16[2,32,128]{2,1,0:T(8,128)(2,1)S(1)} collective-permute-done((bf16[2,32,128]{2,1,0:T(8,128)(2,1)S(1)}, bf16[2,32,128]{2,1,0:T(8,128)(2,1)S(1)}, u32[]{:S(2)}, u32[]{:S(2)}) %collective-permute-start.12) | collective-permute-done | bytes 16416 | tf_op jit(solution)/shard_map/ppermute | solution.py:286
  42.4 0.6 %shard_map.111 = (f32[32,128]{1,0:T(8,128)}, f32[32,128]{1,0:T(8,128)}) custom-call(f32[2,32,128]{2,1,0:T(8,128)S(1)} %get-tuple-element.29.refs_0_, bf16[2,32,128]{2,1,0:T(8,128)(2,1)S(1)} %collective-permute-done.11.refs_1_, bf16[2,32,128]{2,1,0:T(8,128)(2,1)S(1)} %collective-permute-done.12.refs_2_, ...), custom_call_target="tpu_custom_call" | custom-call | tf_op jit(solution)/shard_map/pallas_call | solution.py:412
  (29 shorter events, 1.2 us)
Async XLA Ops:
  0.6 7.8 %copy-start.4 = (bf16[512,512]{1,0:T(8,128)(2,1)S(1)}, bf16[512,512]{1,0:T(8,128)(2,1)}, u32[]{:S(2)}) copy-start(bf16[512,512]{1,0:T(8,128)(2,1)} %known.1) | copy-start | bytes 1572868
  0.6 10.3 %collective-permute-start.3 = (bf16[512,512]{1,0:T(8,128)(2,1)}, bf16[512,512]{1,0:T(8,128)(2,1)S(1)}, u32[]{:S(2)}, u32[]{:S(2)}) collective-permute-start(bf16[512,512]{1,0:T(8,128)(2,1)} %known.1), channel_id=1, source_target_pairs={{0,1},{1,0},{2,3},{3,2},{4,5},{5,4},{6,7},{7,6},{8,9},{9,8},{10,11... | collective-permute-start | bytes 1572872 | tf_op jit(solution)/shard_map/ppermute | solution.py:286
  1.2 9.8 %collective-permute-start = (bf16[1,512,128]{2,1,0:T(8,128)(2,1)}, bf16[1,512,128]{2,1,0:T(8,128)(2,1)S(1)}, u32[]{:S(2)}, u32[]{:S(2)}) collective-permute-start(bf16[1,512,128]{2,1,0:T(8,128)(2,1)} %bitcast.4), channel_id=1, source_target_pairs={{0,2},{1,3},{2,0},{3,1},{4,6},{5,7},{6,4},{7,5},{8,10},{9,11},{10,... | collective-permute-start | bytes 393224 | tf_op jit(solution)/shard_map/ppermute | solution.py:286
  3.7 7.2 %collective-permute-start.1 = (bf16[1,512,128]{2,1,0:T(8,128)(2,1)}, bf16[1,512,128]{2,1,0:T(8,128)(2,1)S(1)}, u32[]{:S(2)}, u32[]{:S(2)}) collective-permute-start(bf16[1,512,128]{2,1,0:T(8,128)(2,1)} %bitcast.8), channel_id=1, source_target_pairs={{0,2},{1,3},{2,0},{3,1},{4,6},{5,7},{6,4},{7,5},{8,10},{9,11},{10,... | collective-permute-start | bytes 393224 | tf_op jit(solution)/shard_map/ppermute | solution.py:286
  5.3 5.6 %collective-permute-start.2 = (bf16[1,16,128]{2,1,0:T(8,128)(2,1)S(1)}, bf16[1,16,128]{2,1,0:T(8,128)(2,1)S(1)}, u32[]{:S(2)}, u32[]{:S(2)}) collective-permute-start(bf16[1,16,128]{2,1,0:T(8,128)(2,1)S(1)} %broadcast_in_dim.2.refs_4_), channel_id=1, source_target_pairs={{0,2},{1,3},{2,0},{3,1},{4,6},{5,7},{6,4},{7,5},{8,10},{9,11},{10,... | collective-permute-start | bytes 12296 | tf_op jit(solution)/shard_map/ppermute | solution.py:286
  8.2 2.7 %copy-start = (bf16[4,1,128,128]{3,2,1,0:T(8,128)(2,1)S(1)}, bf16[4,1,128,128]{3,2,1,0:T(8,128)(2,1)}, u32[]{:S(2)}) copy-start(bf16[4,1,128,128]{3,2,1,0:T(8,128)(2,1)} %param.8) | copy-start | bytes 393220
  8.2 2.7 %copy-start.1 = (bf16[4,1,128,128]{3,2,1,0:T(8,128)(2,1)S(1)}, bf16[4,1,128,128]{3,2,1,0:T(8,128)(2,1)}, u32[]{:S(2)}) copy-start(bf16[4,1,128,128]{3,2,1,0:T(8,128)(2,1)} %param.11) | copy-start | bytes 393220
  8.2 9.9 %collective-permute-start.5 = (bf16[1,528,128]{2,1,0:T(8,128)(2,1)S(1)}, bf16[1,528,128]{2,1,0:T(8,128)(2,1)S(1)}, u32[]{:S(2)}, u32[]{:S(2)}) collective-permute-start(bf16[1,528,128]{2,1,0:T(8,128)(2,1)S(1)} %get-tuple-element.37), channel_id=1, source_target_pairs={{0,2},{1,6},{2,10},{3,14},{4,3},{5,7},{6,11},{7,15},{8,0},{9,4},{1... | collective-permute-start | bytes 405512 | tf_op jit(solution)/shard_map/ppermute | solution.py:306
  11.5 8.2 %collective-permute-start.4 = (bf16[256,512]{1,0:T(8,128)(2,1)S(1)}, bf16[256,512]{1,0:T(8,128)(2,1)S(1)}, u32[]{:S(2)}, u32[]{:S(2)}) collective-permute-start(bf16[256,512]{1,0:T(8,128)(2,1)S(1)} %get-tuple-element.21), channel_id=1, source_target_pairs={{0,1},{1,5},{2,3},{3,7},{4,0},{5,4},{6,2},{7,6},{8,9},{9,13},{10,1... | collective-permute-start | bytes 786440 | tf_op jit(solution)/shard_map/ppermute | solution.py:316
  11.5 12.8 %collective-permute-start.7 = (bf16[256,512]{1,0:T(8,128)(2,1)S(1)}, bf16[256,512]{1,0:T(8,128)(2,1)S(1)}, u32[]{:S(2)}, u32[]{:S(2)}) collective-permute-start(bf16[256,512]{1,0:T(8,128)(2,1)S(1)} %get-tuple-element.25), channel_id=1, source_target_pairs={{0,1},{1,5},{2,3},{3,7},{4,0},{5,4},{6,2},{7,6},{8,9},{9,13},{10,1... | collective-permute-start | bytes 786440 | tf_op jit(solution)/shard_map/ppermute | solution.py:316
  12.7 12.4 %collective-permute-start.10 = (bf16[1,528,128]{2,1,0:T(8,128)(2,1)S(1)}, bf16[1,528,128]{2,1,0:T(8,128)(2,1)S(1)}, u32[]{:S(2)}, u32[]{:S(2)}) collective-permute-start(bf16[1,528,128]{2,1,0:T(8,128)(2,1)S(1)} %get-tuple-element.36), channel_id=1, source_target_pairs={{0,0},{1,4},{2,8},{3,12},{4,1},{5,5},{6,9},{7,13},{8,2},{9,6},{10,... | collective-permute-start | bytes 405512 | tf_op jit(solution)/shard_map/ppermute | solution.py:341
  19.7 12.6 %collective-permute-start.6 = (bf16[256,512]{1,0:T(8,128)(2,1)S(1)}, bf16[256,512]{1,0:T(8,128)(2,1)S(1)}, u32[]{:S(2)}, u32[]{:S(2)}) collective-permute-start(bf16[256,512]{1,0:T(8,128)(2,1)S(1)} %shard_map.106), channel_id=1, source_target_pairs={{0,9},{1,5},{2,11},{3,7},{4,0},{5,12},{6,2},{7,14},{8,1},{9,13},{1... | collective-permute-start | bytes 786440 | tf_op jit(solution)/shard_map/ppermute | solution.py:316
  24.4 12.7 %copy-start.2 = (f32[32,128]{1,0:T(8,128)S(1)}, f32[32,128]{1,0:T(8,128)}, u32[]{:S(2)}) copy-start(f32[32,128]{1,0:T(8,128)} %refs_4_.1) | copy-start | bytes 49156
  24.4 12.7 %collective-permute-start.8 = (bf16[256,512]{1,0:T(8,128)(2,1)S(1)}, bf16[256,512]{1,0:T(8,128)(2,1)S(1)}, u32[]{:S(2)}, u32[]{:S(2)}) collective-permute-start(bf16[256,512]{1,0:T(8,128)(2,1)S(1)} %shard_map.107), channel_id=1, source_target_pairs={{0,8},{1,4},{2,10},{3,6},{4,1},{5,13},{6,3},{7,15},{8,0},{9,12},{1... | collective-permute-start | bytes 786440 | tf_op jit(solution)/shard_map/ppermute | solution.py:316
  25.2 5.0 %collective-permute-start.9 = (bf16[512,128]{1,0:T(8,128)(2,1)S(1)}, bf16[512,128]{1,0:T(8,128)(2,1)S(1)}, u32[]{:S(2)}, u32[]{:S(2)}) collective-permute-start(bf16[512,128]{1,0:T(8,128)(2,1)S(1)} %shard_map.105), channel_id=1, source_target_pairs={{0,2},{1,3},{2,0},{3,1},{4,6},{5,7},{6,4},{7,5},{8,10},{9,11},{10,... | collective-permute-start | bytes 393224 | tf_op jit(solution)/shard_map/ppermute | solution.py:286
  37.8 3.2 %collective-permute-start.11 = (bf16[2,32,128]{2,1,0:T(8,128)(2,1)S(1)}, bf16[2,32,128]{2,1,0:T(8,128)(2,1)S(1)}, u32[]{:S(2)}, u32[]{:S(2)}) collective-permute-start(bf16[2,32,128]{2,1,0:T(8,128)(2,1)S(1)} %get-tuple-element.30), channel_id=1, source_target_pairs={{0,1},{1,0},{2,3},{3,2},{4,5},{5,4},{6,7},{7,6},{8,9},{9,8},{10,11... | collective-permute-start | bytes 49160 | tf_op jit(solution)/shard_map/ppermute | solution.py:286
  38.7 3.7 %collective-permute-start.12 = (bf16[2,32,128]{2,1,0:T(8,128)(2,1)S(1)}, bf16[2,32,128]{2,1,0:T(8,128)(2,1)S(1)}, u32[]{:S(2)}, u32[]{:S(2)}) collective-permute-start(bf16[2,32,128]{2,1,0:T(8,128)(2,1)S(1)} %get-tuple-element.31), channel_id=1, source_target_pairs={{0,2},{1,3},{2,0},{3,1},{4,6},{5,7},{6,4},{7,5},{8,10},{9,11},{10,... | collective-permute-start | bytes 49160 | tf_op jit(solution)/shard_map/ppermute | solution.py:286
  38.7 3.7 %copy-start.3 = (f32[32,128]{1,0:T(8,128)S(1)}, f32[32,128]{1,0:T(8,128)}, u32[]{:S(2)}) copy-start(f32[32,128]{1,0:T(8,128)} %refs_5_.1) | copy-start | bytes 49156
  38.7 3.7 %collective-permute-start.13 = (bf16[2,32,128]{2,1,0:T(8,128)(2,1)S(1)}, bf16[2,32,128]{2,1,0:T(8,128)(2,1)S(1)}, u32[]{:S(2)}, u32[]{:S(2)}) collective-permute-start(bf16[2,32,128]{2,1,0:T(8,128)(2,1)S(1)} %get-tuple-element.32), channel_id=1, source_target_pairs={{0,3},{1,2},{2,1},{3,0},{4,7},{5,6},{6,5},{7,4},{8,11},{9,10},{10,... | collective-permute-start | bytes 49160 | tf_op jit(solution)/shard_map/ppermute | solution.py:286
